TPU v7x, 256 devices: a whole 4x4x8 slice. The times are simulated.
256 devices in a mesh: sector: 32 (over z, y_lo, core), axial: 8 (over y_hi, x).
Axes of the slice: x: 4, y: 4 (y_hi: 2, y_lo: 2; y = y_hi * 2 + y_lo), z: 8, core: 2. Of those that a mesh axis runs over, the one named last changes fastest.
Arguments:
- prior_thermal_state: float32 [128, 64, 4096], P('sector', 'axial'), may hold values from -4 to 4
- stepped_thermal_conductance: float32 [128, 64, 4096], P('sector', 'axial'), may hold values from 0.3 to 1
- dissipated_power_input: float32 [128, 64, 4096], P('sector', 'axial'), may hold values from -3 to 3
- substance_label: int32 [128, 64, 4096], P(None, 'axial', 'sector'), may hold values from 0 to 3
- magnet_quality_line: int32 [128, 64, 4096], P(None, 'axial', 'sector'), may hold values from 0 to 3
- permanent_pole_mask: int32 [128, 64, 4096], P(None, 'axial', 'sector'), may hold values 0 or 1
- operator_main_entry: float32 [128, 64, 4096], P(None, 'axial', 'sector'), may hold values from 0.5 to 2
- vector_potential_now: float32 [128, 64, 4096], P(None, 'axial', 'sector'), may hold values from -0.4 to 0.4
- reverse_magnetizing_burden: float32 [128, 64, 4096], P(None, 'axial', 'sector'), may hold values from 0.2 to 5
- inverse_permeability: float32 [4], replicated, may hold values from 0.5 to 4
- remanence_knot_chart: float32 [4, 4], replicated, may hold values from -1 to 2
- coercivity_knot_chart: float32 [4, 4], replicated, may hold values from 0.3 to 2
Outputs:
- relaxed_thermal_state: float32 [128, 64, 4096], P('sector', 'axial')
- updated_potential: float32 [128, 64, 4096], P(None, 'axial', 'sector')
- recursive_misfit: float32 [128, 64, 4096], P(None, 'axial', 'sector')
All inputs are finite; a program needn't handle non-finite values. No bound on the sum of `permanent_pole_mask` on one device may be relied on, other than what follows from the above.
Results may differ from a plain program's by a relative error of at most 0.0003.
Values sent between devices are 32-bit elements; how exact they have to be, the bound alone decides.
No kernel may reach another device: no remote copies, remote signals or barrier semaphores. Data moves between devices by JAX's collectives and lax.ppermute only.
A program may use at most 128 MiB of HBM per device.

v0:
```python
import jax
import jax.numpy as jnp
from jax import lax
from jax.sharding import PartitionSpec as P

SWEEPS = 4
ITERS = 2


def padded_2(array, sides, width, wrap):
    for axis, dim in sides:
        devices, length = (lax.axis_size(axis), array.shape[dim])
        up = [(i, (i + 1) % devices) for i in range(devices if wrap else devices - 1)]
        down = [(j, i) for i, j in up]
        last = lax.slice_in_dim(array, length - width, length, axis=dim)
        initial = lax.slice_in_dim(array, 0, width, axis=dim)
        before = lax.ppermute(last, axis, up)
        after = lax.ppermute(initial, axis, down)
        array = jnp.concatenate([before, array, after], axis=dim)
    return array


def sweep(padded_t, padded_k, heat):
    center = padded_t[1:-1, 1:-1]
    kcenter = padded_k[1:-1, 1:-1]
    pairs = [
        (padded_t[2:, 1:-1], padded_k[2:, 1:-1]),
        (padded_t[:-2, 1:-1], padded_k[:-2, 1:-1]),
        (padded_t[1:-1, 2:], padded_k[1:-1, 2:]),
        (padded_t[1:-1, :-2], padded_k[1:-1, :-2]),
        (jnp.roll(center, 1, 2), jnp.roll(kcenter, 1, 2)),
        (jnp.roll(center, -1, 2), jnp.roll(kcenter, -1, 2)),
    ]
    flux = jnp.zeros_like(center)
    for other_t, other_k in pairs:
        flux = flux + 0.5 * (kcenter + other_k) * (other_t - center)
    return center + 0.16 * (flux + heat)


def table_value(table, magnet_quality_line, flux_intensity):
    knots = table.shape[1]
    value = jnp.zeros_like(flux_intensity)
    for col in range(knots):
        coef = jnp.zeros_like(flux_intensity)
        for row in range(table.shape[0]):
            coef = coef + jnp.where(magnet_quality_line == row, table[row, col], 0.0)
        if col == 0:
            value = coef
        else:
            value = value + coef * jnp.maximum(flux_intensity - (col - knots // 2), 0.0)
    return value


def magnet_source(
    flux_intensity,
    magnet_quality_line,
    permanent_pole_mask,
    reverse_magnetizing_burden,
    remanence_knot_chart,
    coercivity_knot_chart,
):
    remanence = table_value(remanence_knot_chart, magnet_quality_line, flux_intensity)
    coercivity = table_value(coercivity_knot_chart, magnet_quality_line, flux_intensity)
    square = coercivity * coercivity
    return (
        permanent_pole_mask.astype(jnp.float32)
        * remanence
        * square
        / (square + reverse_magnetizing_burden)
    )


def reluct_field(substance_label, vector_potential_now, inverse_permeability):
    base = jnp.zeros_like(vector_potential_now)
    for row in range(inverse_permeability.shape[0]):
        base = base + jnp.where(substance_label == row, inverse_permeability[row], 0.0)
    return base * (1.0 + 0.25 * vector_potential_now * vector_potential_now)


def stencil(padded_v, padded_nu, operator_main_entry):
    rows, depth, beside_all = operator_main_entry.shape
    vcenter = padded_v[1:-1, 1:-1, 1:-1]
    ncenter = padded_nu[1:-1, 1:-1, 1:-1]
    total = operator_main_entry * vcenter
    for first in range(3):
        for second in range(3):
            for third in range(3):
                moved = (first != 1) + (second != 1) + (third != 1)
                if moved == 0:
                    continue
                weight = 0.5 ** (moved - 1)
                other_v = padded_v[
                    first : first + rows, second : second + depth, third : third + beside_all
                ]
                other_nu = padded_nu[
                    first : first + rows, second : second + depth, third : third + beside_all
                ]
                total = total + weight * (0.5 * (ncenter + other_nu)) * (vcenter - other_v)
    return total


def close_slabs(padded):
    depth = padded.shape[-2]
    slab = lax.axis_index("axial")
    keep_low = (slab > 0).astype(jnp.float32)
    keep_high = (slab < lax.axis_size("axial") - 1).astype(jnp.float32)
    places = jnp.arange(depth)
    factor = jnp.where(places == 0, keep_low, jnp.where(places == depth - 1, keep_high, 1.0))
    closed = padded * factor[:, None]
    widths = [(0, 0)] * (closed.ndim - 3) + [(1, 1), (0, 0), (0, 0)]
    return jnp.pad(closed, widths)


def operate(flux_intensity, nu_pad, operator_main_entry):
    padded = padded_2(flux_intensity, (("sector", 2), ("axial", 1)), 1, True)
    return stencil(close_slabs(padded), nu_pad, operator_main_entry)


def squares(recursive_misfit):
    return lax.psum(jnp.sum(recursive_misfit * recursive_misfit), ("sector", "axial"))


def local(
    prior_thermal_state,
    stepped_thermal_conductance,
    dissipated_power_input,
    substance_label,
    magnet_quality_line,
    permanent_pole_mask,
    operator_main_entry,
    vector_potential_now,
    reverse_magnetizing_burden,
    inverse_permeability,
    remanence_knot_chart,
    coercivity_knot_chart,
):
    padded_k = padded_2(stepped_thermal_conductance, (("sector", 0), ("axial", 1)), 1, False)
    flux_intensity = prior_thermal_state
    for step in range(SWEEPS):
        padded_t = padded_2(flux_intensity, (("sector", 0), ("axial", 1)), 1, False)
        flux_intensity = sweep(padded_t, padded_k, dissipated_power_input)
    sector_field = lax.all_to_all(flux_intensity, "sector", split_axis=2, concat_axis=0, tiled=True)
    source = magnet_source(
        sector_field,
        magnet_quality_line,
        permanent_pole_mask,
        reverse_magnetizing_burden,
        remanence_knot_chart,
        coercivity_knot_chart,
    )
    nu_local = reluct_field(substance_label, vector_potential_now, inverse_permeability)
    both = padded_2(
        jnp.stack([vector_potential_now, nu_local]), (("sector", 3), ("axial", 2)), 1, True
    )
    both = close_slabs(both)
    nu_pad = both[1]
    recursive_misfit = source - stencil(both[0], nu_pad, operator_main_entry)
    linearized_increment = jnp.zeros_like(vector_potential_now)
    direction = recursive_misfit
    norm_now = squares(recursive_misfit)
    for step in range(ITERS):
        image = operate(direction, nu_pad, operator_main_entry)
        alpha = norm_now / lax.psum(jnp.sum(direction * image), ("sector", "axial"))
        linearized_increment = linearized_increment + alpha * direction
        recursive_misfit = recursive_misfit - alpha * image
        if step + 1 < ITERS:
            fresh = squares(recursive_misfit)
            direction = recursive_misfit + fresh / norm_now * direction
            norm_now = fresh
    return (flux_intensity, vector_potential_now + linearized_increment, recursive_misfit)


def solution(mesh):
    return jax.shard_map(
        local,
        mesh=mesh,
        in_specs=(
            P("sector", "axial", None),
            P("sector", "axial", None),
            P("sector", "axial", None),
            P(None, "axial", "sector"),
            P(None, "axial", "sector"),
            P(None, "axial", "sector"),
            P(None, "axial", "sector"),
            P(None, "axial", "sector"),
            P(None, "axial", "sector"),
            P(),
            P(),
            P(),
        ),
        out_specs=(
            P("sector", "axial", None),
            P(None, "axial", "sector"),
            P(None, "axial", "sector"),
        ),
        check_vma=False,
    )
```

profile of v0, /device:TPU:1, one launch (start us, length us, event | category | flops | bytes accessed | tf_op | source)
XLA Modules:
  0.0 608.6 jit_solution(835921451375496571)
XLA Ops:
  2.4 5.1 collective-permute-start
  34.3 4.6 collective-permute-start.6
  43.2 4.6 collective-permute-start.7
  51.7 6.1 %fusion.189 = (f32[4,8,4096]{2,0,1:T(4,128)S(1)}, f32[4,8,4096]{2,0,1:T(4,128)S(1)}, f32[4,8,4096]{2,0,1:T(4,128)S(1)}, f32[4,8,4096]{2,0,1:T(4,128)S(1)}, f32[4,8,4096]{2,0,1:T(4,128)S(1)}) fusion(f32[4,8,4096]{2,0,1:T(4,128)S(1)} %copy.394, f32[6,1,4096]{2,0,1:T(8,128)} %collective-permute-done.7, f32[1,8,4096]{2,0,1:T(1,128)S(1)} %copy.363, ...), kind=kLoop, calls=%fused_computation.293 | loop fusion | flops 6815744 | bytes 7733248 | tf_op jit(solution)/shard_map/add | solution.py:37
  58.2 7.0 %collective-permute-start.8 = (f32[1,8,4096]{2,1,0:T(8,128)S(1)}, f32[1,8,4096]{2,1,0:T(8,128)S(1)}, u32[]{:S(2)}, u32[]{:S(2)}) collective-permute-start(f32[1,8,4096]{2,1,0:T(8,128)S(1)} %copy.395), channel_id=1, source_target_pairs={{8,0},{16,8},{24,16},{32,24},{40,32},{48,40},{56,48},{64,56},{72,6... | collective-permute-start | bytes 393224 | tf_op jit(solution)/shard_map/ppermute | solution.py:18
  104.2 5.5 collective-permute-start.17
  125.3 6.8 %copy.416 = f32[4,8,4096]{1,0,2:T(4,128)} copy(f32[4,8,4096]{2,0,1:T(4,128)} %fusion.141) | data formatting | bytes 1048576 | tf_op jit(solution)/shard_map/add | solution.py:37
  132.2 12.2 %reshape.42 = f32[32,1,4096]{2,1,0:T(1,128)} reshape(f32[4096,4,8]{2,1,0:T(4,128)} %bitcast.121) | data formatting | bytes 1048576
  144.4 18.2 %all-to-all-start = ((f32[32,1,4096]{2,1,0:T(1,128)}), f32[32,1,4096]{2,1,0:T(1,128)}, u32[]{:S(2)}, u32[]{:S(2)}) async-start(f32[32,1,4096]{2,1,0:T(1,128)} %reshape.42), calls=%async_computation | async-start | bytes 1048576 | tf_op jit(solution)/shard_map/all_to_all | solution.py:142
  164.2 5.4 collective-permute-start.22
  169.7 9.2 %collective-permute-start.23 = (f32[2,128,1,130]{3,2,1,0:T(1,128)S(1)}, f32[2,128,1,130]{3,2,1,0:T(1,128)S(1)}, u32[]{:S(2)}, u32[]{:S(2)}) collective-permute-start(f32[2,128,1,130]{3,2,1,0:T(1,128)S(1)} %get-tuple-element.36), channel_id=1, source_target_pairs={{1,0},{2,1},{3,2},{4,3},{5,4},{6,5},{7,6},{0,7},{9,8},{10,9},{11,1... | collective-permute-start | bytes 399368 | tf_op jit(solution)/shard_map/ppermute | solution.py:18
  179.5 5.5 collective-permute-done.22
  193.5 11.3 %reshape.43 = f32[4096,4,8]{2,1,0:T(4,128)} reshape(f32[32,4096]{1,0:T(8,128)S(1)} %reduce) | data formatting | bytes 1048576
  204.9 6.6 %copy.417 = f32[4,8,4096]{2,1,0:T(8,128)S(1)} copy(f32[4,8,4096]{1,0,2:T(4,128)} %bitcast.120) | data formatting | bytes 1048576 | tf_op jit(solution)/shard_map/all_to_all | solution.py:142
  215.3 42.4 %fusion.57 = f32[128,8,128]{2,1,0:T(8,128)S(1)} fusion(f32[130,10,130]{2,1,0:T(8,128)} %get-tuple-element.34, f32[32,4,8,128]{3,2,1,0:T(8,128)} %copy.422, f32[32,4,8,128]{3,2,1,0:T(8,128)} %copy.420, f32[32,4,8,128]{3,2,1,0:T(8,128)} %copy.418, f32[128,8,128]{2,1,0:T(8,128)S(1)} %copy-done.4, f32[128,8,128]{2,1,0:T(8,128)} %param.20, ...), kind=kLoop, calls=%fused_computation.85 | loop fusion | flops 27525120 | bytes 32505984 | tf_op jit(solution)/shard_map/sub | solution.py:157
  260.0 11.7 %collective-permute-done.24 = f32[128,8,1]{2,1,0:T(8,128)S(1)} collective-permute-done((f32[128,8,1]{2,1,0:T(8,128)S(1)}, f32[128,8,1]{2,1,0:T(8,128)S(1)}, u32[]{:S(2)}, u32[]{:S(2)}) %collective-permute-start.24) | collective-permute-done | bytes 4128 | tf_op jit(solution)/shard_map/ppermute | solution.py:17
  279.2 5.7 collective-permute-start.27
  291.0 23.1 %multiply_reduce_fusion.2 = (f32[]{:T(128)}, f32[]{:T(128)}, f32[128,8,128]{2,1,0:T(8,128)S(1)}) fusion(f32[128,8,128]{2,1,0:T(8,128)S(1)} %fusion.57, f32[130,10,130]{2,1,0:T(8,128)S(1)} %get-tuple-element.33, f32[128,10,130]{2,1,0:T(8,128)} %maximum_multiply_fusion.1, f32[128,8,128]{2,1,0:T(8,128)} %param.18), kind=kLoop, calls=%fused_computation.418 | loop fusion | flops 17694720 | bytes 22544392 | tf_op jit(solution)/shard_map/reduce_sum | solution.py:163
  314.1 82.7 %all-reduce.3 = (f32[]{:T(128)}, f32[]{:T(128)}) all-reduce(f32[]{:T(128)} %get-tuple-element.22, f32[]{:T(128)} %get-tuple-element.21), channel_id=1, replica_groups=mesh['sector'=32,'axial'=8] {'sector','axial'}, use_global_device_ids=true, to_apply=%region_1.2 | all-reduce | flops 2 | bytes 16 | tf_op jit(solution)/shard_map/psum | solution.py:120
  398.8 74.7 %psum.30 = f32[]{:T(128)} all-reduce(f32[]{:T(128)} %multiply_reduce_fusion.1), channel_id=1, replica_groups=mesh['sector'=32,'axial'=8] {'sector','axial'}, use_global_device_ids=true, to_apply=%region_5.6 | all-reduce | flops 1 | bytes 8 | tf_op jit(solution)/shard_map/psum | solution.py:120
  477.7 11.7 %collective-permute-done.28 = f32[128,8,1]{2,1,0:T(8,128)S(1)} collective-permute-done((f32[128,8,1]{2,1,0:T(8,128)S(1)}, f32[128,8,1]{2,1,0:T(8,128)S(1)}, u32[]{:S(2)}, u32[]{:S(2)}) %collective-permute-start.28) | collective-permute-done | bytes 4128 | tf_op jit(solution)/shard_map/ppermute | solution.py:17
  493.8 5.3 collective-permute-start.31
  506.0 23.9 %multiply_reduce_fusion = (f32[]{:T(128)}, f32[128,8,128]{2,1,0:T(8,128)}) fusion(f32[128,8,128]{2,1,0:T(8,128)S(1)} %multiply_add_fusion, f32[130,10,130]{2,1,0:T(8,128)S(1)} %get-tuple-element.33, f32[128,10,130]{2,1,0:T(8,128)} %maximum_multiply_fusion.2, f32[128,8,128]{2,1,0:T(8,128)} %param.18), kind=kLoop, calls=%fused_computation.363 | loop fusion | flops 17432576 | bytes 22544388 | tf_op jit(solution)/shard_map/reduce_sum | solution.py:163
  529.8 74.7 %psum.31 = f32[]{:T(128)} all-reduce(f32[]{:T(128)} %get-tuple-element.25), channel_id=1, replica_groups=mesh['sector'=32,'axial'=8] {'sector','axial'}, use_global_device_ids=true, to_apply=%region_7.8 | all-reduce | flops 1 | bytes 8 | tf_op jit(solution)/shard_map/psum | solution.py:163
  (156 shorter events, 139.1 us)
Async XLA Ops:
  2.4 27.7 %collective-permute-start = (f32[1,8,4096]{2,1,0:T(8,128)S(1)}, f32[1,8,4096]{2,1,0:T(8,128)S(1)}, u32[]{:S(2)}, u32[]{:S(2)}) collective-permute-start(f32[1,8,4096]{2,1,0:T(8,128)S(1)} %get-tuple-element.85), channel_id=1, source_target_pairs={{8,0},{16,8},{24,16},{32,24},{40,32},{48,40},{56,48},{64,56},{72,6... | collective-permute-start | bytes 393224 | tf_op jit(solution)/shard_map/ppermute | solution.py:18
  7.5 23.1 %collective-permute-start.2 = (f32[1,8,4096]{2,1,0:T(8,128)}, f32[1,8,4096]{2,1,0:T(8,128)}, u32[]{:S(2)}, u32[]{:S(2)}) collective-permute-start(f32[1,8,4096]{2,1,0:T(8,128)} %get-tuple-element.84), channel_id=1, source_target_pairs={{0,8},{8,16},{16,24},{24,32},{32,40},{40,48},{48,56},{56,64},{64,7... | collective-permute-start | bytes 393224 | tf_op jit(solution)/shard_map/ppermute | solution.py:17
  11.1 22.6 %collective-permute-start.1 = (f32[1,8,4096]{2,1,0:T(8,128)}, f32[1,8,4096]{2,1,0:T(8,128)S(1)}, u32[]{:S(2)}, u32[]{:S(2)}) collective-permute-start(f32[1,8,4096]{2,1,0:T(8,128)} %get-tuple-element.91), channel_id=1, source_target_pairs={{8,0},{16,8},{24,16},{32,24},{40,32},{48,40},{56,48},{64,56},{72,6... | collective-permute-start | bytes 393224 | tf_op jit(solution)/shard_map/ppermute | solution.py:18
  14.2 25.9 %collective-permute-start.3 = (f32[1,8,4096]{2,1,0:T(8,128)}, f32[1,8,4096]{2,1,0:T(8,128)}, u32[]{:S(2)}, u32[]{:S(2)}) collective-permute-start(f32[1,8,4096]{2,1,0:T(8,128)} %get-tuple-element.90), channel_id=1, source_target_pairs={{0,8},{8,16},{16,24},{24,32},{32,40},{40,48},{48,56},{56,64},{64,7... | collective-permute-start | bytes 393224 | tf_op jit(solution)/shard_map/ppermute | solution.py:17
  23.5 19.7 %collective-permute-start.20 = (f32[2,128,8,1]{1,2,3,0:T(8,128)}, f32[2,128,8,1]{1,2,3,0:T(8,128)}, u32[]{:S(2)}, u32[]{:S(2)}) collective-permute-start(f32[2,128,8,1]{1,2,3,0:T(8,128)} %copy.423), channel_id=1, source_target_pairs={{0,8},{8,16},{16,24},{24,32},{32,40},{40,48},{48,56},{56,64},{64,7... | collective-permute-start | bytes 24584 | tf_op jit(solution)/shard_map/ppermute | solution.py:17
  30.0 19.6 %collective-permute-start.21 = (f32[2,128,8,1]{1,2,3,0:T(8,128)}, f32[2,128,8,1]{1,2,3,0:T(8,128)}, u32[]{:S(2)}, u32[]{:S(2)}) collective-permute-start(f32[2,128,8,1]{1,2,3,0:T(8,128)} %copy.424), channel_id=1, source_target_pairs={{8,0},{16,8},{24,16},{32,24},{40,32},{48,40},{56,48},{64,56},{72,6... | collective-permute-start | bytes 24584 | tf_op jit(solution)/shard_map/ppermute | solution.py:18
  32.4 19.3 %collective-permute-start.4 = (f32[6,1,4096]{2,0,1:T(8,128)}, f32[6,1,4096]{2,0,1:T(8,128)}, u32[]{:S(2)}, u32[]{:S(2)}) collective-permute-start(f32[6,1,4096]{2,0,1:T(8,128)} %get-tuple-element.50), channel_id=1, source_target_pairs={{1,0},{2,1},{3,2},{4,3},{5,4},{6,5},{7,6},{9,8},{10,9},{11,10},{12... | collective-permute-start | bytes 294920 | tf_op jit(solution)/shard_map/ppermute | solution.py:18
  34.3 17.3 %collective-permute-start.6 = (f32[6,1,4096]{2,0,1:T(8,128)}, f32[6,1,4096]{2,0,1:T(8,128)}, u32[]{:S(2)}, u32[]{:S(2)}) collective-permute-start(f32[6,1,4096]{2,0,1:T(8,128)} %get-tuple-element.49), channel_id=1, source_target_pairs={{0,1},{1,2},{2,3},{3,4},{4,5},{5,6},{6,7},{8,9},{9,10},{10,11},{11... | collective-permute-start | bytes 294920 | tf_op jit(solution)/shard_map/ppermute | solution.py:17
  41.9 9.8 %collective-permute-start.5 = (f32[6,1,4096]{2,0,1:T(8,128)}, f32[6,1,4096]{2,0,1:T(8,128)}, u32[]{:S(2)}, u32[]{:S(2)}) collective-permute-start(f32[6,1,4096]{2,0,1:T(8,128)} %get-tuple-element.51), channel_id=1, source_target_pairs={{1,0},{2,1},{3,2},{4,3},{5,4},{6,5},{7,6},{9,8},{10,9},{11,10},{12... | collective-permute-start | bytes 294920 | tf_op jit(solution)/shard_map/ppermute | solution.py:18
  43.2 8.5 %collective-permute-start.7 = (f32[6,1,4096]{2,0,1:T(8,128)}, f32[6,1,4096]{2,0,1:T(8,128)}, u32[]{:S(2)}, u32[]{:S(2)}) collective-permute-start(f32[6,1,4096]{2,0,1:T(8,128)} %get-tuple-element.52), channel_id=1, source_target_pairs={{0,1},{1,2},{2,3},{3,4},{4,5},{5,6},{6,7},{8,9},{9,10},{10,11},{11... | collective-permute-start | bytes 294920 | tf_op jit(solution)/shard_map/ppermute | solution.py:17
  58.2 9.4 %collective-permute-start.8 = (f32[1,8,4096]{2,1,0:T(8,128)S(1)}, f32[1,8,4096]{2,1,0:T(8,128)S(1)}, u32[]{:S(2)}, u32[]{:S(2)}) collective-permute-start(f32[1,8,4096]{2,1,0:T(8,128)S(1)} %copy.395), channel_id=1, source_target_pairs={{8,0},{16,8},{24,16},{32,24},{40,32},{48,40},{56,48},{64,56},{72,6... | collective-permute-start | bytes 393224 | tf_op jit(solution)/shard_map/ppermute | solution.py:18
  83.6 7.9 %collective-permute-start.13 = (f32[1,8,4096]{2,1,0:T(8,128)S(1)}, f32[1,8,4096]{2,1,0:T(8,128)S(1)}, u32[]{:S(2)}, u32[]{:S(2)}) collective-permute-start(f32[1,8,4096]{2,1,0:T(8,128)S(1)} %copy.404), channel_id=1, source_target_pairs={{0,8},{8,16},{16,24},{24,32},{32,40},{40,48},{48,56},{56,64},{64,7... | collective-permute-start | bytes 393224 | tf_op jit(solution)/shard_map/ppermute | solution.py:17
  102.2 8.2 %collective-permute-start.16 = (f32[1,8,4096]{2,1,0:T(8,128)S(1)}, f32[1,8,4096]{2,1,0:T(8,128)S(1)}, u32[]{:S(2)}, u32[]{:S(2)}) collective-permute-start(f32[1,8,4096]{2,1,0:T(8,128)S(1)} %copy.409), channel_id=1, source_target_pairs={{8,0},{16,8},{24,16},{32,24},{40,32},{48,40},{56,48},{64,56},{72,6... | collective-permute-start | bytes 393224 | tf_op jit(solution)/shard_map/ppermute | solution.py:18
  104.2 10.1 %collective-permute-start.17 = (f32[1,8,4096]{2,1,0:T(8,128)S(1)}, f32[1,8,4096]{2,1,0:T(8,128)S(1)}, u32[]{:S(2)}, u32[]{:S(2)}) collective-permute-start(f32[1,8,4096]{2,1,0:T(8,128)S(1)} %copy.411), channel_id=1, source_target_pairs={{0,8},{8,16},{16,24},{24,32},{32,40},{40,48},{48,56},{56,64},{64,7... | collective-permute-start | bytes 393224 | tf_op jit(solution)/shard_map/ppermute | solution.py:17
  144.4 45.7 %all-to-all-start = ((f32[32,1,4096]{2,1,0:T(1,128)}), f32[32,1,4096]{2,1,0:T(1,128)}, u32[]{:S(2)}, u32[]{:S(2)}) async-start(f32[32,1,4096]{2,1,0:T(1,128)} %reshape.42), calls=%async_computation | async-start | bytes 1048576 | tf_op jit(solution)/shard_map/all_to_all | solution.py:142
  164.2 20.8 %collective-permute-start.22 = (f32[2,128,1,130]{3,2,1,0:T(1,128)S(1)}, f32[2,128,1,130]{3,2,1,0:T(1,128)S(1)}, u32[]{:S(2)}, u32[]{:S(2)}) collective-permute-start(f32[2,128,1,130]{3,2,1,0:T(1,128)S(1)} %get-tuple-element.35), channel_id=1, source_target_pairs={{0,1},{1,2},{2,3},{3,4},{4,5},{5,6},{6,7},{7,0},{8,9},{9,10},{10,1... | collective-permute-start | bytes 399368 | tf_op jit(solution)/shard_map/ppermute | solution.py:17
  169.7 16.0 %collective-permute-start.23 = (f32[2,128,1,130]{3,2,1,0:T(1,128)S(1)}, f32[2,128,1,130]{3,2,1,0:T(1,128)S(1)}, u32[]{:S(2)}, u32[]{:S(2)}) collective-permute-start(f32[2,128,1,130]{3,2,1,0:T(1,128)S(1)} %get-tuple-element.36), channel_id=1, source_target_pairs={{1,0},{2,1},{3,2},{4,3},{5,4},{6,5},{7,6},{0,7},{9,8},{10,9},{11,1... | collective-permute-start | bytes 399368 | tf_op jit(solution)/shard_map/ppermute | solution.py:18
  257.9 13.9 %collective-permute-start.24 = (f32[128,8,1]{2,1,0:T(8,128)S(1)}, f32[128,8,1]{2,1,0:T(8,128)S(1)}, u32[]{:S(2)}, u32[]{:S(2)}) collective-permute-start(f32[128,8,1]{2,1,0:T(8,128)S(1)} %get-tuple-element.57), channel_id=1, source_target_pairs={{0,8},{8,16},{16,24},{24,32},{32,40},{40,48},{48,56},{56,64},{64,7... | collective-permute-start | bytes 12296 | tf_op jit(solution)/shard_map/ppermute | solution.py:17
  260.0 14.2 %collective-permute-start.25 = (f32[128,8,1]{2,1,0:T(8,128)S(1)}, f32[128,8,1]{2,1,0:T(8,128)S(1)}, u32[]{:S(2)}, u32[]{:S(2)}) collective-permute-start(f32[128,8,1]{2,1,0:T(8,128)S(1)} %get-tuple-element.58), channel_id=1, source_target_pairs={{8,0},{16,8},{24,16},{32,24},{40,32},{48,40},{56,48},{64,56},{72,6... | collective-permute-start | bytes 12296 | tf_op jit(solution)/shard_map/ppermute | solution.py:18
  276.0 9.8 %collective-permute-start.26 = (f32[128,1,130]{0,2,1:T(8,128)S(1)}, f32[128,1,130]{0,2,1:T(8,128)S(1)}, u32[]{:S(2)}, u32[]{:S(2)}) collective-permute-start(f32[128,1,130]{0,2,1:T(8,128)S(1)} %copy.427), channel_id=1, source_target_pairs={{0,1},{1,2},{2,3},{3,4},{4,5},{5,6},{6,7},{7,0},{8,9},{9,10},{10,1... | collective-permute-start | bytes 199688 | tf_op jit(solution)/shard_map/ppermute | solution.py:17
  476.1 13.4 %collective-permute-start.28 = (f32[128,8,1]{2,1,0:T(8,128)S(1)}, f32[128,8,1]{2,1,0:T(8,128)S(1)}, u32[]{:S(2)}, u32[]{:S(2)}) collective-permute-start(f32[128,8,1]{2,1,0:T(8,128)S(1)} %get-tuple-element.55), channel_id=1, source_target_pairs={{0,8},{8,16},{16,24},{24,32},{32,40},{40,48},{48,56},{56,64},{64,7... | collective-permute-start | bytes 12296 | tf_op jit(solution)/shard_map/ppermute | solution.py:17
  477.7 14.2 %collective-permute-start.29 = (f32[128,8,1]{2,1,0:T(8,128)S(1)}, f32[128,8,1]{2,1,0:T(8,128)S(1)}, u32[]{:S(2)}, u32[]{:S(2)}) collective-permute-start(f32[128,8,1]{2,1,0:T(8,128)S(1)} %get-tuple-element.56), channel_id=1, source_target_pairs={{8,0},{16,8},{24,16},{32,24},{40,32},{48,40},{56,48},{64,56},{72,6... | collective-permute-start | bytes 12296 | tf_op jit(solution)/shard_map/ppermute | solution.py:18
  493.0 8.3 %collective-permute-start.30 = (f32[128,1,130]{0,2,1:T(8,128)S(1)}, f32[128,1,130]{0,2,1:T(8,128)S(1)}, u32[]{:S(2)}, u32[]{:S(2)}) collective-permute-start(f32[128,1,130]{0,2,1:T(8,128)S(1)} %copy.431), channel_id=1, source_target_pairs={{0,1},{1,2},{2,3},{3,4},{4,5},{5,6},{6,7},{7,0},{8,9},{9,10},{10,1... | collective-permute-start | bytes 199688 | tf_op jit(solution)/shard_map/ppermute | solution.py:17
  493.8 7.6 %collective-permute-start.31 = (f32[128,1,130]{0,2,1:T(8,128)}, f32[128,1,130]{0,2,1:T(8,128)}, u32[]{:S(2)}, u32[]{:S(2)}) collective-permute-start(f32[128,1,130]{0,2,1:T(8,128)} %copy.432), channel_id=1, source_target_pairs={{1,0},{2,1},{3,2},{4,3},{5,4},{6,5},{7,6},{0,7},{9,8},{10,9},{11,1... | collective-permute-start | bytes 199688 | tf_op jit(solution)/shard_map/ppermute | solution.py:18
  (21 other events, 354.9 us)
where the time goes:
time: 619 us; the launch traced here: 609 us
  blocking collectives  232 us (37%)
  other arithmetic  131 us (21%)
  starting transfers between devices  114 us (18%)
  local copies, waits for them, and re-layouts  74.1 us (12%)
  waiting for transfers between devices  51.6 us (8%)
    psum x2, blocking collectives, squares(): lax.psum(jnp.sum(recursive_misfit * recursive_misfit), ('sector', 'axial'))  157 us
    psum x1, blocking collectives, local(): alpha = norm_now / lax.psum(jnp.sum(direction * image), ('sector', 'axial'))  74.7 us
    ppermute x16, starting transfers between devices, padded_2(): before = lax.ppermute(last, axis, up)  49.3 us
    reduce_sum x2, other arithmetic, local(): alpha = norm_now / lax.psum(jnp.sum(direction * image), ('sector', 'axial'))  46.9 us
    ppermute x16, starting transfers between devices, padded_2(): after = lax.ppermute(initial, axis, down)  46.7 us
    sub x1, other arithmetic, local(): recursive_misfit = source - stencil(both[0], nu_pad, operator_main_entry)  42.4 us
    ppermute x16, waiting for transfers between devices, padded_2(): before = lax.ppermute(last, axis, up)  42.3 us
    unnamed x32, local copies, waits for them, and re-layouts  30.2 us
  transfers between devices with their start and end apart: 33, of which 18 were waited for; matrix products, arithmetic and copies ran while one was open for 6% of the time, Pallas kernels for 0%

commit v1 on v0

v1 whole, which is shorter than its diff:
```python
import jax
import jax.numpy as jnp
from jax import lax
from jax.experimental import pallas as pl
from jax.experimental.pallas import tpu as pltpu
from jax.sharding import PartitionSpec as P

SWEEPS = 4
F32 = jnp.float32
MIB = 1024 * 1024


def call(kernel, out_shapes, args, smem=(), scratch=(), vmem=24, flops=10_000_000):
    specs = [
        pl.BlockSpec(memory_space=pltpu.SMEM if i in smem else pltpu.VMEM)
        for i in range(len(args))
    ]
    moved = sum(a.size * 4 for a in args)
    return pl.pallas_call(
        kernel,
        out_shape=[jax.ShapeDtypeStruct(s, F32) for s in out_shapes],
        in_specs=specs,
        out_specs=[pl.BlockSpec(memory_space=pltpu.VMEM)] * len(out_shapes),
        scratch_shapes=list(scratch),
        compiler_params=pltpu.CompilerParams(vmem_limit_bytes=vmem * MIB),
        cost_estimate=pl.CostEstimate(flops=flops, bytes_accessed=moved, transcendentals=0),
    )(*args)


def roll(x, shift, axis):
    return pltpu.roll(x, shift % x.shape[axis], axis)


def iota(shape, axis):
    return lax.broadcasted_iota(jnp.int32, shape, axis)


def beside(x, low, high):
    place = iota(x.shape, 0)
    depth = x.shape[0]
    minus = jnp.where(place == 0, low, roll(x, 1, 0))
    plus = jnp.where(place == depth - 1, high, roll(x, -1, 0))
    return minus, plus


def conduct_kernel(k, k_up, k_down, k_low, k_high, radial, around, minus, plus):
    rows = k.shape[0]
    for r in range(rows):
        own = k[r]
        above = k_up[0] if r == 0 else k[r - 1]
        radial[r] = 0.08 * (own + above)
        around[r] = 0.08 * (own + roll(own, -1, 1))
        low, high = beside(own, k_low[r : r + 1], k_high[r : r + 1])
        minus[r] = 0.08 * (own + low)
        plus[r] = 0.08 * (own + high)
    radial[rows] = 0.08 * (k[rows - 1] + k_down[0])


def sweep_kernel(
    last, u, u_up, u_down, u_low, u_high, heat, radial, around, minus, plus, *outs
):
    rows, depth, width = u.shape
    for r in range(rows):
        own = u[r]
        above = u_up[0] if r == 0 else u[r - 1]
        below = u_down[0] if r == rows - 1 else u[r + 1]
        flow = around[r] * (roll(own, -1, 1) - own)
        low, high = beside(own, u_low[r : r + 1], u_high[r : r + 1])
        new = own + (
            (flow - roll(flow, 1, 1))
            + (radial[r] * (above - own) + radial[r + 1] * (below - own))
            + (minus[r] * (low - own) + plus[r] * (high - own))
            + 0.16 * heat[r]
        )
        outs[0][r] = new
        if last:
            for j in range(width // 128):
                outs[1][j, r] = new[:, 128 * j : 128 * j + 128]
        else:
            outs[1][r : r + 1] = new[0:1]
            outs[2][r : r + 1] = new[depth - 1 : depth]


def packed_pair(tile_of, rows, width, col):
    lane = iota((8, width), 1)
    half = width // 2
    out = []
    for t in range(rows // half):
        acc = jnp.zeros((8, width), F32)
        for i in range(half):
            acc = jnp.where(lane // 2 == i, tile_of(half * t + i, 2 * i - col), acc)
        out.append(acc)
    return out


def prep_kernel(v, label, diag, table, nu, pack_up, pack_down):
    rows, _, width = v.shape

    def body(r, _):
        kind = label[r]
        base = jnp.full(kind.shape, table[0], F32)
        for m in range(1, table.shape[0]):
            base = jnp.where(kind == m, table[m], base)
        here = v[r]
        nu[r] = base * (1.0 + 0.25 * here * here)
        return 0

    lax.fori_loop(0, rows, body, 0, unroll=8)
    lane = iota((8, width), 1)
    even = lane % 2 == 0
    for pack, nu_col, col in ((pack_up, width - 2, width - 1), (pack_down, 0, 0)):
        pairs = packed_pair(lambda r, s: roll(nu[r], s, 1), rows, width, nu_col)
        mixed = packed_pair(
            lambda r, s: jnp.where(even, roll(v[r], s, 1), roll(diag[r], s + 1, 1)),
            rows,
            width,
            col,
        )
        for t, tile in enumerate(pairs + mixed):
            pack[t] = tile


def edges_kernel(nu, v, diag, from_low, from_high, up, down):
    rows, depth, _ = nu.shape
    up[0:rows] = nu[:, depth - 2 : depth, :]
    down[0:rows] = nu[:, 0:2, :]
    up[rows : 2 * rows, 0:1] = v[:, depth - 1 : depth, :]
    up[rows : 2 * rows, 1:2] = diag[:, depth - 1 : depth, :]
    down[rows : 2 * rows, 0:1] = v[:, 0:1, :]
    down[rows : 2 * rows, 1:2] = diag[:, 0:1, :]
    for j, ref in ((0, from_low), (4, from_high)):
        up[2 * rows + j : 2 * rows + j + 4] = ref[:, depth - 2 : depth, :]
        down[2 * rows + j : 2 * rows + j + 4] = ref[:, 0:2, :]


def tall_tile(own, high, low):
    width = own.shape[1]
    empty = jnp.zeros((4, width), F32)
    return jnp.concatenate([own, high, empty, low], axis=0)


def blur(x):
    x = x + 0.5 * (roll(x, 1, 1) + roll(x, -1, 1))
    return x + 0.5 * (roll(x, 1, 0) + roll(x, -1, 0))


def setup_kernel(
    v, nu, diag, from_low, from_high, ax_low, ax_high, nu_ext, main, load, v_ext, one, two
):
    rows, depth, width = v.shape
    half = width // 2
    lane = iota((2 * depth, width), 1)
    sides = []
    for j, ref in ((0, from_low), (4, from_high)):
        sides.append(
            [
                tall_tile(ref[t], ax_high[2 * rows + j + t], ax_low[2 * rows + j + t])
                for t in range(2 * (rows // half))
            ]
        )
    lows, highs = sides
    own = slice(0, depth)
    for t in range(rows // half):

        def fill(i, _):
            r = half * t + i
            nu_ext[r, own, 0:width] = nu[r]
            v_ext[r, own, 0:width] = v[r]
            main[r, own, 0:width] = diag[r]
            empty = jnp.zeros((depth - 4, width), F32)
            one_row = jnp.zeros((depth - 2, width), F32)
            nu_ext[r, depth : 2 * depth, 0:width] = jnp.concatenate(
                [ax_high[r], empty, ax_low[r]], axis=0
            )
            mixed_high, mixed_low = ax_high[rows + r], ax_low[rows + r]
            v_ext[r, depth : 2 * depth, 0:width] = jnp.concatenate(
                [mixed_high[0:1], one_row, mixed_low[0:1]], axis=0
            )
            main[r, depth : 2 * depth, 0:width] = jnp.concatenate(
                [mixed_high[1:2], one_row, mixed_low[1:2]], axis=0
            )

            def lanes(low, high, low_at, high_at, count):
                return jnp.where(
                    lane < count,
                    pltpu.roll(high, (width + high_at - 2 * i) % width, 1),
                    jnp.where(
                        lane >= width - count,
                        pltpu.roll(low, (2 * width + low_at - 2 * i) % width, 1),
                        0.0,
                    ),
                )

            n = rows // half
            nu_ext[r, :, width : 2 * width] = lanes(lows[t], highs[t], width - 2, 0, 2)
            v_ext[r, :, width : 2 * width] = lanes(lows[n + t], highs[n + t], width - 1, 0, 1)
            main[r, :, width : 2 * width] = lanes(
                lows[n + t], highs[n + t], width - 2, width - 1, 1
            )
            return 0

        lax.fori_loop(0, half, fill, 0, unroll=4)

    zero = jnp.zeros((2 * depth, 2 * width), F32)
    one[0] = zero
    one[rows + 1] = zero
    two[0] = zero
    two[rows + 1] = zero

    def first(r, _):
        one[r + 1] = blur(nu_ext[r])
        return 0

    lax.fori_loop(0, rows, first, 0, unroll=2)

    def second(r, _):
        n = nu_ext[r]
        main[r] = main[r] + 8.0 * n + (one[r + 1] + 0.5 * (one[r] + one[r + 2]))
        return 0

    lax.fori_loop(0, rows, second, 0, unroll=2)

    def third(r, _):
        x = v_ext[r]
        one[r + 1] = blur(x)
        two[r + 1] = blur(x * nu_ext[r])
        return 0

    lax.fori_loop(0, rows, third, 0, unroll=2)

    def fourth(r, _):
        load[r] = applied(r, v_ext, nu_ext, main, one, two, own, slice(0, width))
        return 0

    lax.fori_loop(0, rows, fourth, 0, unroll=2)


def applied(r, x, nu, main, one, two, places, lanes):
    at = (places, lanes)
    near = one[(r + 1, *at)] + 0.5 * (one[(r, *at)] + one[(r + 2, *at)])
    weighed = two[(r + 1, *at)] + 0.5 * (two[(r, *at)] + two[(r + 2, *at)])
    return main[(r, *at)] * x[(r, *at)] - nu[(r, *at)] * near - weighed


def residual_kernel(t, grade, mask, burden, load, rem, coer, res, pack_up, pack_down):
    rows, _, width = t.shape
    grades, knots = rem.shape

    def body(r, _):
        which = grade[r]
        here = t[r]
        chosen = [which == g for g in range(grades)]

        def value(table):
            total = None
            for col in range(knots):
                coef = jnp.full(here.shape, table[0, col], F32)
                for g in range(1, grades):
                    coef = jnp.where(chosen[g], table[g, col], coef)
                if col:
                    coef = total + coef * jnp.maximum(here - (col - knots // 2), 0.0)
                total = coef
            return total

        remanence = value(rem)
        coercivity = value(coer)
        square = coercivity * coercivity
        source = mask[r].astype(F32) * remanence * square / (square + burden[r])
        res[r] = source - load[r]
        return 0

    lax.fori_loop(0, rows, body, 0, unroll=4)
    for pack, col in ((pack_up, width - 2), (pack_down, 0)):
        for i, tile in enumerate(
            packed_pair(lambda r, s: roll(res[r], s, 1), rows, width, col)
        ):
            pack[i] = tile


def res_edges_kernel(res, from_low, from_high, up, down):
    rows, depth, _ = res.shape
    up[0:rows] = res[:, depth - 2 : depth, :]
    down[0:rows] = res[:, 0:2, :]
    for j, ref in ((0, from_low), (2, from_high)):
        up[rows + j : rows + j + 2] = ref[:, depth - 2 : depth, :]
        down[rows + j : rows + j + 2] = ref[:, 0:2, :]


def gram_kernel(
    res, from_low, from_high, ax_low, ax_high, nu, main, q, kq, sums, x_ext, q_ext, one, two
):
    rows, depth, width = res.shape
    half = width // 2
    lane = iota((2 * depth, width), 1)
    lows, highs = [
        [
            tall_tile(ref[t], ax_high[rows + j + t], ax_low[rows + j + t])
            for t in range(rows // half)
        ]
        for j, ref in ((0, from_low), (2, from_high))
    ]
    zero = jnp.zeros((2 * depth, 2 * width), F32)
    for ref in (one, two):
        ref[0] = zero
        ref[rows + 1] = zero
    for t in range(rows // half):

        def fill(i, _):
            r = half * t + i
            empty = jnp.zeros((depth - 4, width), F32)
            x_ext[r, 0:depth, 0:width] = res[r]
            x_ext[r, depth : 2 * depth, 0:width] = jnp.concatenate(
                [ax_high[r], empty, ax_low[r]], axis=0
            )
            x_ext[r, :, width : 2 * width] = jnp.where(
                lane < 2,
                pltpu.roll(highs[t], (width - 2 * i) % width, 1),
                jnp.where(
                    lane >= width - 2,
                    pltpu.roll(lows[t], (2 * width - 2 - 2 * i) % width, 1),
                    0.0,
                ),
            )
            x = x_ext[r]
            one[r + 1] = blur(x)
            two[r + 1] = blur(x * nu[r])
            return 0

        lax.fori_loop(0, half, fill, 0, unroll=2)

    slab = lax.axis_index("axial")
    place = iota((2 * depth, 2 * width), 0)
    outside = jnp.logical_or(
        jnp.logical_and(place >= 2 * depth - 4, slab == 0),
        jnp.logical_and(
            jnp.logical_and(place >= depth, place < depth + 4),
            slab == lax.axis_size("axial") - 1,
        ),
    )
    whole = (slice(None), slice(None))
    own = (slice(0, depth), slice(0, width))

    def image(r, carry):
        a, b, c = carry
        y = applied(r, x_ext, nu, main, one, two, *whole)
        y = jnp.where(outside, 0.0, y)
        q_ext[r] = y
        y = y[0:depth, 0:width]
        q[r] = y
        x = res[r]
        return a + x * x, b + x * y, c + y * y

    none = jnp.zeros((depth, width), F32)
    a, b, c = lax.fori_loop(0, rows, image, (none, none, none), unroll=2)

    def third(r, _):
        x = q_ext[r]
        one[r + 1] = blur(x)
        two[r + 1] = blur(x * nu[r])
        return 0

    lax.fori_loop(0, rows, third, 0, unroll=2)

    def again(r, d):
        y = applied(r, q_ext, nu, main, one, two, *own)
        kq[r] = y
        return d + y * q[r]

    d = lax.fori_loop(0, rows, again, none, unroll=2)
    spot = iota((1, width), 1)
    line = jnp.zeros((1, width), F32)
    for i, part in enumerate((a, b, c, d)):
        line = jnp.where(spot == i, jnp.sum(part), line)
    for j in range(sums.shape[0]):
        sums[j] = line


def final_kernel(parts, v, res, q, kq, potential, misfit):
    rows = v.shape[0]
    total = parts[0]
    for j in range(1, parts.shape[0]):
        total = total + parts[j]
    rr, rq, qq, qk = [total[0:1, i : i + 1] for i in range(4)]
    alpha = rr / rq
    fresh = alpha * alpha * qq - 2.0 * alpha * rq + rr
    ratio = 1.0 + fresh / rr
    bend = ratio * ratio * rq - 2.0 * alpha * ratio * qq + alpha * alpha * qk
    again = fresh / bend
    straight = alpha + again * ratio
    cross = again * alpha
    straight = jnp.broadcast_to(straight, v.shape[1:])
    cross = jnp.broadcast_to(cross, v.shape[1:])

    def body(r, _):
        x, y = res[r], q[r]
        potential[r] = v[r] + (straight * x - cross * y)
        misfit[r] = x - straight * y + cross * kq[r]
        return 0

    lax.fori_loop(0, rows, body, 0, unroll=8)


def shifted(x, axis, step, wrap):
    n = lax.axis_size(axis)
    pairs = [(i, (i + step) % n) for i in range(n) if wrap or 0 <= i + step < n]
    return lax.ppermute(x, axis, pairs)


def both_ways(up, down, axis, wrap):
    return shifted(up, axis, 1, wrap), shifted(down, axis, -1, wrap)


def local(
    prior_thermal_state,
    stepped_thermal_conductance,
    dissipated_power_input,
    substance_label,
    magnet_quality_line,
    permanent_pole_mask,
    operator_main_entry,
    vector_potential_now,
    reverse_magnetizing_burden,
    inverse_permeability,
    remanence_knot_chart,
    coercivity_knot_chart,
):
    u, k, heat = prior_thermal_state, stepped_thermal_conductance, dissipated_power_input
    v, diag = vector_potential_now, operator_main_entry
    thick, depth, around = u.shape
    rows, _, width = v.shape
    block = (rows, depth, width)
    wide = (rows, 2 * depth, 2 * width)
    scratch_wide = pltpu.VMEM(wide, F32)
    scratch_tall = pltpu.VMEM((rows + 2, 2 * depth, 2 * width), F32)
    tiles = rows * 2 // width
    sectors = lax.axis_size("sector")

    k_up, k_down = both_ways(k[thick - 1 :], k[:1], "sector", False)
    k_low, k_high = both_ways(k[:, depth - 1], k[:, 0], "axial", False)
    faces = (thick + 1, depth, around)
    planes = call(
        conduct_kernel, [faces, u.shape, u.shape, u.shape], [k, k_up, k_down, k_low, k_high]
    )
    nu, pack_up, pack_down = call(
        prep_kernel,
        [block, (2 * tiles, depth, width), (2 * tiles, depth, width)],
        [v, substance_label, diag, inverse_permeability],
        smem=(3,),
    )
    first, last = u[:, 0], u[:, depth - 1]
    for step in range(SWEEPS):
        u_up, u_down = both_ways(u[thick - 1 :], u[:1], "sector", False)
        u_low, u_high = both_ways(last, first, "axial", False)
        final = step + 1 == SWEEPS
        edge = (thick, around)
        outs = (
            [u.shape, (sectors, thick, depth, width)] if final else [u.shape, edge, edge]
        )
        made = call(
            lambda *refs, final=final: sweep_kernel(final, *refs),
            outs,
            [u, u_up, u_down, u_low, u_high, heat, *planes],
        )
        if final:
            u, cut = made
        else:
            u, first, last = made
        if step == 0:
            from_low, from_high = both_ways(pack_up, pack_down, "sector", True)
            spread = (2 * rows + 8 * tiles // 2, 2, width)
            up, down = call(
                edges_kernel, [spread, spread], [nu, v, diag, from_low, from_high]
            )
        if step == 1:
            ax_low, ax_high = both_ways(up, down, "axial", False)
            nu_ext, main, load = call(
                setup_kernel,
                [wide, wide, block],
                [v, nu, diag, from_low, from_high, ax_low, ax_high],
                scratch=[scratch_wide, scratch_tall, scratch_tall],
                vmem=40,
            )
    sector_field = lax.all_to_all(cut, "sector", 0, 0).reshape(block)
    pair = (tiles, depth, width)
    res, pack_up, pack_down = call(
        residual_kernel,
        [block, pair, pair],
        [
            sector_field,
            magnet_quality_line,
            permanent_pole_mask,
            reverse_magnetizing_burden,
            load,
            remanence_knot_chart,
            coercivity_knot_chart,
        ],
        smem=(5, 6),
    )
    from_low, from_high = both_ways(pack_up, pack_down, "sector", True)
    spread = (rows + 2 * tiles, 2, width)
    up, down = call(res_edges_kernel, [spread, spread], [res, from_low, from_high])
    ax_low, ax_high = both_ways(up, down, "axial", False)
    q, kq, sums = call(
        gram_kernel,
        [block, block, (sectors, 1, width)],
        [res, from_low, from_high, ax_low, ax_high, nu_ext, main],
        scratch=[scratch_wide, scratch_wide, scratch_tall, scratch_tall],
        vmem=40,
    )
    slabs = lax.axis_size("axial")
    sums = jnp.sum(lax.all_to_all(sums, "sector", 0, 0), axis=0)
    sums = lax.all_to_all(jnp.broadcast_to(sums[None], (slabs, 1, width)), "axial", 0, 0)
    potential, misfit = call(final_kernel, [block, block], [sums, v, res, q, kq])
    return u, potential, misfit


def solution(mesh):
    thermal = P("sector", "axial", None)
    magnetic = P(None, "axial", "sector")
    return jax.shard_map(
        local,
        mesh=mesh,
        in_specs=(thermal,) * 3 + (magnetic,) * 6 + (P(),) * 3,
        out_specs=(thermal, magnetic, magnetic),
        check_vma=False,
    )
```

time: 619 us -> 236 us (0.38); the launches traced: 609 us -> 235 us
  blocking collectives: 232 us -> 34.6 us
  other arithmetic: 131 us -> 0.05 us
  local copies, waits for them, and re-layouts: 74.1 us -> 15.2 us
  Pallas kernels: 0 us -> 49.5 us
  waiting for transfers between devices: 51.6 us -> 35.8 us
  starting transfers between devices: 114 us -> 98.9 us
    psum x3 -> x0, blocking collectives: 232 us -> none  [the longest x2 157 us: squares(): lax.psum(jnp.sum(recursive_misfit * recursive_misfit), ('sector', 'axial'))]
    pallas_call x0 -> x12, Pallas kernels: none -> 49.5 us  [call(): pl.pallas_call(kernel, out_shape=[jax.ShapeDtypeStruct(s, F32) for s in o...]
    reduce_sum x3 -> x1, other arithmetic: 47.7 us -> 0.05 us  [local(): sums = jnp.sum(lax.all_to_all(sums, 'sector', 0, 0), axis=0)]
    sub x2 -> x0, other arithmetic: 44.8 us -> none  [the longest x1 42.4 us: local(): recursive_misfit = source - stencil(both[0], nu_pad, operator_main_entry)]
    all_to_all x0 -> x2, blocking collectives: none -> 34.6 us  [the longest x1 19.4 us: local(): sums = jnp.sum(lax.all_to_all(sums, 'sector', 0, 0), axis=0)]
    unnamed x32 -> x44, local copies, waits for them, and re-layouts: 30.2 us -> 10.3 us
    add x5 -> x0, other arithmetic: 16.4 us -> none  [the longest x4 15.3 us: sweep(): return center + 0.16 * (flux + heat)]
    ppermute x32 -> x28, waiting for transfers between devices: 51.6 us -> 35.8 us  [shifted(): return lax.ppermute(x, axis, pairs)]
  transfers between devices with their start and end apart: 33 -> 29, of which waited for: 18 -> 12; matrix products, arithmetic and copies ran while one was open for 6% -> 1% of each run, Pallas kernels for 0% -> 9%
where the time goes in v1:
time: 236 us; the launch traced here: 235 us
  starting transfers between devices  98.9 us (42%)
  Pallas kernels  49.5 us (21%)
  waiting for transfers between devices  35.8 us (15%)
  blocking collectives  34.6 us (15%)
  local copies, waits for them, and re-layouts  15.2 us (6%)
    ppermute x28, starting transfers between devices, shifted(): return lax.ppermute(x, axis, pairs)  83.3 us
    pallas_call x12, Pallas kernels, call(): pl.pallas_call(kernel, out_shape=[jax.ShapeDtypeStruct(s, F32) for s in o...  49.5 us
    ppermute x28, waiting for transfers between devices, shifted(): return lax.ppermute(x, axis, pairs)  35.8 us
    all_to_all x1, blocking collectives, local(): sums = jnp.sum(lax.all_to_all(sums, 'sector', 0, 0), axis=0)  19.4 us
    all_to_all x1, starting transfers between devices, local(): sector_field = lax.all_to_all(cut, 'sector', 0, 0).reshape(block)  15.7 us
    all_to_all x1, blocking collectives, local(): lax.all_to_all(jnp.broadcast_to(sums[None], (slabs, 1, width)), 'axial',...  15.1 us
    unnamed x44, local copies, waits for them, and re-layouts  10.3 us
  transfers between devices with their start and end apart: 29, of which 12 were waited for; matrix products, arithmetic and copies ran while one was open for 1% of the time, Pallas kernels for 9%

profile of v1, /device:TPU:1, one launch (start us, length us, event | category | flops | bytes accessed | tf_op | source)
XLA Modules:
  0.0 235.2 jit_solution(5216575320793518615)
XLA Ops:
  2.1 3.9 %collective-permute-start.6 = (f32[4,4096]{1,0:T(4,128)S(1)}, f32[4,4096]{1,0:T(4,128)S(1)}, u32[]{:S(2)}, u32[]{:S(2)}) collective-permute-start(f32[4,4096]{1,0:T(4,128)S(1)} %bitcast.15), channel_id=1, source_target_pairs={{0,1},{1,2},{2,3},{3,4},{4,5},{5,6},{6,7},{8,9},{9,10},{10,11},{11... | collective-permute-start | bytes 196616 | tf_op jit(solution)/shard_map/ppermute | solution.py:406
  17.3 3.6 %collective-permute-start.4 = (f32[1,8,4096]{2,1,0:T(8,128)S(1)}, f32[1,8,4096]{2,1,0:T(8,128)S(1)}, u32[]{:S(2)}, u32[]{:S(2)}) collective-permute-start(f32[1,8,4096]{2,1,0:T(8,128)S(1)} %get-tuple-element.78), channel_id=1, source_target_pairs={{0,8},{8,16},{16,24},{24,32},{32,40},{40,48},{48,56},{56,64},{64,7... | collective-permute-start | bytes 393224 | tf_op jit(solution)/shard_map/ppermute | solution.py:406
  22.5 4.3 %collective-permute-start.2 = (f32[4,4096]{1,0:T(4,128)S(1)}, f32[4,4096]{1,0:T(4,128)S(1)}, u32[]{:S(2)}, u32[]{:S(2)}) collective-permute-start(f32[4,4096]{1,0:T(4,128)S(1)} %bitcast.16), channel_id=1, source_target_pairs={{0,1},{1,2},{2,3},{3,4},{4,5},{5,6},{6,7},{8,9},{9,10},{10,11},{11... | collective-permute-start | bytes 196616 | tf_op jit(solution)/shard_map/ppermute | solution.py:406
  28.4 3.6 %collective-permute-done.3.refs_4_ = f32[4,4096]{1,0:T(4,128)S(1)} collective-permute-done((f32[4,4096]{1,0:T(4,128)S(1)}, f32[4,4096]{1,0:T(4,128)S(1)}, u32[]{:S(2)}, u32[]{:S(2)}) %collective-permute-start.3) | collective-permute-done | bytes 65568 | tf_op jit(solution)/shard_map/ppermute | solution.py:406
  34.9 3.4 %collective-permute-start.8 = (f32[1,8,4096]{2,1,0:T(8,128)S(1)}, f32[1,8,4096]{2,1,0:T(8,128)S(1)}, u32[]{:S(2)}, u32[]{:S(2)}) collective-permute-start(f32[1,8,4096]{2,1,0:T(8,128)S(1)} %get-tuple-element.74), channel_id=1, source_target_pairs={{0,8},{8,16},{16,24},{24,32},{32,40},{40,48},{48,56},{56,64},{64,7... | collective-permute-start | bytes 393224 | tf_op jit(solution)/shard_map/ppermute | solution.py:406
  38.2 3.1 %collective-permute-start.10 = (f32[4,4096]{1,0:T(4,128)S(1)}, f32[4,4096]{1,0:T(4,128)S(1)}, u32[]{:S(2)}, u32[]{:S(2)}) collective-permute-start(f32[4,4096]{1,0:T(4,128)S(1)} %get-tuple-element.41), channel_id=1, source_target_pairs={{0,1},{1,2},{2,3},{3,4},{4,5},{5,6},{6,7},{8,9},{9,10},{10,11},{11... | collective-permute-start | bytes 196616 | tf_op jit(solution)/shard_map/ppermute | solution.py:406
  42.7 7.6 %collective-permute-done.11.refs_4_ = f32[4,4096]{1,0:T(4,128)S(1)} collective-permute-done((f32[4,4096]{1,0:T(4,128)S(1)}, f32[4,4096]{1,0:T(4,128)S(1)}, u32[]{:S(2)}, u32[]{:S(2)}) %collective-permute-start.11) | collective-permute-done | bytes 65568 | tf_op jit(solution)/shard_map/ppermute | solution.py:406
  52.9 3.8 %collective-permute-start.12 = (f32[1,8,4096]{2,1,0:T(8,128)S(1)}, f32[1,8,4096]{2,1,0:T(8,128)S(1)}, u32[]{:S(2)}, u32[]{:S(2)}) collective-permute-start(f32[1,8,4096]{2,1,0:T(8,128)S(1)} %get-tuple-element.72), channel_id=1, source_target_pairs={{0,8},{8,16},{16,24},{24,32},{32,40},{40,48},{48,56},{56,64},{64,7... | collective-permute-start | bytes 393224 | tf_op jit(solution)/shard_map/ppermute | solution.py:406
  56.7 7.2 %collective-permute-start.14 = (f32[4,4096]{1,0:T(4,128)S(1)}, f32[4,4096]{1,0:T(4,128)S(1)}, u32[]{:S(2)}, u32[]{:S(2)}) collective-permute-start(f32[4,4096]{1,0:T(4,128)S(1)} %get-tuple-element.44), channel_id=1, source_target_pairs={{0,1},{1,2},{2,3},{3,4},{4,5},{5,6},{6,7},{8,9},{9,10},{10,11},{11... | collective-permute-start | bytes 196616 | tf_op jit(solution)/shard_map/ppermute | solution.py:406
  65.2 4.3 %collective-permute-done.15.refs_4_ = f32[4,4096]{1,0:T(4,128)S(1)} collective-permute-done((f32[4,4096]{1,0:T(4,128)S(1)}, f32[4,4096]{1,0:T(4,128)S(1)}, u32[]{:S(2)}, u32[]{:S(2)}) %collective-permute-start.15) | collective-permute-done | bytes 65568 | tf_op jit(solution)/shard_map/ppermute | solution.py:406
  72.5 3.6 %collective-permute-start.16 = (f32[1,8,4096]{2,1,0:T(8,128)S(1)}, f32[1,8,4096]{2,1,0:T(8,128)S(1)}, u32[]{:S(2)}, u32[]{:S(2)}) collective-permute-start(f32[1,8,4096]{2,1,0:T(8,128)S(1)} %get-tuple-element.70), channel_id=1, source_target_pairs={{0,8},{8,16},{16,24},{24,32},{32,40},{40,48},{48,56},{56,64},{64,7... | collective-permute-start | bytes 393224 | tf_op jit(solution)/shard_map/ppermute | solution.py:406
  76.1 5.3 %collective-permute-start.18 = (f32[4,4096]{1,0:T(4,128)S(1)}, f32[4,4096]{1,0:T(4,128)S(1)}, u32[]{:S(2)}, u32[]{:S(2)}) collective-permute-start(f32[4,4096]{1,0:T(4,128)S(1)} %get-tuple-element.47), channel_id=1, source_target_pairs={{0,1},{1,2},{2,3},{3,4},{4,5},{5,6},{6,7},{8,9},{9,10},{10,11},{11... | collective-permute-start | bytes 196616 | tf_op jit(solution)/shard_map/ppermute | solution.py:406
  82.8 4.0 %collective-permute-done.19.refs_4_ = f32[4,4096]{1,0:T(4,128)S(1)} collective-permute-done((f32[4,4096]{1,0:T(4,128)S(1)}, f32[4,4096]{1,0:T(4,128)S(1)}, u32[]{:S(2)}, u32[]{:S(2)}) %collective-permute-start.19) | collective-permute-done | bytes 65568 | tf_op jit(solution)/shard_map/ppermute | solution.py:406
  88.3 15.7 %all-to-all-start = ((f32[32,4,8,128]{3,2,1,0:T(8,128)}), f32[32,4,8,128]{3,2,1,0:T(8,128)}, u32[]{:S(2)}, u32[]{:S(2)}) async-start(f32[32,4,8,128]{3,2,1,0:T(8,128)} %get-tuple-element.50), calls=%async_computation | async-start | bytes 1048576 | tf_op jit(solution)/shard_map/all_to_all | solution.py:483
  108.3 3.6 %collective-permute-done.21.from_high = f32[4,8,128]{2,1,0:T(8,128)S(1)} collective-permute-done((f32[4,8,128]{2,1,0:T(8,128)S(1)}, f32[4,8,128]{2,1,0:T(8,128)S(1)}, u32[]{:S(2)}, u32[]{:S(2)}) %collective-permute-start.21) | collective-permute-done | bytes 16416 | tf_op jit(solution)/shard_map/ppermute | solution.py:406
  112.2 5.3 %collective-permute-start.22 = (f32[264,2,128]{2,1,0:T(2,128)S(1)}, f32[264,2,128]{2,1,0:T(2,128)S(1)}, u32[]{:S(2)}, u32[]{:S(2)}) collective-permute-start(f32[264,2,128]{2,1,0:T(2,128)S(1)} %get-tuple-element.54), channel_id=1, source_target_pairs={{0,1},{1,2},{2,3},{3,4},{4,5},{5,6},{6,7},{8,9},{9,10},{10,11},{11... | collective-permute-start | bytes 811016 | tf_op jit(solution)/shard_map/ppermute | solution.py:406
  120.9 4.1 %collective-permute-done.23.ax_high = f32[264,2,128]{2,1,0:T(2,128)S(1)} collective-permute-done((f32[264,2,128]{2,1,0:T(2,128)S(1)}, f32[264,2,128]{2,1,0:T(2,128)S(1)}, u32[]{:S(2)}, u32[]{:S(2)}) %collective-permute-start.23) | collective-permute-done | bytes 270368 | tf_op jit(solution)/shard_map/ppermute | solution.py:406
  125.0 19.0 %shard_map.146 = (f32[128,16,256]{2,1,0:T(8,128)S(1)}, f32[128,16,256]{2,1,0:T(8,128)S(1)}, f32[128,8,128]{2,1,0:T(8,128)S(1)}) custom-call(f32[128,8,128]{2,1,0:T(8,128)S(1)} %copy-done.1, f32[128,8,128]{2,1,0:T(8,128)S(1)} %get-tuple-element.51.nu, f32[128,8,128]{2,1,0:T(8,128)S(1)} %copy-done.2, f32[4,8,128]{2,1,0:T(8,128)S(1)} %collective-permute-done.20.from_low, ...), custom_call_target="tpu_custom_call" | custom-call | flops 10000000 | bytes 2146304 | tf_op jit(solution)/shard_map/pallas_call | solution.py:19
  153.3 8.2 %collective-permute-start.25 = (f32[2,8,128]{2,1,0:T(8,128)S(1)}, f32[2,8,128]{2,1,0:T(8,128)S(1)}, u32[]{:S(2)}, u32[]{:S(2)}) collective-permute-start(f32[2,8,128]{2,1,0:T(8,128)S(1)} %get-tuple-element.59), channel_id=1, source_target_pairs={{0,248},{8,0},{16,8},{24,16},{32,24},{40,32},{48,40},{56,48},{64,5... | collective-permute-start | bytes 24584 | tf_op jit(solution)/shard_map/ppermute | solution.py:406
  162.5 6.2 %collective-permute-start.26 = (f32[132,2,128]{2,1,0:T(2,128)S(1)}, f32[132,2,128]{2,1,0:T(2,128)S(1)}, u32[]{:S(2)}, u32[]{:S(2)}) collective-permute-start(f32[132,2,128]{2,1,0:T(2,128)S(1)} %get-tuple-element.60), channel_id=1, source_target_pairs={{0,1},{1,2},{2,3},{3,4},{4,5},{5,6},{6,7},{8,9},{9,10},{10,11},{11... | collective-permute-start | bytes 405512 | tf_op jit(solution)/shard_map/ppermute | solution.py:406
  170.7 4.0 %collective-permute-done.27.ax_high = f32[132,2,128]{2,1,0:T(2,128)S(1)} collective-permute-done((f32[132,2,128]{2,1,0:T(2,128)S(1)}, f32[132,2,128]{2,1,0:T(2,128)S(1)}, u32[]{:S(2)}, u32[]{:S(2)}) %collective-permute-start.27) | collective-permute-done | bytes 135200 | tf_op jit(solution)/shard_map/ppermute | solution.py:406
  174.7 20.8 %shard_map.149 = (f32[128,8,128]{2,1,0:T(8,128)S(1)}, f32[128,8,128]{2,1,0:T(8,128)S(1)}, f32[32,1,128]{2,1,0:T(1,128)S(1)}) custom-call(f32[128,8,128]{2,1,0:T(8,128)S(1)} %get-tuple-element.57.res, f32[2,8,128]{2,1,0:T(8,128)S(1)} %collective-permute-done.24.from_low, f32[2,8,128]{2,1,0:T(8,128)S(1)} %collective-permute-done.25.from_high, ...), custom_call_target="tpu_custom_call" | custom-call | flops 10000000 | bytes 5005312 | tf_op jit(solution)/shard_map/pallas_call | solution.py:19
  197.2 19.4 %all_to_all.15 = f32[32,1,128]{2,1,0:T(1,128)S(1)} all-to-all(f32[32,1,128]{2,1,0:T(1,128)S(1)} %get-tuple-element.64), channel_id=1, replica_groups=mesh['sector'=32,'axial'=8] {'sector'}, dimensions={0} | all-to-all | bytes 32768 | tf_op jit(solution)/shard_map/all_to_all | solution.py:511
  216.6 15.1 %all_to_all.16.parts = f32[8,1,128]{2,1,0:T(1,128)S(1)} all-to-all(f32[8,1,128]{2,1,0:T(1,128)S(1)} %broadcast_in_dim.2), channel_id=1, replica_groups=mesh['sector'=32,'axial'=8] {'axial'}, dimensions={0} | all-to-all | bytes 8192 | tf_op jit(solution)/shard_map/all_to_all | solution.py:512
  (101 shorter events, 54.7 us)
Async XLA Ops:
  2.1 15.2 %collective-permute-start.6 = (f32[4,4096]{1,0:T(4,128)S(1)}, f32[4,4096]{1,0:T(4,128)S(1)}, u32[]{:S(2)}, u32[]{:S(2)}) collective-permute-start(f32[4,4096]{1,0:T(4,128)S(1)} %bitcast.15), channel_id=1, source_target_pairs={{0,1},{1,2},{2,3},{3,4},{4,5},{5,6},{6,7},{8,9},{9,10},{10,11},{11... | collective-permute-start | bytes 196616 | tf_op jit(solution)/shard_map/ppermute | solution.py:406
  6.1 16.4 %collective-permute-start.7 = (f32[4,4096]{1,0:T(4,128)S(1)}, f32[4,4096]{1,0:T(4,128)S(1)}, u32[]{:S(2)}, u32[]{:S(2)}) collective-permute-start(f32[4,4096]{1,0:T(4,128)S(1)} %bitcast.13), channel_id=1, source_target_pairs={{1,0},{2,1},{3,2},{4,3},{5,4},{6,5},{7,6},{9,8},{10,9},{11,10},{12... | collective-permute-start | bytes 196616 | tf_op jit(solution)/shard_map/ppermute | solution.py:406
  8.4 23.6 %collective-permute-start.1 = (f32[1,8,4096]{2,1,0:T(8,128)S(1)}, f32[1,8,4096]{2,1,0:T(8,128)S(1)}, u32[]{:S(2)}, u32[]{:S(2)}) collective-permute-start(f32[1,8,4096]{2,1,0:T(8,128)S(1)} %get-tuple-element.81), channel_id=1, source_target_pairs={{8,0},{16,8},{24,16},{32,24},{40,32},{48,40},{56,48},{64,56},{72,6... | collective-permute-start | bytes 393224 | tf_op jit(solution)/shard_map/ppermute | solution.py:406
  11.3 20.7 %collective-permute-start = (f32[1,8,4096]{2,1,0:T(8,128)S(1)}, f32[1,8,4096]{2,1,0:T(8,128)S(1)}, u32[]{:S(2)}, u32[]{:S(2)}) collective-permute-start(f32[1,8,4096]{2,1,0:T(8,128)S(1)} %get-tuple-element.82), channel_id=1, source_target_pairs={{0,8},{8,16},{16,24},{24,32},{32,40},{40,48},{48,56},{56,64},{64,7... | collective-permute-start | bytes 393224 | tf_op jit(solution)/shard_map/ppermute | solution.py:406
  15.4 11.4 %collective-permute-start.5 = (f32[1,8,4096]{2,1,0:T(8,128)S(1)}, f32[1,8,4096]{2,1,0:T(8,128)S(1)}, u32[]{:S(2)}, u32[]{:S(2)}) collective-permute-start(f32[1,8,4096]{2,1,0:T(8,128)S(1)} %get-tuple-element.77), channel_id=1, source_target_pairs={{8,0},{16,8},{24,16},{32,24},{40,32},{48,40},{56,48},{64,56},{72,6... | collective-permute-start | bytes 393224 | tf_op jit(solution)/shard_map/ppermute | solution.py:406
  17.3 10.8 %collective-permute-start.4 = (f32[1,8,4096]{2,1,0:T(8,128)S(1)}, f32[1,8,4096]{2,1,0:T(8,128)S(1)}, u32[]{:S(2)}, u32[]{:S(2)}) collective-permute-start(f32[1,8,4096]{2,1,0:T(8,128)S(1)} %get-tuple-element.78), channel_id=1, source_target_pairs={{0,8},{8,16},{16,24},{24,32},{32,40},{40,48},{48,56},{56,64},{64,7... | collective-permute-start | bytes 393224 | tf_op jit(solution)/shard_map/ppermute | solution.py:406
  22.5 5.9 %collective-permute-start.2 = (f32[4,4096]{1,0:T(4,128)S(1)}, f32[4,4096]{1,0:T(4,128)S(1)}, u32[]{:S(2)}, u32[]{:S(2)}) collective-permute-start(f32[4,4096]{1,0:T(4,128)S(1)} %bitcast.16), channel_id=1, source_target_pairs={{0,1},{1,2},{2,3},{3,4},{4,5},{5,6},{6,7},{8,9},{9,10},{10,11},{11... | collective-permute-start | bytes 196616 | tf_op jit(solution)/shard_map/ppermute | solution.py:406
  32.7 17.7 %collective-permute-start.9 = (f32[1,8,4096]{2,1,0:T(8,128)S(1)}, f32[1,8,4096]{2,1,0:T(8,128)S(1)}, u32[]{:S(2)}, u32[]{:S(2)}) collective-permute-start(f32[1,8,4096]{2,1,0:T(8,128)S(1)} %get-tuple-element.73), channel_id=1, source_target_pairs={{8,0},{16,8},{24,16},{32,24},{40,32},{48,40},{56,48},{64,56},{72,6... | collective-permute-start | bytes 393224 | tf_op jit(solution)/shard_map/ppermute | solution.py:406
  34.9 15.5 %collective-permute-start.8 = (f32[1,8,4096]{2,1,0:T(8,128)S(1)}, f32[1,8,4096]{2,1,0:T(8,128)S(1)}, u32[]{:S(2)}, u32[]{:S(2)}) collective-permute-start(f32[1,8,4096]{2,1,0:T(8,128)S(1)} %get-tuple-element.74), channel_id=1, source_target_pairs={{0,8},{8,16},{16,24},{24,32},{32,40},{40,48},{48,56},{56,64},{64,7... | collective-permute-start | bytes 393224 | tf_op jit(solution)/shard_map/ppermute | solution.py:406
  41.4 8.9 %collective-permute-start.11 = (f32[4,4096]{1,0:T(4,128)S(1)}, f32[4,4096]{1,0:T(4,128)S(1)}, u32[]{:S(2)}, u32[]{:S(2)}) collective-permute-start(f32[4,4096]{1,0:T(4,128)S(1)} %get-tuple-element.42), channel_id=1, source_target_pairs={{1,0},{2,1},{3,2},{4,3},{5,4},{6,5},{7,6},{9,8},{10,9},{11,10},{12... | collective-permute-start | bytes 196616 | tf_op jit(solution)/shard_map/ppermute | solution.py:406
  50.9 18.6 %collective-permute-start.13 = (f32[1,8,4096]{2,1,0:T(8,128)S(1)}, f32[1,8,4096]{2,1,0:T(8,128)S(1)}, u32[]{:S(2)}, u32[]{:S(2)}) collective-permute-start(f32[1,8,4096]{2,1,0:T(8,128)S(1)} %get-tuple-element.71), channel_id=1, source_target_pairs={{8,0},{16,8},{24,16},{32,24},{40,32},{48,40},{56,48},{64,56},{72,6... | collective-permute-start | bytes 393224 | tf_op jit(solution)/shard_map/ppermute | solution.py:406
  52.9 16.7 %collective-permute-start.12 = (f32[1,8,4096]{2,1,0:T(8,128)S(1)}, f32[1,8,4096]{2,1,0:T(8,128)S(1)}, u32[]{:S(2)}, u32[]{:S(2)}) collective-permute-start(f32[1,8,4096]{2,1,0:T(8,128)S(1)} %get-tuple-element.72), channel_id=1, source_target_pairs={{0,8},{8,16},{16,24},{24,32},{32,40},{40,48},{48,56},{56,64},{64,7... | collective-permute-start | bytes 393224 | tf_op jit(solution)/shard_map/ppermute | solution.py:406
  56.7 8.5 %collective-permute-start.14 = (f32[4,4096]{1,0:T(4,128)S(1)}, f32[4,4096]{1,0:T(4,128)S(1)}, u32[]{:S(2)}, u32[]{:S(2)}) collective-permute-start(f32[4,4096]{1,0:T(4,128)S(1)} %get-tuple-element.44), channel_id=1, source_target_pairs={{0,1},{1,2},{2,3},{3,4},{4,5},{5,6},{6,7},{8,9},{9,10},{10,11},{11... | collective-permute-start | bytes 196616 | tf_op jit(solution)/shard_map/ppermute | solution.py:406
  63.9 5.6 %collective-permute-start.15 = (f32[4,4096]{1,0:T(4,128)S(1)}, f32[4,4096]{1,0:T(4,128)S(1)}, u32[]{:S(2)}, u32[]{:S(2)}) collective-permute-start(f32[4,4096]{1,0:T(4,128)S(1)} %get-tuple-element.45), channel_id=1, source_target_pairs={{1,0},{2,1},{3,2},{4,3},{5,4},{6,5},{7,6},{9,8},{10,9},{11,10},{12... | collective-permute-start | bytes 196616 | tf_op jit(solution)/shard_map/ppermute | solution.py:406
  70.2 16.6 %collective-permute-start.17 = (f32[1,8,4096]{2,1,0:T(8,128)S(1)}, f32[1,8,4096]{2,1,0:T(8,128)S(1)}, u32[]{:S(2)}, u32[]{:S(2)}) collective-permute-start(f32[1,8,4096]{2,1,0:T(8,128)S(1)} %get-tuple-element.69), channel_id=1, source_target_pairs={{8,0},{16,8},{24,16},{32,24},{40,32},{48,40},{56,48},{64,56},{72,6... | collective-permute-start | bytes 393224 | tf_op jit(solution)/shard_map/ppermute | solution.py:406
  72.5 14.3 %collective-permute-start.16 = (f32[1,8,4096]{2,1,0:T(8,128)S(1)}, f32[1,8,4096]{2,1,0:T(8,128)S(1)}, u32[]{:S(2)}, u32[]{:S(2)}) collective-permute-start(f32[1,8,4096]{2,1,0:T(8,128)S(1)} %get-tuple-element.70), channel_id=1, source_target_pairs={{0,8},{8,16},{16,24},{24,32},{32,40},{40,48},{48,56},{56,64},{64,7... | collective-permute-start | bytes 393224 | tf_op jit(solution)/shard_map/ppermute | solution.py:406
  76.1 6.7 %collective-permute-start.18 = (f32[4,4096]{1,0:T(4,128)S(1)}, f32[4,4096]{1,0:T(4,128)S(1)}, u32[]{:S(2)}, u32[]{:S(2)}) collective-permute-start(f32[4,4096]{1,0:T(4,128)S(1)} %get-tuple-element.47), channel_id=1, source_target_pairs={{0,1},{1,2},{2,3},{3,4},{4,5},{5,6},{6,7},{8,9},{9,10},{10,11},{11... | collective-permute-start | bytes 196616 | tf_op jit(solution)/shard_map/ppermute | solution.py:406
  88.3 57.8 %all-to-all-start = ((f32[32,4,8,128]{3,2,1,0:T(8,128)}), f32[32,4,8,128]{3,2,1,0:T(8,128)}, u32[]{:S(2)}, u32[]{:S(2)}) async-start(f32[32,4,8,128]{3,2,1,0:T(8,128)} %get-tuple-element.50), calls=%async_computation | async-start | bytes 1048576 | tf_op jit(solution)/shard_map/all_to_all | solution.py:483
  112.2 8.7 %collective-permute-start.22 = (f32[264,2,128]{2,1,0:T(2,128)S(1)}, f32[264,2,128]{2,1,0:T(2,128)S(1)}, u32[]{:S(2)}, u32[]{:S(2)}) collective-permute-start(f32[264,2,128]{2,1,0:T(2,128)S(1)} %get-tuple-element.54), channel_id=1, source_target_pairs={{0,1},{1,2},{2,3},{3,4},{4,5},{5,6},{6,7},{8,9},{9,10},{10,11},{11... | collective-permute-start | bytes 811016 | tf_op jit(solution)/shard_map/ppermute | solution.py:406
  117.5 7.5 %collective-permute-start.23 = (f32[264,2,128]{2,1,0:T(2,128)S(1)}, f32[264,2,128]{2,1,0:T(2,128)S(1)}, u32[]{:S(2)}, u32[]{:S(2)}) collective-permute-start(f32[264,2,128]{2,1,0:T(2,128)S(1)} %get-tuple-element.55), channel_id=1, source_target_pairs={{1,0},{2,1},{3,2},{4,3},{5,4},{6,5},{7,6},{9,8},{10,9},{11,10},{12... | collective-permute-start | bytes 811016 | tf_op jit(solution)/shard_map/ppermute | solution.py:406
  153.2 8.9 %collective-permute-start.24 = (f32[2,8,128]{2,1,0:T(8,128)S(1)}, f32[2,8,128]{2,1,0:T(8,128)S(1)}, u32[]{:S(2)}, u32[]{:S(2)}) collective-permute-start(f32[2,8,128]{2,1,0:T(8,128)S(1)} %get-tuple-element.58), channel_id=1, source_target_pairs={{0,8},{8,16},{16,24},{24,32},{32,40},{40,48},{48,56},{56,64},{64,7... | collective-permute-start | bytes 24584 | tf_op jit(solution)/shard_map/ppermute | solution.py:406
  153.3 9.1 %collective-permute-start.25 = (f32[2,8,128]{2,1,0:T(8,128)S(1)}, f32[2,8,128]{2,1,0:T(8,128)S(1)}, u32[]{:S(2)}, u32[]{:S(2)}) collective-permute-start(f32[2,8,128]{2,1,0:T(8,128)S(1)} %get-tuple-element.59), channel_id=1, source_target_pairs={{0,248},{8,0},{16,8},{24,16},{32,24},{40,32},{48,40},{56,48},{64,5... | collective-permute-start | bytes 24584 | tf_op jit(solution)/shard_map/ppermute | solution.py:406
  162.5 8.2 %collective-permute-start.26 = (f32[132,2,128]{2,1,0:T(2,128)S(1)}, f32[132,2,128]{2,1,0:T(2,128)S(1)}, u32[]{:S(2)}, u32[]{:S(2)}) collective-permute-start(f32[132,2,128]{2,1,0:T(2,128)S(1)} %get-tuple-element.60), channel_id=1, source_target_pairs={{0,1},{1,2},{2,3},{3,4},{4,5},{5,6},{6,7},{8,9},{9,10},{10,11},{11... | collective-permute-start | bytes 405512 | tf_op jit(solution)/shard_map/ppermute | solution.py:406
  168.7 6.0 %collective-permute-start.27 = (f32[132,2,128]{2,1,0:T(2,128)S(1)}, f32[132,2,128]{2,1,0:T(2,128)S(1)}, u32[]{:S(2)}, u32[]{:S(2)}) collective-permute-start(f32[132,2,128]{2,1,0:T(2,128)S(1)} %get-tuple-element.61), channel_id=1, source_target_pairs={{1,0},{2,1},{3,2},{4,3},{5,4},{6,5},{7,6},{9,8},{10,9},{11,10},{12... | collective-permute-start | bytes 405512 | tf_op jit(solution)/shard_map/ppermute | solution.py:406
  (25 other events, 322.6 us)

commit v2 on v0

v2 whole, which is shorter than its diff:
```python
import jax
import jax.numpy as jnp
from jax import lax
from jax.experimental import pallas as pl
from jax.experimental.pallas import tpu as pltpu
from jax.sharding import PartitionSpec as P

SWEEPS = 4
SECTOR = ("chip", "core")
AXIAL = "axial"
F32 = jnp.float32
MIB = 1024 * 1024


def call(kernel, out_shapes, args, smem=(), hbm=(), scratch=(), vmem=14, flops=10_000_000):
    spaces = [
        pltpu.SMEM if i in smem else pl.ANY if i in hbm else pltpu.VMEM
        for i in range(len(args))
    ]
    specs = [pl.BlockSpec(memory_space=space) for space in spaces]
    moved = sum(a.size * 4 for a in args)
    return pl.pallas_call(
        kernel,
        out_shape=[jax.ShapeDtypeStruct(s, F32) for s in out_shapes],
        in_specs=specs,
        out_specs=[pl.BlockSpec(memory_space=pltpu.VMEM)] * len(out_shapes),
        scratch_shapes=list(scratch),
        compiler_params=pltpu.CompilerParams(vmem_limit_bytes=vmem * MIB),
        cost_estimate=pl.CostEstimate(flops=flops, bytes_accessed=moved, transcendentals=0),
    )(*args)


def roll(x, shift, axis):
    return pltpu.roll(x, shift % x.shape[axis], axis)


def iota(shape, axis):
    return lax.broadcasted_iota(jnp.int32, shape, axis)


def place_on(axis):
    if isinstance(axis, str):
        return lax.axis_index(axis), lax.axis_size(axis)
    major, minor = axis
    size = lax.axis_size(minor)
    return lax.axis_index(major) * size + lax.axis_index(minor), lax.axis_size(major) * size


def is_even(axis):
    return place_on(axis)[0] % 2 == 0


def by_parity(even, a, b):
    return jnp.where(even, a, b), jnp.where(even, b, a)


def swapped(a, b, axis):
    if axis == SECTOR:
        n = lax.axis_size("chip") * lax.axis_size("core")
        first = [(i, i ^ 1) for i in range(n)]
        second = [(i, (i + 1) % n if i % 2 else (i - 1) % n) for i in range(n)]
        return lax.ppermute(a, SECTOR, first), lax.ppermute(b, SECTOR, second)
    n = lax.axis_size(AXIAL)
    first = [(i, i ^ 1) for i in range(n)]
    second = []
    for s in range(lax.axis_size("chip") * lax.axis_size("core")):
        for i in range(n):
            if 0 < i < n - 1:
                second.append((s * n + i, s * n + (i + 1 if i % 2 else i - 1)))
            else:
                second.append((s * n + i, (s ^ 1) * n + i))
    b = lax.ppermute(b, (*SECTOR, AXIAL), second)
    return lax.ppermute(a, AXIAL, first), b


def thermal_swaps(row_a, row_b, edge_a, edge_b):
    edges = swapped(edge_a, edge_b, AXIAL)
    return [*swapped(row_a, row_b, SECTOR), *edges]


def inner(axis):
    place, size = place_on(axis)
    return place > 0, place < size - 1


def thermal_edges_kernel(u, k, row_a, row_b, edge_a, edge_b):
    rows, depth, _ = u.shape
    even, even_slab = is_even(SECTOR), is_even(AXIAL)
    for i, x in enumerate((u, k)):
        row_a[i], row_b[i] = by_parity(even, x[rows - 1], x[0])
        for r in range(rows):
            at = slice(i * rows + r, i * rows + r + 1)
            edge_a[at], edge_b[at] = by_parity(even_slab, x[r, depth - 1 : depth], x[r, 0:1])


def beside(x, low, high):
    place = iota(x.shape, 0)
    depth = x.shape[0]
    minus = jnp.where(place == 0, low, roll(x, 1, 0))
    plus = jnp.where(place == depth - 1, high, roll(x, -1, 0))
    return minus, plus


def conduct(k, edges, radial, around, minus, plus):
    k_up, k_down, k_low, k_high = edges
    rows = k.shape[0]
    for r in range(rows):
        own = k[r]
        above = k_up if r == 0 else k[r - 1]
        radial[r] = 0.08 * (own + above)
        around[r] = 0.08 * (own + roll(own, -1, 1))
        low, high = beside(own, k_low[r], k_high[r])
        minus[r] = 0.08 * (own + low)
        plus[r] = 0.08 * (own + high)
    radial[rows] = 0.08 * (k[rows - 1] + k_down)


def edges_of(refs, which, rows, width):
    row_a, row_b, edge_a, edge_b = refs
    above, below = inner(SECTOR)
    before, after = inner(AXIAL)
    even_slab = is_even(AXIAL)
    down, up = by_parity(is_even(SECTOR), row_a[which, :, 0:width], row_b[which, :, 0:width])
    lows, highs = [], []
    for i in range(which * rows, which * rows + rows):
        high, low = by_parity(even_slab, edge_a[i : i + 1], edge_b[i : i + 1])
        lows.append(jnp.where(before, low, 0.0))
        highs.append(jnp.where(after, high, 0.0))
    return jnp.where(above, up, 0.0), jnp.where(below, down, 0.0), lows, highs


def sweep(u, edges, heat, radial, around, minus, plus):
    u_up, u_down, u_low, u_high = edges
    rows = u.shape[0]
    for r in range(rows):
        own = u[r]
        above = u_up if r == 0 else u[r - 1]
        below = u_down if r == rows - 1 else u[r + 1]
        flow = around[r] * (roll(own, -1, 1) - own)
        low, high = beside(own, u_low[r], u_high[r])
        yield r, own + (
            (flow - roll(flow, 1, 1))
            + (radial[r] * (above - own) + radial[r + 1] * (below - own))
            + (minus[r] * (low - own) + plus[r] * (high - own))
            + 0.16 * heat[r]
        )


def keep_edge(swept, out, edge_b):
    even_slab = is_even(AXIAL)
    for r, new in swept:
        depth = new.shape[0]
        out[r] = new
        edge_b[r : r + 1] = by_parity(even_slab, new[depth - 1 : depth], new[0:1])[1]


def rest_kernel(u, *refs):
    *packs, row_a, row_b, edge_a = refs
    rows, depth, width = u.shape
    even_slab = is_even(AXIAL)
    row_a[0, :, 0:width], row_b[0, :, 0:width] = by_parity(
        is_even(SECTOR), u[rows - 1], u[0]
    )
    for r in range(rows):
        edge_a[r : r + 1] = by_parity(even_slab, u[r, depth - 1 : depth], u[r, 0:1])[0]
    for out, pack in zip((row_a, row_b), packs):
        for i in range(2):
            lanes = pack.shape[2]
            out[0, :, width + i * lanes : width + (i + 1) * lanes] = pack[i]


def first_sweep_kernel(u, k, row_a, row_b, edge_a, edge_b, heat, out, edge_out, *planes):
    refs = (row_a, row_b, edge_a, edge_b)
    rows, _, width = u.shape
    conduct(k, edges_of(refs, 1, rows, width), *planes)
    keep_edge(sweep(u, edges_of(refs, 0, rows, width), heat, *planes), out, edge_out)


def sweep_kernel(u, row_a, row_b, edge_a, edge_b, heat, *rest):
    planes, (out, edge_out) = rest[:4], rest[4:]
    rows, _, width = u.shape
    edges = edges_of((row_a, row_b, edge_a, edge_b), 0, rows, width)
    keep_edge(sweep(u, edges, heat, *planes), out, edge_out)


def last_sweep_kernel(u, row_a, row_b, edge_a, edge_b, heat, *rest):
    planes, cut = rest[:4], rest[-1]
    rows, _, width = u.shape
    edges = edges_of((row_a, row_b, edge_a, edge_b), 0, rows, width)
    for r, new in sweep(u, edges, heat, *planes):
        for j in range(new.shape[1] // 128):
            cut[j, r] = new[:, 128 * j : 128 * j + 128]


def whole_kernel(cut, out):
    for r in range(out.shape[0]):
        for j in range(cut.shape[0]):
            out[r, :, 128 * j : 128 * j + 128] = cut[j, r]


def packed(tile_of, rows, width, col):
    lane = iota((8, width), 1)
    half = width // 2
    out = []
    for t in range(rows // half):
        acc = jnp.zeros((8, width), F32)
        for i in range(half):
            acc = jnp.where(lane // 2 == i, tile_of(half * t + i, 2 * i - col), acc)
        out.append(acc)
    return jnp.concatenate(out, axis=1)


def prep_kernel(v, label, diag, table, nu, pack_a, pack_b):
    rows, _, width = v.shape

    def body(r, _):
        kind = label[r]
        base = jnp.full(kind.shape, table[0], F32)
        for m in range(1, table.shape[0]):
            base = jnp.where(kind == m, table[m], base)
        here = v[r]
        nu[r] = base * (1.0 + 0.25 * here * here)
        return 0

    lax.fori_loop(0, rows, body, 0, unroll=16)
    even = iota((8, width), 1) % 2 == 0
    made = []
    for nu_col, col in ((width - 2, width - 1), (0, 0)):
        pairs = packed(lambda r, s: roll(nu[r], s, 1), rows, width, nu_col)
        mixed = packed(
            lambda r, s: jnp.where(even, roll(v[r], s, 1), roll(diag[r], s + 1, 1)),
            rows,
            width,
            col,
        )
        made.append((pairs, mixed))
    for i in range(2):
        pack_a[i], pack_b[i] = by_parity(is_even(SECTOR), made[0][i], made[1][i])


def put_packs(packs, at, even, out_a, out_b):
    for pack in packs:
        depth, lanes = pack.shape
        for j in range(lanes // 128):
            cut = pack[:, 128 * j : 128 * j + 128]
            out_a[at], out_b[at] = by_parity(even, cut[depth - 2 : depth], cut[0:2])
            at += 1


def put_edges(field, at, even, out_a, out_b):
    rows, depth, _ = field.shape
    out_a[at : at + rows], out_b[at : at + rows] = by_parity(
        even, field[:, depth - 2 : depth, :], field[:, 0:2, :]
    )


def static_packs(own_a, own_b, row_a, row_b):
    even = is_even(SECTOR)
    lanes = own_a.shape[2]
    width = row_a.shape[2] - 2 * lanes
    own_up, own_down = by_parity(even, own_a[0], own_b[0])
    spans = [slice(width + i * lanes, width + (i + 1) * lanes) for i in range(2)]
    nu_high, nu_low = by_parity(even, row_a[0, :, spans[0]], row_b[0, :, spans[0]])
    mix_high, mix_low = by_parity(even, row_a[0, :, spans[1]], row_b[0, :, spans[1]])
    return [nu_low, nu_high, own_down, own_up, mix_low, mix_high]


def edges_kernel(nu, v, diag, own_a, own_b, row_a, row_b, out_a, out_b):
    rows, depth, _ = nu.shape
    even = is_even(AXIAL)
    put_edges(nu, 0, even, out_a, out_b)
    for i, field in enumerate((v, diag)):
        out_a[rows : 2 * rows, i : i + 1], out_b[rows : 2 * rows, i : i + 1] = by_parity(
            even, field[:, depth - 1 : depth, :], field[:, 0:1, :]
        )
    put_packs(static_packs(own_a, own_b, row_a, row_b), 2 * rows, even, out_a, out_b)


def residual_packs(own_a, own_b, got_a, got_b):
    even = is_even(SECTOR)
    up, down = by_parity(even, own_a[...], own_b[...])
    high, low = by_parity(even, got_a[...], got_b[...])
    return [low, high, down, up]


def residual_edges_kernel(res, own_a, own_b, got_a, got_b, out_a, out_b):
    even = is_even(AXIAL)
    put_edges(res, 0, even, out_a, out_b)
    put_packs(residual_packs(own_a, own_b, got_a, got_b), res.shape[0], even, out_a, out_b)


def tall(own, high, low):
    empty = jnp.zeros((own.shape[0] - 4, own.shape[1]), F32)
    return jnp.concatenate([own, high, empty, low], axis=0)


def beyond(ax_a, ax_b, at):
    before, after = inner(AXIAL)
    high, low = by_parity(is_even(AXIAL), ax_a[at], ax_b[at])
    return jnp.where(after, high, 0.0), jnp.where(before, low, 0.0)


def tall_packs(packs, at, ax_a, ax_b):
    out = []
    for pack in packs:
        span = range(at, at + pack.shape[1] // 128)
        pairs = [beyond(ax_a, ax_b, j) for j in span]
        high, low = [jnp.concatenate(parts, axis=1) for parts in zip(*pairs)]
        out.append(tall(pack, high, low))
        at = span.stop
    return out


def side_of(low, high):
    return jnp.where(iota(low.shape, 1) % 2 == 1, low, high)


def axial_blur(x):
    return x + 0.5 * (roll(x, 1, 0) + roll(x, -1, 0))


def radial_blur_side(x):
    lane = iota(x.shape, 1)
    lanes = x.shape[1]
    above = jnp.where(lane < 2, 0.0, roll(x, 2, 1))
    below = jnp.where(lane >= lanes - 2, 0.0, roll(x, -2, 1))
    return x + 0.5 * (above + below)


def blur_side(low, high, down, up):
    left = low + 0.5 * roll(low + down, 1, 1)
    right = high + 0.5 * roll(high + up, -1, 1)
    return radial_blur_side(axial_blur(side_of(left, right)))


def around_blur(x, side):
    lane = iota(x.shape, 1)
    width = x.shape[1]
    before = jnp.where(lane == 0, side, roll(x, 1, 1))
    after = jnp.where(lane == width - 1, side, roll(x, -1, 1))
    return x + 0.5 * (before + after)


def radial_blur(ref, r):
    return ref[r + 1] + 0.5 * (ref[r] + ref[r + 2])


def clear_ends(*refs):
    for ref in refs:
        zero = jnp.zeros(ref.shape[1:], F32)
        ref[0] = zero
        ref[ref.shape[0] - 1] = zero


def by_half(rows, width, body, carry, unroll):
    half = width // 2
    for t in range(rows // half):

        def step(i, c, t=t):
            return body(half * t + i, t, (2 * width - 1 - 2 * i) % width, c)

        carry = lax.fori_loop(0, half, step, carry, unroll=unroll)
    return carry


def tile(ref, t, depth):
    return ref[0:depth, 128 * t : 128 * t + 128]


def setup_kernel(
    v, nu, diag, grade, mask, burden, own_a, own_b, row_a, row_b, ax_a, ax_b,
    nu_tall, main, ready, packs, main_side, v_tall, p_tall, blurred
):
    rows, depth, width = v.shape
    nu_low, nu_high, nu_down, nu_up, mix_low, mix_high = tall_packs(
        static_packs(own_a, own_b, row_a, row_b), 2 * rows, ax_a, ax_b
    )
    odd = iota(mix_low.shape, 1) % 2 == 1
    v_side = jnp.where(odd, roll(mix_low, 1, 1), mix_high)
    diag_side = jnp.where(odd, mix_low, roll(mix_high, -1, 1))
    nu_side = side_of(nu_low, nu_high)
    for i, pack in enumerate((nu_low, nu_high, nu_down, nu_up)):
        packs[i] = pack
    main_side[...] = diag_side + 8.0 * nu_side + blur_side(nu_low, nu_high, nu_down, nu_up)
    for i, side in enumerate((nu_side, v_side, v_side * nu_side)):
        blurred[i] = radial_blur_side(axial_blur(side))
    clear_ends(nu_tall, v_tall, p_tall)

    def fill(r, _):
        mixed_high, mixed_low = beyond(ax_a, ax_b, rows + r)
        n = tall(nu[r], *beyond(ax_a, ax_b, r))
        empty = jnp.zeros((depth - 2, width), F32)
        x = jnp.concatenate([v[r], mixed_high[0:1], empty, mixed_low[0:1]], axis=0)
        nu_tall[r + 1] = n
        v_tall[r + 1] = x
        p_tall[r + 1] = x * n
        ready[0, r] = jnp.where(mask[r] == 1, grade[r], -1).astype(F32)
        ready[1, r] = burden[r]
        main[r] = jnp.concatenate([diag[r], mixed_high[1:2], empty, mixed_low[1:2]], axis=0)
        return 0

    lax.fori_loop(0, rows, fill, 0, unroll=16)

    def body(r, t, shift, _):
        n = nu_tall[r + 1]
        side = pltpu.roll(tile(blurred.at[0], t, 2 * depth), shift, 1)
        field = around_blur(axial_blur(radial_blur(nu_tall, r)), side)
        whole = main[r] + 8.0 * n + field
        main[r] = whole
        near, weighed = [
            around_blur(
                axial_blur(radial_blur(ref, r))[0:depth],
                pltpu.roll(tile(blurred.at[i], t, depth), shift, 1),
            )
            for i, ref in ((1, v_tall), (2, p_tall))
        ]
        ready[2, r] = whole[0:depth] * v[r] - n[0:depth] * near - weighed
        return 0

    by_half(rows, width, body, 0, 16)


def residual_kernel(t, ready, rem, coer, res, pack_a, pack_b):
    rows, _, width = t.shape
    grades, knots = rem.shape

    def body(r, _):
        which = ready[0, r]
        here = t[r]
        chosen = [which == g for g in range(grades)]
        ramps = [jnp.maximum(here - (col - knots // 2), 0.0) for col in range(1, knots)]

        def value(table):
            total = None
            for col in range(knots):
                coef = jnp.zeros(here.shape, F32)
                for g in range(grades):
                    coef = jnp.where(chosen[g], table[g, col], coef)
                total = total + coef * ramps[col - 1] if col else coef
            return total

        remanence = value(rem)
        coercivity = value(coer)
        square = coercivity * coercivity
        res[r] = remanence * square / (square + ready[1, r]) - ready[2, r]
        return 0

    lax.fori_loop(0, rows, body, 0, unroll=16)
    up, down = [
        packed(lambda r, s: roll(res[r], s, 1), rows, width, col) for col in (width - 2, 0)
    ]
    pack_a[...], pack_b[...] = by_parity(is_even(SECTOR), up, down)


def gram_kernel(
    res, own_a, own_b, got_a, got_b, ax_a, ax_b, nu, main, packs, main_side,
    q, kq, sums, x_tall, p_tall, q_tall, s_tall, blurred
):
    rows, depth, width = res.shape
    before, after = inner(AXIAL)
    x_packs = tall_packs(residual_packs(own_a, own_b, got_a, got_b), rows, ax_a, ax_b)
    n_packs = [packs[i] for i in range(4)]
    p_packs = [x * n for x, n in zip(x_packs, n_packs)]
    x_side, n_side, p_side = [side_of(p[0], p[1]) for p in (x_packs, n_packs, p_packs)]
    for i, side in enumerate((x_side, p_side)):
        blurred[i] = radial_blur_side(axial_blur(side))
    q_side = main_side[...] * x_side - n_side * blur_side(*x_packs) - blur_side(*p_packs)
    clear_ends(x_tall, p_tall, q_tall, s_tall)

    def outside(shape):
        place = iota(shape, 0)
        high = jnp.logical_and(place >= depth, place < 2 * depth - 4)
        low = place >= 2 * depth - 4
        return jnp.logical_or(
            jnp.logical_and(low, jnp.logical_not(before)),
            jnp.logical_and(high, jnp.logical_not(after)),
        )

    q_side = jnp.where(outside(q_side.shape), 0.0, q_side)
    for i, side in enumerate((q_side, q_side * n_side)):
        blurred[2 + i] = radial_blur_side(axial_blur(side))

    def fill(r, _):
        x = tall(res[r], *beyond(ax_a, ax_b, r))
        x_tall[r + 1] = x
        p_tall[r + 1] = x * nu[r + 1]
        return 0

    lax.fori_loop(0, rows, fill, 0, unroll=16)
    off = outside((2 * depth, width))

    def image(r, t, shift, carry):
        a, b, c = carry
        near, weighed = [
            around_blur(
                axial_blur(radial_blur(ref, r)),
                pltpu.roll(tile(blurred.at[i], t, 2 * depth), shift, 1),
            )
            for i, ref in ((0, x_tall), (1, p_tall))
        ]
        n = nu[r + 1]
        y = jnp.where(off, 0.0, main[r] * x_tall[r + 1] - n * near - weighed)
        q_tall[r + 1] = y
        s_tall[r + 1] = y * n
        y = y[0:depth]
        q[r] = y
        x = res[r]
        return a + x * x, b + x * y, c + y * y

    none = jnp.zeros((depth, width), F32)
    a, b, c = by_half(rows, width, image, (none, none, none), 32)

    def again(r, t, shift, d):
        near, weighed = [
            around_blur(
                axial_blur(radial_blur(ref, r))[0:depth],
                pltpu.roll(tile(blurred.at[i], t, depth), shift, 1),
            )
            for i, ref in ((2, q_tall), (3, s_tall))
        ]
        x = q[r]
        y = main[r, 0:depth] * x - nu[r + 1, 0:depth] * near - weighed
        kq[r] = y
        return d + y * x

    d = by_half(rows, width, again, none, 32)
    spot = iota((1, width), 1)
    line = jnp.zeros((1, width), F32)
    for i, part in enumerate((a, b, c, d)):
        line = jnp.where(spot == i, jnp.sum(part), line)
    sums[...] = line


def final_kernel(parts, v, res, q, kq, potential, misfit):
    rows = v.shape[0]
    total = parts[...].reshape(parts.shape[0] // 8, 8, parts.shape[1])
    total = jnp.sum(jnp.sum(total, axis=0), axis=0, keepdims=True)
    rr, rq, qq, qk = [total[0:1, i : i + 1] for i in range(4)]
    alpha = rr / rq
    fresh = alpha * alpha * qq - 2.0 * alpha * rq + rr
    ratio = 1.0 + fresh / rr
    bend = ratio * ratio * rq - 2.0 * alpha * ratio * qq + alpha * alpha * qk
    again = fresh / bend
    straight = alpha + again * ratio
    cross = again * alpha
    straight = jnp.broadcast_to(straight, v.shape[1:])
    cross = jnp.broadcast_to(cross, v.shape[1:])

    def body(r, _):
        x, y = res[r], q[r]
        potential[r] = v[r] + (straight * x - cross * y)
        misfit[r] = x - straight * y + cross * kq[r]
        return 0

    lax.fori_loop(0, rows, body, 0, unroll=16)


def local(
    prior_thermal_state,
    stepped_thermal_conductance,
    dissipated_power_input,
    substance_label,
    magnet_quality_line,
    permanent_pole_mask,
    operator_main_entry,
    vector_potential_now,
    reverse_magnetizing_burden,
    inverse_permeability,
    remanence_knot_chart,
    coercivity_knot_chart,
):
    u, k, heat = prior_thermal_state, stepped_thermal_conductance, dissipated_power_input
    v, diag = vector_potential_now, operator_main_entry
    thick, depth, around = u.shape
    rows, _, width = v.shape
    block = (rows, depth, width)
    high = (rows, 2 * depth, width)
    padded = (rows + 2, 2 * depth, width)
    pack = (depth, 2 * rows)
    tall_pack = (2 * depth, 2 * rows)
    per_pack = 2 * rows // width
    sectors = lax.axis_size("chip") * lax.axis_size("core")
    slabs = lax.axis_size(AXIAL)

    row_pair, edge_pair = (2, depth, around), (2 * thick, around)
    *row, edge_a, edge_b = call(
        thermal_edges_kernel,
        [row_pair, row_pair, edge_pair, edge_pair],
        [u, k],
    )
    nu, *own = call(
        prep_kernel,
        [block, (2, *pack), (2, *pack)],
        [v, substance_label, diag, inverse_permeability],
        smem=(3,),
    )
    edge = (thick, around)
    line = (1, depth, around)
    longer = (1, depth, around + 4 * rows)
    faces = (thick + 1, depth, around)
    got = thermal_swaps(*row, edge_a, edge_b)
    u, edge_b, *planes = call(
        first_sweep_kernel,
        [u.shape, edge, faces, u.shape, u.shape, u.shape],
        [u, k, *got, heat],
    )
    *row, edge_a = call(rest_kernel, [longer, longer, edge], [u, *own])
    got = thermal_swaps(*row, edge_a, edge_b)
    static = [*own, *got[:2]]
    spread = (2 * rows + 6 * per_pack, 2, width)
    ax = call(edges_kernel, [spread, spread], [nu, v, diag, *static])
    for _ in range(SWEEPS - 2):
        u, edge_b = call(sweep_kernel, [u.shape, edge], [u, *got, heat, *planes])
        *row, edge_a = call(rest_kernel, [line, line, edge], [u])
        got = thermal_swaps(*row, edge_a, edge_b)
    ax = swapped(*ax, AXIAL)
    (cut,) = call(
        last_sweep_kernel, [(sectors, thick, depth, width)], [u, *got, heat, *planes]
    )
    sector_field = lax.all_to_all(cut, SECTOR, 0, 0).reshape(block)
    (relaxed,) = call(whole_kernel, [u.shape], [cut])
    nu_tall, main, ready, nu_packs, main_side = call(
        setup_kernel,
        [padded, high, (3, *block), (4, *tall_pack), tall_pack],
        [
            v,
            nu,
            diag,
            magnet_quality_line,
            permanent_pole_mask,
            reverse_magnetizing_burden,
            *static,
            *ax,
        ],
        scratch=[
            pltpu.VMEM(padded, F32),
            pltpu.VMEM(padded, F32),
            pltpu.VMEM((3, *tall_pack), F32),
        ],
    )
    res, *own = call(
        residual_kernel,
        [block, pack, pack],
        [sector_field, ready, remanence_knot_chart, coercivity_knot_chart],
        smem=(2, 3),
    )
    packs = [*own, *swapped(*own, SECTOR)]
    spread = (rows + 4 * per_pack, 2, width)
    ax = call(residual_edges_kernel, [spread, spread], [res, *packs])
    q, kq, sums = call(
        gram_kernel,
        [block, block, (1, width)],
        [res, *packs, *swapped(*ax, AXIAL), nu_tall, main, nu_packs, main_side],
        scratch=[pltpu.VMEM(padded, F32)] * 4 + [pltpu.VMEM((4, *tall_pack), F32)],
    )
    sums = sums + lax.ppermute(sums, "core", [(0, 1), (1, 0)])
    chips = sectors * slabs // 2
    sums = jnp.broadcast_to(sums[None], (chips, 1, width))
    sums = lax.all_to_all(sums, ("chip", AXIAL), 0, 0)
    potential, misfit = call(final_kernel, [block, block], [sums.reshape(chips, width), v, res, q, kq])
    return relaxed, potential, misfit


def solution(mesh):
    thermal = P(SECTOR, AXIAL, None)
    magnetic = P(None, AXIAL, SECTOR)
    sectors, slabs = mesh.devices.shape
    cores = mesh.devices.reshape(sectors // 2, 2, slabs)
    return jax.shard_map(
        local,
        mesh=jax.sharding.Mesh(cores, (*SECTOR, AXIAL)),
        in_specs=(thermal,) * 3 + (magnetic,) * 6 + (P(),) * 3,
        out_specs=(thermal, magnetic, magnetic),
        check_vma=False,
    )
```

time: 619 us -> 126 us (0.20); the launches traced: 609 us -> 125 us
  blocking collectives: 232 us -> 0 us
  other arithmetic: 131 us -> 0.01 us
  local copies, waits for them, and re-layouts: 74.1 us -> 12.2 us
  starting transfers between devices: 114 us -> 66.7 us
  waiting for transfers between devices: 51.6 us -> 27.6 us
  Pallas kernels: 0 us -> 17.9 us
    psum x3 -> x0, blocking collectives: 232 us -> none  [the longest x2 157 us: squares(): lax.psum(jnp.sum(recursive_misfit * recursive_misfit), ('sector', 'axial'))]
    ppermute x32 -> x23, starting transfers between devices: 96.1 us -> 42.2 us  [the longest x6 16.1 us: swapped(): b = lax.ppermute(b, (*SECTOR, AXIAL), second)]
    reduce_sum x3 -> x0, other arithmetic: 47.7 us -> none  [the longest x2 46.9 us: local(): alpha = norm_now / lax.psum(jnp.sum(direction * image), ('sector', 'axial'))]
    sub x2 -> x0, other arithmetic: 44.8 us -> none  [the longest x1 42.4 us: local(): recursive_misfit = source - stencil(both[0], nu_pad, operator_main_entry)]
    ppermute x32 -> x23, waiting for transfers between devices: 51.6 us -> 17.4 us  [the longest x6 12.8 us: swapped(): return (lax.ppermute(a, AXIAL, first), b)]
    unnamed x32 -> x44, local copies, waits for them, and re-layouts: 30.2 us -> 11.5 us
    pallas_call x0 -> x16, Pallas kernels: none -> 17.9 us  [call(): pl.pallas_call(kernel, out_shape=[jax.ShapeDtypeStruct(s, F32) for s in o...]
    add x5 -> x0, other arithmetic: 16.4 us -> none  [the longest x4 15.3 us: sweep(): return center + 0.16 * (flux + heat)]
  transfers between devices with their start and end apart: 33 -> 25, of which waited for: 18 -> 10; matrix products, arithmetic and copies ran while one was open for 6% -> 0% of each run, Pallas kernels for 0% -> 5%
where the time goes in v2:
time: 126 us; the launch traced here: 125 us
  starting transfers between devices  66.7 us (53%)
  waiting for transfers between devices  27.6 us (22%)
  Pallas kernels  17.9 us (14%)
  local copies, waits for them, and re-layouts  12.2 us (10%)
    all_to_all x1, starting transfers between devices, local(): sums = lax.all_to_all(sums, ('chip', AXIAL), 0, 0)  18.8 us
    pallas_call x16, Pallas kernels, call(): pl.pallas_call(kernel, out_shape=[jax.ShapeDtypeStruct(s, F32) for s in o...  17.9 us
    ppermute x6, starting transfers between devices, swapped(): b = lax.ppermute(b, (*SECTOR, AXIAL), second)  16.1 us
    ppermute x6, starting transfers between devices, swapped(): return (lax.ppermute(a, AXIAL, first), b)  14.4 us
    ppermute x6, waiting for transfers between devices, swapped(): return (lax.ppermute(a, AXIAL, first), b)  12.8 us
    unnamed x44, local copies, waits for them, and re-layouts  11.5 us
    ppermute x10, starting transfers between devices, swapped(): return (lax.ppermute(a, SECTOR, first), lax.ppermute(b, SECTOR, second))  9.62 us
    all_to_all x1, waiting for transfers between devices, local(): sums = lax.all_to_all(sums, ('chip', AXIAL), 0, 0)  8.21 us
  transfers between devices with their start and end apart: 25, of which 10 were waited for; matrix products, arithmetic and copies ran while one was open for 0% of the time, Pallas kernels for 5%

profile of v2, /device:TPU:1, one launch (start us, length us, event | category | flops | bytes accessed | tf_op | source)
XLA Modules:
  0.0 125.3 jit_solution(12264288710182381685)
XLA Ops:
  2.9 3.3 %collective-permute-start = (f32[2,8,4096]{2,1,0:T(8,128)S(1)}, f32[2,8,4096]{2,1,0:T(8,128)S(1)}, u32[]{:S(2)}, u32[]{:S(2)}) collective-permute-start(f32[2,8,4096]{2,1,0:T(8,128)S(1)} %get-tuple-element.46), channel_id=1, source_target_pairs={{0,8},{8,0},{16,24},{24,16},{32,40},{40,32},{48,56},{56,48},{64,72... | collective-permute-start | bytes 786440 | tf_op jit(solution)/shard_map/ppermute | solution.py:62
  7.0 6.0 %collective-permute-start.3 = (f32[8,4096]{1,0:T(8,128)S(1)}, f32[8,4096]{1,0:T(8,128)S(1)}, u32[]{:S(2)}, u32[]{:S(2)}) collective-permute-start(f32[8,4096]{1,0:T(8,128)S(1)} %get-tuple-element.49), channel_id=1, source_target_pairs={{0,8},{1,2},{2,1},{3,4},{4,3},{5,6},{6,5},{7,15},{8,0},{9,10},{10,... | collective-permute-start | bytes 393224 | tf_op jit(solution)/shard_map/ppermute | solution.py:72
  19.6 3.0 %collective-permute-start.7 = (f32[4,4096]{1,0:T(4,128)S(1)}, f32[4,4096]{1,0:T(4,128)S(1)}, u32[]{:S(2)}, u32[]{:S(2)}) collective-permute-start(f32[4,4096]{1,0:T(4,128)S(1)} %get-tuple-element.56), channel_id=1, source_target_pairs={{0,8},{1,2},{2,1},{3,4},{4,3},{5,6},{6,5},{7,15},{8,0},{9,10},{10,... | collective-permute-start | bytes 196616 | tf_op jit(solution)/shard_map/ppermute | solution.py:72
  23.5 2.8 %collective-permute-done.6.edge_a = f32[4,4096]{1,0:T(4,128)S(1)} collective-permute-done((f32[4,4096]{1,0:T(4,128)S(1)}, f32[4,4096]{1,0:T(4,128)S(1)}, u32[]{:S(2)}, u32[]{:S(2)}) %collective-permute-start.6) | collective-permute-done | bytes 65568 | tf_op jit(solution)/shard_map/ppermute | solution.py:73
  28.0 2.1 %collective-permute-start.11 = (f32[4,4096]{1,0:T(4,128)S(1)}, f32[4,4096]{1,0:T(4,128)S(1)}, u32[]{:S(2)}, u32[]{:S(2)}) collective-permute-start(f32[4,4096]{1,0:T(4,128)S(1)} %get-tuple-element.65), channel_id=1, source_target_pairs={{0,8},{1,2},{2,1},{3,4},{4,3},{5,6},{6,5},{7,15},{8,0},{9,10},{10,... | collective-permute-start | bytes 196616 | tf_op jit(solution)/shard_map/ppermute | solution.py:72
  30.2 3.9 %collective-permute-start.10 = (f32[4,4096]{1,0:T(4,128)S(1)}, f32[4,4096]{1,0:T(4,128)S(1)}, u32[]{:S(2)}, u32[]{:S(2)}) collective-permute-start(f32[4,4096]{1,0:T(4,128)S(1)} %get-tuple-element.64), channel_id=1, source_target_pairs={{0,1},{1,0},{2,3},{3,2},{4,5},{5,4},{6,7},{7,6},{8,9},{9,8},{10,11... | collective-permute-start | bytes 196616 | tf_op jit(solution)/shard_map/ppermute | solution.py:73
  36.4 2.3 %collective-permute-start.12 = (f32[1,8,4096]{2,1,0:T(8,128)S(1)}, f32[1,8,4096]{2,1,0:T(8,128)S(1)}, u32[]{:S(2)}, u32[]{:S(2)}) collective-permute-start(f32[1,8,4096]{2,1,0:T(8,128)S(1)} %get-tuple-element.67), channel_id=1, source_target_pairs={{0,8},{8,0},{16,24},{24,16},{32,40},{40,32},{48,56},{56,48},{64,72... | collective-permute-start | bytes 393224 | tf_op jit(solution)/shard_map/ppermute | solution.py:62
  38.7 2.0 %collective-permute-start.15 = (f32[4,4096]{1,0:T(4,128)S(1)}, f32[4,4096]{1,0:T(4,128)S(1)}, u32[]{:S(2)}, u32[]{:S(2)}) collective-permute-start(f32[4,4096]{1,0:T(4,128)S(1)} %get-tuple-element.70), channel_id=1, source_target_pairs={{0,8},{1,2},{2,1},{3,4},{4,3},{5,6},{6,5},{7,15},{8,0},{9,10},{10,... | collective-permute-start | bytes 196616 | tf_op jit(solution)/shard_map/ppermute | solution.py:72
  40.7 4.4 %collective-permute-start.14 = (f32[4,4096]{1,0:T(4,128)S(1)}, f32[4,4096]{1,0:T(4,128)S(1)}, u32[]{:S(2)}, u32[]{:S(2)}) collective-permute-start(f32[4,4096]{1,0:T(4,128)S(1)} %get-tuple-element.69), channel_id=1, source_target_pairs={{0,1},{1,0},{2,3},{3,2},{4,5},{5,4},{6,7},{7,6},{8,9},{9,8},{10,11... | collective-permute-start | bytes 196616 | tf_op jit(solution)/shard_map/ppermute | solution.py:73
  45.1 2.0 %collective-permute-done.14.edge_a = f32[4,4096]{1,0:T(4,128)S(1)} collective-permute-done((f32[4,4096]{1,0:T(4,128)S(1)}, f32[4,4096]{1,0:T(4,128)S(1)}, u32[]{:S(2)}, u32[]{:S(2)}) %collective-permute-start.14) | collective-permute-done | bytes 65568 | tf_op jit(solution)/shard_map/ppermute | solution.py:73
  48.5 5.7 %all-to-all-start = ((f32[32,4,8,128]{3,2,1,0:T(8,128)}), f32[32,4,8,128]{3,2,1,0:T(8,128)S(1)}, u32[]{:S(2)}, u32[]{:S(2)}) async-start(f32[32,4,8,128]{3,2,1,0:T(8,128)} %shard_map.147.cut), calls=%async_computation | async-start | bytes 1048576 | tf_op jit(solution)/shard_map/all_to_all | solution.py:620
  54.5 1.8 %collective-permute-start.16 = (f32[268,2,128]{2,1,0:T(2,128)S(1)}, f32[268,2,128]{2,1,0:T(2,128)S(1)}, u32[]{:S(2)}, u32[]{:S(2)}) collective-permute-start(f32[268,2,128]{2,1,0:T(2,128)S(1)} %get-tuple-element.72), channel_id=1, source_target_pairs={{0,1},{1,0},{2,3},{3,2},{4,5},{5,4},{6,7},{7,6},{8,9},{9,8},{10,11... | collective-permute-start | bytes 823304 | tf_op jit(solution)/shard_map/ppermute | solution.py:73
  56.9 6.3 %collective-permute-done.16.ax_a = f32[268,2,128]{2,1,0:T(2,128)S(1)} collective-permute-done((f32[268,2,128]{2,1,0:T(2,128)S(1)}, f32[268,2,128]{2,1,0:T(2,128)S(1)}, u32[]{:S(2)}, u32[]{:S(2)}) %collective-permute-start.16) | collective-permute-done | bytes 274464 | tf_op jit(solution)/shard_map/ppermute | solution.py:73
  63.2 3.0 %shard_map.150 = (f32[130,16,128]{2,1,0:T(8,128)S(1)}, f32[128,16,128]{2,1,0:T(8,128)S(1)}, f32[3,128,8,128]{3,2,1,0:T(8,128)S(1)}, f32[4,16,256]{2,1,0:T(8,128)S(1)}, f32[16,256]{1,0:T(8,128)S(1)}) custom-call(f32[128,8,128]{2,1,0:T(8,128)S(1)} %copy-done.1, f32[128,8,128]{2,1,0:T(8,128)S(1)} %get-tuple-element.71.nu, f32[128,8,128]{2,1,0:T(8,128)S(1)} %copy-done.4, ...), custom_call_target="tpu_custom_call" | custom-call | flops 10000000 | bytes 4022272 | tf_op jit(solution)/shard_map/pallas_call | solution.py:22
  68.9 1.9 %all-to-all-done = f32[32,4,8,128]{3,2,1,0:T(8,128)S(1)} async-done(((f32[32,4,8,128]{3,2,1,0:T(8,128)}), f32[32,4,8,128]{3,2,1,0:T(8,128)S(1)}, u32[]{:S(2)}, u32[]{:S(2)}) %all-to-all-start) | async-done | bytes 524320 | tf_op jit(solution)/shard_map/all_to_all | solution.py:620
  73.6 2.2 %shard_map.151 = (f32[128,8,128]{2,1,0:T(8,128)S(1)}, f32[8,256]{1,0:T(8,128)S(1)}, f32[8,256]{1,0:T(8,128)S(1)}) custom-call(f32[128,8,128]{2,1,0:T(8,128)S(1)} %bitcast.4, f32[3,128,8,128]{3,2,1,0:T(8,128)S(1)} %copy-done.10, f32[4,4]{1,0:T(4,128)S(1)} %copy-done.19, f32[4,4]{1,0:T(4,128)S(1)} %copy-done.20), custom_call_target="tpu_custom_call" | custom-call | flops 10000000 | bytes 2097280 | tf_op jit(solution)/shard_map/pallas_call | solution.py:22
  78.6 1.9 %collective-permute-done.19.got_b = f32[8,256]{1,0:T(8,128)S(1)} collective-permute-done((f32[8,256]{1,0:T(8,128)S(1)}, f32[8,256]{1,0:T(8,128)S(1)}, u32[]{:S(2)}, u32[]{:S(2)}) %collective-permute-start.19) | collective-permute-done | bytes 8224 | tf_op jit(solution)/shard_map/ppermute | solution.py:62
  80.6 3.5 %collective-permute-start.20 = (f32[136,2,128]{2,1,0:T(2,128)S(1)}, f32[136,2,128]{2,1,0:T(2,128)S(1)}, u32[]{:S(2)}, u32[]{:S(2)}) collective-permute-start(f32[136,2,128]{2,1,0:T(2,128)S(1)} %get-tuple-element.78), channel_id=1, source_target_pairs={{0,1},{1,0},{2,3},{3,2},{4,5},{5,4},{6,7},{7,6},{8,9},{9,8},{10,11... | collective-permute-start | bytes 417800 | tf_op jit(solution)/shard_map/ppermute | solution.py:73
  84.1 2.5 %collective-permute-start.21 = (f32[136,2,128]{2,1,0:T(2,128)S(1)}, f32[136,2,128]{2,1,0:T(2,128)S(1)}, u32[]{:S(2)}, u32[]{:S(2)}) collective-permute-start(f32[136,2,128]{2,1,0:T(2,128)S(1)} %get-tuple-element.79), channel_id=1, source_target_pairs={{0,8},{1,2},{2,1},{3,4},{4,3},{5,6},{6,5},{7,15},{8,0},{9,10},{10,... | collective-permute-start | bytes 417800 | tf_op jit(solution)/shard_map/ppermute | solution.py:72
  87.7 3.7 %shard_map.153 = (f32[128,8,128]{2,1,0:T(8,128)S(1)}, f32[128,8,128]{2,1,0:T(8,128)S(1)}, f32[1,128]{1,0:T(1,128)S(1)}) custom-call(f32[128,8,128]{2,1,0:T(8,128)S(1)} %get-tuple-element.75.res, f32[8,256]{1,0:T(8,128)S(1)} %get-tuple-element.76.own_a, f32[8,256]{1,0:T(8,128)S(1)} %get-tuple-element.77.own_b, f32[8,256]{1,0:T(8,128)S(1)} %collective-permute-done.18.got_a, ...), custom_call_target="tpu_custom_call" | custom-call | flops 10000000 | bytes 3031040 | tf_op jit(solution)/shard_map/pallas_call | solution.py:22
  91.4 2.1 %collective-permute-start.22 = (f32[1,128]{1,0:T(1,128)S(1)}, f32[1,128]{1,0:T(1,128)S(1)}, u32[]{:S(2)}, u32[]{:S(2)}) collective-permute-start(f32[1,128]{1,0:T(1,128)S(1)} %get-tuple-element.84), channel_id=1, source_target_pairs={{0,8},{8,0},{1,9},{9,1},{2,10},{10,2},{3,11},{11,3},{4,12},{12,4},... | collective-permute-start | bytes 1544 | tf_op jit(solution)/shard_map/ppermute | solution.py:656
  95.1 18.8 %all-to-all-start.1 = ((f32[128,1,128]{2,1,0:T(1,128)}), f32[128,1,128]{2,1,0:T(1,128)S(1)}, u32[]{:S(2)}, u32[]{:S(2)}) async-start(f32[128,1,128]{2,1,0:T(1,128)} %broadcast_in_dim.9), calls=%async_computation.1 | async-start | bytes 131072 | tf_op jit(solution)/shard_map/all_to_all | solution.py:659
  113.9 1.9 %shard_map.148 = f32[4,8,4096]{2,1,0:T(8,128)} custom-call(f32[32,4,8,128]{3,2,1,0:T(8,128)} %shard_map.147.cut), custom_call_target="tpu_custom_call" | custom-call | flops 10000000 | bytes 524288 | tf_op jit(solution)/shard_map/pallas_call | solution.py:22
  115.8 8.2 %all-to-all-done.1 = f32[128,1,128]{2,1,0:T(1,128)S(1)} async-done(((f32[128,1,128]{2,1,0:T(1,128)}), f32[128,1,128]{2,1,0:T(1,128)S(1)}, u32[]{:S(2)}, u32[]{:S(2)}) %all-to-all-start.1) | async-done | bytes 65568 | tf_op jit(solution)/shard_map/all_to_all | solution.py:659
  (88 shorter events, 29.0 us)
Async XLA Ops:
  2.9 15.5 %collective-permute-start = (f32[2,8,4096]{2,1,0:T(8,128)S(1)}, f32[2,8,4096]{2,1,0:T(8,128)S(1)}, u32[]{:S(2)}, u32[]{:S(2)}) collective-permute-start(f32[2,8,4096]{2,1,0:T(8,128)S(1)} %get-tuple-element.46), channel_id=1, source_target_pairs={{0,8},{8,0},{16,24},{24,16},{32,40},{40,32},{48,56},{56,48},{64,72... | collective-permute-start | bytes 786440 | tf_op jit(solution)/shard_map/ppermute | solution.py:62
  6.2 12.2 %collective-permute-start.1 = (f32[2,8,4096]{2,1,0:T(8,128)S(1)}, f32[2,8,4096]{2,1,0:T(8,128)S(1)}, u32[]{:S(2)}, u32[]{:S(2)}) collective-permute-start(f32[2,8,4096]{2,1,0:T(8,128)S(1)} %get-tuple-element.47), channel_id=1, source_target_pairs={{0,248},{8,16},{16,8},{24,32},{32,24},{40,48},{48,40},{56,64},{64,... | collective-permute-start | bytes 786440 | tf_op jit(solution)/shard_map/ppermute | solution.py:62
  6.2 12.2 %collective-permute-start.2 = (f32[8,4096]{1,0:T(8,128)S(1)}, f32[8,4096]{1,0:T(8,128)S(1)}, u32[]{:S(2)}, u32[]{:S(2)}) collective-permute-start(f32[8,4096]{1,0:T(8,128)S(1)} %get-tuple-element.48), channel_id=1, source_target_pairs={{0,1},{1,0},{2,3},{3,2},{4,5},{5,4},{6,7},{7,6},{8,9},{9,8},{10,11... | collective-permute-start | bytes 393224 | tf_op jit(solution)/shard_map/ppermute | solution.py:73
  7.0 11.4 %collective-permute-start.3 = (f32[8,4096]{1,0:T(8,128)S(1)}, f32[8,4096]{1,0:T(8,128)S(1)}, u32[]{:S(2)}, u32[]{:S(2)}) collective-permute-start(f32[8,4096]{1,0:T(8,128)S(1)} %get-tuple-element.49), channel_id=1, source_target_pairs={{0,8},{1,2},{2,1},{3,4},{4,3},{5,6},{6,5},{7,15},{8,0},{9,10},{10,... | collective-permute-start | bytes 393224 | tf_op jit(solution)/shard_map/ppermute | solution.py:72
  19.4 6.9 %collective-permute-start.4 = (f32[1,8,4608]{2,1,0:T(8,128)S(1)}, f32[1,8,4608]{2,1,0:T(8,128)S(1)}, u32[]{:S(2)}, u32[]{:S(2)}) collective-permute-start(f32[1,8,4608]{2,1,0:T(8,128)S(1)} %get-tuple-element.53), channel_id=1, source_target_pairs={{0,8},{8,0},{16,24},{24,16},{32,40},{40,32},{48,56},{56,48},{64,72... | collective-permute-start | bytes 442376 | tf_op jit(solution)/shard_map/ppermute | solution.py:62
  19.5 6.8 %collective-permute-start.5 = (f32[1,8,4608]{2,1,0:T(8,128)S(1)}, f32[1,8,4608]{2,1,0:T(8,128)S(1)}, u32[]{:S(2)}, u32[]{:S(2)}) collective-permute-start(f32[1,8,4608]{2,1,0:T(8,128)S(1)} %get-tuple-element.54), channel_id=1, source_target_pairs={{0,248},{8,16},{16,8},{24,32},{32,24},{40,48},{48,40},{56,64},{64,... | collective-permute-start | bytes 442376 | tf_op jit(solution)/shard_map/ppermute | solution.py:62
  19.6 3.9 %collective-permute-start.7 = (f32[4,4096]{1,0:T(4,128)S(1)}, f32[4,4096]{1,0:T(4,128)S(1)}, u32[]{:S(2)}, u32[]{:S(2)}) collective-permute-start(f32[4,4096]{1,0:T(4,128)S(1)} %get-tuple-element.56), channel_id=1, source_target_pairs={{0,8},{1,2},{2,1},{3,4},{4,3},{5,6},{6,5},{7,15},{8,0},{9,10},{10,... | collective-permute-start | bytes 196616 | tf_op jit(solution)/shard_map/ppermute | solution.py:72
  22.6 3.7 %collective-permute-start.6 = (f32[4,4096]{1,0:T(4,128)S(1)}, f32[4,4096]{1,0:T(4,128)S(1)}, u32[]{:S(2)}, u32[]{:S(2)}) collective-permute-start(f32[4,4096]{1,0:T(4,128)S(1)} %get-tuple-element.55), channel_id=1, source_target_pairs={{0,1},{1,0},{2,3},{3,2},{4,5},{5,4},{6,7},{7,6},{8,9},{9,8},{10,11... | collective-permute-start | bytes 196616 | tf_op jit(solution)/shard_map/ppermute | solution.py:73
  27.0 8.7 %collective-permute-start.8 = (f32[1,8,4096]{2,1,0:T(8,128)S(1)}, f32[1,8,4096]{2,1,0:T(8,128)S(1)}, u32[]{:S(2)}, u32[]{:S(2)}) collective-permute-start(f32[1,8,4096]{2,1,0:T(8,128)S(1)} %get-tuple-element.62), channel_id=1, source_target_pairs={{0,8},{8,0},{16,24},{24,16},{32,40},{40,32},{48,56},{56,48},{64,72... | collective-permute-start | bytes 393224 | tf_op jit(solution)/shard_map/ppermute | solution.py:62
  28.0 7.7 %collective-permute-start.9 = (f32[1,8,4096]{2,1,0:T(8,128)S(1)}, f32[1,8,4096]{2,1,0:T(8,128)S(1)}, u32[]{:S(2)}, u32[]{:S(2)}) collective-permute-start(f32[1,8,4096]{2,1,0:T(8,128)S(1)} %get-tuple-element.63), channel_id=1, source_target_pairs={{0,248},{8,16},{16,8},{24,32},{32,24},{40,48},{48,40},{56,64},{64,... | collective-permute-start | bytes 393224 | tf_op jit(solution)/shard_map/ppermute | solution.py:62
  28.0 6.0 %collective-permute-start.11 = (f32[4,4096]{1,0:T(4,128)S(1)}, f32[4,4096]{1,0:T(4,128)S(1)}, u32[]{:S(2)}, u32[]{:S(2)}) collective-permute-start(f32[4,4096]{1,0:T(4,128)S(1)} %get-tuple-element.65), channel_id=1, source_target_pairs={{0,8},{1,2},{2,1},{3,4},{4,3},{5,6},{6,5},{7,15},{8,0},{9,10},{10,... | collective-permute-start | bytes 196616 | tf_op jit(solution)/shard_map/ppermute | solution.py:72
  30.2 5.6 %collective-permute-start.10 = (f32[4,4096]{1,0:T(4,128)S(1)}, f32[4,4096]{1,0:T(4,128)S(1)}, u32[]{:S(2)}, u32[]{:S(2)}) collective-permute-start(f32[4,4096]{1,0:T(4,128)S(1)} %get-tuple-element.64), channel_id=1, source_target_pairs={{0,1},{1,0},{2,3},{3,2},{4,5},{5,4},{6,7},{7,6},{8,9},{9,8},{10,11... | collective-permute-start | bytes 196616 | tf_op jit(solution)/shard_map/ppermute | solution.py:73
  36.4 10.7 %collective-permute-start.12 = (f32[1,8,4096]{2,1,0:T(8,128)S(1)}, f32[1,8,4096]{2,1,0:T(8,128)S(1)}, u32[]{:S(2)}, u32[]{:S(2)}) collective-permute-start(f32[1,8,4096]{2,1,0:T(8,128)S(1)} %get-tuple-element.67), channel_id=1, source_target_pairs={{0,8},{8,0},{16,24},{24,16},{32,40},{40,32},{48,56},{56,48},{64,72... | collective-permute-start | bytes 393224 | tf_op jit(solution)/shard_map/ppermute | solution.py:62
  38.7 8.4 %collective-permute-start.13 = (f32[1,8,4096]{2,1,0:T(8,128)S(1)}, f32[1,8,4096]{2,1,0:T(8,128)S(1)}, u32[]{:S(2)}, u32[]{:S(2)}) collective-permute-start(f32[1,8,4096]{2,1,0:T(8,128)S(1)} %get-tuple-element.68), channel_id=1, source_target_pairs={{0,248},{8,16},{16,8},{24,32},{32,24},{40,48},{48,40},{56,64},{64,... | collective-permute-start | bytes 393224 | tf_op jit(solution)/shard_map/ppermute | solution.py:62
  38.7 6.3 %collective-permute-start.15 = (f32[4,4096]{1,0:T(4,128)S(1)}, f32[4,4096]{1,0:T(4,128)S(1)}, u32[]{:S(2)}, u32[]{:S(2)}) collective-permute-start(f32[4,4096]{1,0:T(4,128)S(1)} %get-tuple-element.70), channel_id=1, source_target_pairs={{0,8},{1,2},{2,1},{3,4},{4,3},{5,6},{6,5},{7,15},{8,0},{9,10},{10,... | collective-permute-start | bytes 196616 | tf_op jit(solution)/shard_map/ppermute | solution.py:72
  40.7 6.4 %collective-permute-start.14 = (f32[4,4096]{1,0:T(4,128)S(1)}, f32[4,4096]{1,0:T(4,128)S(1)}, u32[]{:S(2)}, u32[]{:S(2)}) collective-permute-start(f32[4,4096]{1,0:T(4,128)S(1)} %get-tuple-element.69), channel_id=1, source_target_pairs={{0,1},{1,0},{2,3},{3,2},{4,5},{5,4},{6,7},{7,6},{8,9},{9,8},{10,11... | collective-permute-start | bytes 196616 | tf_op jit(solution)/shard_map/ppermute | solution.py:73
  48.5 22.4 %all-to-all-start = ((f32[32,4,8,128]{3,2,1,0:T(8,128)}), f32[32,4,8,128]{3,2,1,0:T(8,128)S(1)}, u32[]{:S(2)}, u32[]{:S(2)}) async-start(f32[32,4,8,128]{3,2,1,0:T(8,128)} %shard_map.147.cut), calls=%async_computation | async-start | bytes 1048576 | tf_op jit(solution)/shard_map/all_to_all | solution.py:620
  54.5 8.6 %collective-permute-start.16 = (f32[268,2,128]{2,1,0:T(2,128)S(1)}, f32[268,2,128]{2,1,0:T(2,128)S(1)}, u32[]{:S(2)}, u32[]{:S(2)}) collective-permute-start(f32[268,2,128]{2,1,0:T(2,128)S(1)} %get-tuple-element.72), channel_id=1, source_target_pairs={{0,1},{1,0},{2,3},{3,2},{4,5},{5,4},{6,7},{7,6},{8,9},{9,8},{10,11... | collective-permute-start | bytes 823304 | tf_op jit(solution)/shard_map/ppermute | solution.py:73
  56.4 6.8 %collective-permute-start.17 = (f32[268,2,128]{2,1,0:T(2,128)S(1)}, f32[268,2,128]{2,1,0:T(2,128)S(1)}, u32[]{:S(2)}, u32[]{:S(2)}) collective-permute-start(f32[268,2,128]{2,1,0:T(2,128)S(1)} %get-tuple-element.73), channel_id=1, source_target_pairs={{0,8},{1,2},{2,1},{3,4},{4,3},{5,6},{6,5},{7,15},{8,0},{9,10},{10,... | collective-permute-start | bytes 823304 | tf_op jit(solution)/shard_map/ppermute | solution.py:72
  77.4 3.1 %collective-permute-start.19 = (f32[8,256]{1,0:T(8,128)S(1)}, f32[8,256]{1,0:T(8,128)S(1)}, u32[]{:S(2)}, u32[]{:S(2)}) collective-permute-start(f32[8,256]{1,0:T(8,128)S(1)} %get-tuple-element.77.own_b), channel_id=1, source_target_pairs={{0,248},{8,16},{16,8},{24,32},{32,24},{40,48},{48,40},{56,64},{64,... | collective-permute-start | bytes 24584 | tf_op jit(solution)/shard_map/ppermute | solution.py:62
  80.6 6.0 %collective-permute-start.20 = (f32[136,2,128]{2,1,0:T(2,128)S(1)}, f32[136,2,128]{2,1,0:T(2,128)S(1)}, u32[]{:S(2)}, u32[]{:S(2)}) collective-permute-start(f32[136,2,128]{2,1,0:T(2,128)S(1)} %get-tuple-element.78), channel_id=1, source_target_pairs={{0,1},{1,0},{2,3},{3,2},{4,5},{5,4},{6,7},{7,6},{8,9},{9,8},{10,11... | collective-permute-start | bytes 417800 | tf_op jit(solution)/shard_map/ppermute | solution.py:73
  84.1 3.5 %collective-permute-start.21 = (f32[136,2,128]{2,1,0:T(2,128)S(1)}, f32[136,2,128]{2,1,0:T(2,128)S(1)}, u32[]{:S(2)}, u32[]{:S(2)}) collective-permute-start(f32[136,2,128]{2,1,0:T(2,128)S(1)} %get-tuple-element.79), channel_id=1, source_target_pairs={{0,8},{1,2},{2,1},{3,4},{4,3},{5,6},{6,5},{7,15},{8,0},{9,10},{10,... | collective-permute-start | bytes 417800 | tf_op jit(solution)/shard_map/ppermute | solution.py:72
  91.4 3.0 %collective-permute-start.22 = (f32[1,128]{1,0:T(1,128)S(1)}, f32[1,128]{1,0:T(1,128)S(1)}, u32[]{:S(2)}, u32[]{:S(2)}) collective-permute-start(f32[1,128]{1,0:T(1,128)S(1)} %get-tuple-element.84), channel_id=1, source_target_pairs={{0,8},{8,0},{1,9},{9,1},{2,10},{10,2},{3,11},{11,3},{4,12},{12,4},... | collective-permute-start | bytes 1544 | tf_op jit(solution)/shard_map/ppermute | solution.py:656
  95.1 28.9 %all-to-all-start.1 = ((f32[128,1,128]{2,1,0:T(1,128)}), f32[128,1,128]{2,1,0:T(1,128)S(1)}, u32[]{:S(2)}, u32[]{:S(2)}) async-start(f32[128,1,128]{2,1,0:T(1,128)} %broadcast_in_dim.9), calls=%async_computation.1 | async-start | bytes 131072 | tf_op jit(solution)/shard_map/all_to_all | solution.py:659
  (23 other events, 131.6 us)

commit v3 on v2

--- a/solution.py
+++ b/solution.py
@@ -6,18 +6,18 @@
 from jax.sharding import PartitionSpec as P
 
 SWEEPS = 4
+TABLE = (4, 4)
 SECTOR = ("chip", "core")
 AXIAL = "axial"
 F32 = jnp.float32
 MIB = 1024 * 1024
 
 
-def call(kernel, out_shapes, args, smem=(), hbm=(), scratch=(), vmem=14, flops=10_000_000):
-    spaces = [
-        pltpu.SMEM if i in smem else pl.ANY if i in hbm else pltpu.VMEM
+def call(kernel, out_shapes, args, smem=(), scratch=(), vmem=14, micros=1):
+    specs = [
+        pl.BlockSpec(memory_space=pltpu.SMEM if i in smem else pltpu.VMEM)
         for i in range(len(args))
     ]
-    specs = [pl.BlockSpec(memory_space=space) for space in spaces]
     moved = sum(a.size * 4 for a in args)
     return pl.pallas_call(
         kernel,
@@ -26,7 +26,9 @@
         out_specs=[pl.BlockSpec(memory_space=pltpu.VMEM)] * len(out_shapes),
         scratch_shapes=list(scratch),
         compiler_params=pltpu.CompilerParams(vmem_limit_bytes=vmem * MIB),
-        cost_estimate=pl.CostEstimate(flops=flops, bytes_accessed=moved, transcendentals=0),
+        cost_estimate=pl.CostEstimate(
+            flops=micros * 1_150_000_000, bytes_accessed=moved, transcendentals=0
+        ),
     )(*args)
 
 
@@ -83,36 +85,55 @@
     return place > 0, place < size - 1
 
 
-def thermal_edges_kernel(u, k, row_a, row_b, edge_a, edge_b):
+def thermal_edges_kernel(u, k, edge_a, edge_b):
     rows, depth, _ = u.shape
-    even, even_slab = is_even(SECTOR), is_even(AXIAL)
+    even_slab = is_even(AXIAL)
     for i, x in enumerate((u, k)):
-        row_a[i], row_b[i] = by_parity(even, x[rows - 1], x[0])
         for r in range(rows):
             at = slice(i * rows + r, i * rows + r + 1)
             edge_a[at], edge_b[at] = by_parity(even_slab, x[r, depth - 1 : depth], x[r, 0:1])
 
 
-def beside(x, low, high):
-    place = iota(x.shape, 0)
-    depth = x.shape[0]
-    minus = jnp.where(place == 0, low, roll(x, 1, 0))
-    plus = jnp.where(place == depth - 1, high, roll(x, -1, 0))
-    return minus, plus
-
-
-def conduct(k, edges, radial, around, minus, plus):
-    k_up, k_down, k_low, k_high = edges
-    rows = k.shape[0]
+def own_fluxes(u, heat, around, radial, minus, plus):
+    for r in range(u.shape[0]):
+        own = u[r]
+        flow = around[r] * (roll(own, -1, 1) - own)
+        new = own + (flow - roll(flow, 1, 1)) + 0.16 * heat[r]
+        if r > 0:
+            new = new + radial[r - 1] * (u[r - 1] - own)
+        if r < u.shape[0] - 1:
+            new = new + radial[r] * (u[r + 1] - own)
+        yield r, new + (
+            minus[r] * (roll(own, 1, 0) - own) + plus[r] * (roll(own, -1, 0) - own)
+        )
+
+
+def first_inner_kernel(u, k, heat, part, around, radial, minus, plus):
+    rows, depth, _ = u.shape
     for r in range(rows):
         own = k[r]
-        above = k_up if r == 0 else k[r - 1]
-        radial[r] = 0.08 * (own + above)
+        place = iota(own.shape, 0)
         around[r] = 0.08 * (own + roll(own, -1, 1))
-        low, high = beside(own, k_low[r], k_high[r])
-        minus[r] = 0.08 * (own + low)
-        plus[r] = 0.08 * (own + high)
-    radial[rows] = 0.08 * (k[rows - 1] + k_down)
+        minus[r] = jnp.where(place == 0, 0.0, 0.08 * (own + roll(own, 1, 0)))
+        plus[r] = jnp.where(place == depth - 1, 0.0, 0.08 * (own + roll(own, -1, 0)))
+        if r:
+            radial[r - 1] = 0.08 * (own + k[r - 1])
+    for r, new in own_fluxes(u, heat, around, radial, minus, plus):
+        part[r] = new
+
+
+def inner_kernel(u, heat, around, radial, minus, plus, part, edge_a):
+    even_slab = is_even(AXIAL)
+    depth = u.shape[1]
+    for r, new in own_fluxes(u, heat, around, radial, minus, plus):
+        part[r] = new
+        edge_a[r : r + 1] = by_parity(even_slab, u[r, depth - 1 : depth], u[r, 0:1])[0]
+
+
+def at_ends(low, high, between):
+    place = iota(between.shape, 0)
+    depth = between.shape[0]
+    return jnp.where(place == 0, low, jnp.where(place == depth - 1, high, between))
 
 
 def edges_of(refs, which, rows, width):
@@ -129,21 +150,17 @@
     return jnp.where(above, up, 0.0), jnp.where(below, down, 0.0), lows, highs
 
 
-def sweep(u, edges, heat, radial, around, minus, plus):
+def whole_sweep(u, part, edges, ends, rim):
     u_up, u_down, u_low, u_high = edges
     rows = u.shape[0]
     for r in range(rows):
         own = u[r]
-        above = u_up if r == 0 else u[r - 1]
-        below = u_down if r == rows - 1 else u[r + 1]
-        flow = around[r] * (roll(own, -1, 1) - own)
-        low, high = beside(own, u_low[r], u_high[r])
-        yield r, own + (
-            (flow - roll(flow, 1, 1))
-            + (radial[r] * (above - own) + radial[r + 1] * (below - own))
-            + (minus[r] * (low - own) + plus[r] * (high - own))
-            + 0.16 * heat[r]
-        )
+        new = part[r] + rim[r] * (at_ends(u_low[r], u_high[r], own) - own)
+        if r == 0:
+            new = new + ends[0] * (u_up - own)
+        if r == rows - 1:
+            new = new + ends[1] * (u_down - own)
+        yield r, new
 
 
 def keep_edge(swept, out, edge_b):
@@ -154,41 +171,45 @@
         edge_b[r : r + 1] = by_parity(even_slab, new[depth - 1 : depth], new[0:1])[1]
 
 
-def rest_kernel(u, *refs):
-    *packs, row_a, row_b, edge_a = refs
-    rows, depth, width = u.shape
-    even_slab = is_even(AXIAL)
+def rows_kernel(u, *refs):
+    *packs, row_b, row_a = refs
+    rows, _, width = u.shape
     row_a[0, :, 0:width], row_b[0, :, 0:width] = by_parity(
         is_even(SECTOR), u[rows - 1], u[0]
     )
-    for r in range(rows):
-        edge_a[r : r + 1] = by_parity(even_slab, u[r, depth - 1 : depth], u[r, 0:1])[0]
     for out, pack in zip((row_a, row_b), packs):
         for i in range(2):
             lanes = pack.shape[2]
             out[0, :, width + i * lanes : width + (i + 1) * lanes] = pack[i]
 
 
-def first_sweep_kernel(u, k, row_a, row_b, edge_a, edge_b, heat, out, edge_out, *planes):
+def first_outer_kernel(
+    u, k, part, row_a, row_b, edge_a, edge_b, out, edge_out, ends, rim
+):
     refs = (row_a, row_b, edge_a, edge_b)
     rows, _, width = u.shape
-    conduct(k, edges_of(refs, 1, rows, width), *planes)
-    keep_edge(sweep(u, edges_of(refs, 0, rows, width), heat, *planes), out, edge_out)
-
-
-def sweep_kernel(u, row_a, row_b, edge_a, edge_b, heat, *rest):
-    planes, (out, edge_out) = rest[:4], rest[4:]
+    k_up, k_down, k_low, k_high = edges_of(refs, 1, rows, width)
+    ends[0] = 0.08 * (k[0] + k_up)
+    ends[1] = 0.08 * (k[rows - 1] + k_down)
+    for r in range(rows):
+        own = k[r]
+        rim[r] = at_ends(0.08 * (own + k_low[r]), 0.08 * (own + k_high[r]), 0.0 * own)
+    edges = edges_of(refs, 0, rows, width)
+    keep_edge(whole_sweep(u, part, edges, ends, rim), out, edge_out)
+
+
+def outer_kernel(u, part, ends, rim, row_a, row_b, edge_a, edge_b, out, edge_out):
     rows, _, width = u.shape
     edges = edges_of((row_a, row_b, edge_a, edge_b), 0, rows, width)
-    keep_edge(sweep(u, edges, heat, *planes), out, edge_out)
-
-
-def last_sweep_kernel(u, row_a, row_b, edge_a, edge_b, heat, *rest):
-    planes, cut = rest[:4], rest[-1]
+    keep_edge(whole_sweep(u, part, edges, ends, rim), out, edge_out)
+
+
+def last_outer_kernel(u, part, ends, rim, row_a, row_b, edge_a, edge_b, *rest):
+    cut = rest[-1]
     rows, _, width = u.shape
     edges = edges_of((row_a, row_b, edge_a, edge_b), 0, rows, width)
-    for r, new in sweep(u, edges, heat, *planes):
-        for j in range(new.shape[1] // 128):
+    for r, new in whole_sweep(u, part, edges, ends, rim):
+        for j in range(width // 128):
             cut[j, r] = new[:, 128 * j : 128 * j + 128]
 
 
@@ -210,8 +231,8 @@
     return jnp.concatenate(out, axis=1)
 
 
-def prep_kernel(v, label, diag, table, nu, pack_a, pack_b):
-    rows, _, width = v.shape
+def nu_kernel(v, label, table, nu):
+    rows = v.shape[0]
 
     def body(r, _):
         kind = label[r]
@@ -223,6 +244,10 @@
         return 0
 
     lax.fori_loop(0, rows, body, 0, unroll=16)
+
+
+def packs_kernel(nu, v, diag, pack_a, pack_b):
+    rows, _, width = v.shape
     even = iota((8, width), 1) % 2 == 0
     made = []
     for nu_col, col in ((width - 2, width - 1), (0, 0)):
@@ -265,7 +290,7 @@
     return [nu_low, nu_high, own_down, own_up, mix_low, mix_high]
 
 
-def edges_kernel(nu, v, diag, own_a, own_b, row_a, row_b, out_a, out_b):
+def edges_kernel(nu, v, diag, own_a, own_b, row_a, row_b, out_b, out_a):
     rows, depth, _ = nu.shape
     even = is_even(AXIAL)
     put_edges(nu, 0, even, out_a, out_b)
@@ -367,24 +392,27 @@
     return ref[0:depth, 128 * t : 128 * t + 128]
 
 
-def setup_kernel(
-    v, nu, diag, grade, mask, burden, own_a, own_b, row_a, row_b, ax_a, ax_b,
-    nu_tall, main, ready, packs, main_side, v_tall, p_tall, blurred
+def ready_kernel(
+    v, nu, diag, grade, mask, burden, rem, coer, own_a, own_b, row_a, row_b, ax_a, ax_b,
+    ready, nu_tall, v_tall, p_tall, blurred
 ):
     rows, depth, width = v.shape
-    nu_low, nu_high, nu_down, nu_up, mix_low, mix_high = tall_packs(
+    nu_low, nu_high, _, _, mix_low, mix_high = tall_packs(
         static_packs(own_a, own_b, row_a, row_b), 2 * rows, ax_a, ax_b
     )
     odd = iota(mix_low.shape, 1) % 2 == 1
     v_side = jnp.where(odd, roll(mix_low, 1, 1), mix_high)
-    diag_side = jnp.where(odd, mix_low, roll(mix_high, -1, 1))
     nu_side = side_of(nu_low, nu_high)
-    for i, pack in enumerate((nu_low, nu_high, nu_down, nu_up)):
-        packs[i] = pack
-    main_side[...] = diag_side + 8.0 * nu_side + blur_side(nu_low, nu_high, nu_down, nu_up)
     for i, side in enumerate((nu_side, v_side, v_side * nu_side)):
         blurred[i] = radial_blur_side(axial_blur(side))
     clear_ends(nu_tall, v_tall, p_tall)
+    grades, knots = TABLE
+    for i, table in enumerate((rem, coer)):
+        for g in range(grades):
+            for col in range(knots):
+                at = (i * grades + g) * knots + col
+                line = jnp.full((1, width), table[g, col], F32)
+                ready[3 * rows + at // depth, at % depth : at % depth + 1] = line
 
     def fill(r, _):
         mixed_high, mixed_low = beyond(ax_a, ax_b, rows + r)
@@ -394,38 +422,77 @@
         nu_tall[r + 1] = n
         v_tall[r + 1] = x
         p_tall[r + 1] = x * n
-        ready[0, r] = jnp.where(mask[r] == 1, grade[r], -1).astype(F32)
-        ready[1, r] = burden[r]
-        main[r] = jnp.concatenate([diag[r], mixed_high[1:2], empty, mixed_low[1:2]], axis=0)
+        ready[r] = jnp.where(mask[r] == 1, grade[r], -1).astype(F32)
+        ready[rows + r] = burden[r]
         return 0
 
     lax.fori_loop(0, rows, fill, 0, unroll=16)
 
     def body(r, t, shift, _):
-        n = nu_tall[r + 1]
-        side = pltpu.roll(tile(blurred.at[0], t, 2 * depth), shift, 1)
-        field = around_blur(axial_blur(radial_blur(nu_tall, r)), side)
-        whole = main[r] + 8.0 * n + field
-        main[r] = whole
-        near, weighed = [
+        field, near, weighed = [
             around_blur(
                 axial_blur(radial_blur(ref, r))[0:depth],
                 pltpu.roll(tile(blurred.at[i], t, depth), shift, 1),
             )
-            for i, ref in ((1, v_tall), (2, p_tall))
+            for i, ref in enumerate((nu_tall, v_tall, p_tall))
         ]
-        ready[2, r] = whole[0:depth] * v[r] - n[0:depth] * near - weighed
+        n = nu[r]
+        ready[2 * rows + r] = (diag[r] + 8.0 * n + field) * v[r] - n * near - weighed
         return 0
 
-    by_half(rows, width, body, 0, 16)
-
-
-def residual_kernel(t, ready, rem, coer, res, pack_a, pack_b):
-    rows, _, width = t.shape
-    grades, knots = rem.shape
+    by_half(rows, width, body, 0, 32)
+
+
+def operator_kernel(
+    nu, diag, own_a, own_b, row_a, row_b, ax_a, ax_b, res_a, res_b,
+    nu_tall, main, packs, main_side, blurred
+):
+    rows, depth, width = nu.shape
+    nu_low, nu_high, nu_down, nu_up, mix_low, mix_high = tall_packs(
+        static_packs(own_a, own_b, row_a, row_b), 2 * rows, ax_a, ax_b
+    )
+    odd = iota(mix_low.shape, 1) % 2 == 1
+    diag_side = jnp.where(odd, mix_low, roll(mix_high, -1, 1))
+    nu_side = side_of(nu_low, nu_high)
+    for i, pack in enumerate((nu_low, nu_high, nu_down, nu_up)):
+        packs[i] = pack
+    main_side[...] = diag_side + 8.0 * nu_side + blur_side(nu_low, nu_high, nu_down, nu_up)
+    blurred[...] = radial_blur_side(axial_blur(nu_side))
+    clear_ends(nu_tall)
+
+    def fill(r, _):
+        nu_tall[r + 1] = tall(nu[r], *beyond(ax_a, ax_b, r))
+        return 0
+
+    lax.fori_loop(0, rows, fill, 0, unroll=16)
+
+    def body(r, t, shift, _):
+        high, low = beyond(ax_a, ax_b, rows + r)
+        empty = jnp.zeros((depth - 2, width), F32)
+        side = pltpu.roll(tile(blurred, t, 2 * depth), shift, 1)
+        field = around_blur(axial_blur(radial_blur(nu_tall, r)), side)
+        diag_tall = jnp.concatenate([diag[r], high[1:2], empty, low[1:2]], axis=0)
+        main[r] = diag_tall + 8.0 * nu_tall[r + 1] + field
+        return 0
+
+    by_half(rows, width, body, 0, 32)
+
+
+def residual_kernel(t, ready, res, pack_a, pack_b):
+    rows, depth, width = t.shape
+    grades, knots = TABLE
+
+    def entry(i):
+        spot = 3 * rows + i // depth, slice(i % depth, i % depth + 1)
+        return jnp.broadcast_to(ready[spot], (depth, width))
+
+    tables = [
+        [[entry((i * grades + g) * knots + col) for col in range(knots)] for g in range(grades)]
+        for i in range(2)
+    ]
 
     def body(r, _):
-        which = ready[0, r]
+        which = ready[r]
         here = t[r]
         chosen = [which == g for g in range(grades)]
         ramps = [jnp.maximum(here - (col - knots // 2), 0.0) for col in range(1, knots)]
@@ -435,14 +502,14 @@
             for col in range(knots):
                 coef = jnp.zeros(here.shape, F32)
                 for g in range(grades):
-                    coef = jnp.where(chosen[g], table[g, col], coef)
+                    coef = jnp.where(chosen[g], table[g][col], coef)
                 total = total + coef * ramps[col - 1] if col else coef
             return total
 
-        remanence = value(rem)
-        coercivity = value(coer)
+        remanence, coercivity = [value(table) for table in tables]
         square = coercivity * coercivity
-        res[r] = remanence * square / (square + ready[1, r]) - ready[2, r]
+        source = remanence * square / (square + ready[rows + r])
+        res[r] = source - ready[2 * rows + r]
         return 0
 
     lax.fori_loop(0, rows, body, 0, unroll=16)
@@ -508,7 +575,7 @@
         return a + x * x, b + x * y, c + y * y
 
     none = jnp.zeros((depth, width), F32)
-    a, b, c = by_half(rows, width, image, (none, none, none), 32)
+    a, b, c = by_half(rows, width, image, (none, none, none), 64)
 
     def again(r, t, shift, d):
         near, weighed = [
@@ -523,7 +590,7 @@
         kq[r] = y
         return d + y * x
 
-    d = by_half(rows, width, again, none, 32)
+    d = by_half(rows, width, again, none, 64)
     spot = iota((1, width), 1)
     line = jnp.zeros((1, width), F32)
     for i, part in enumerate((a, b, c, d)):
@@ -582,46 +649,52 @@
     sectors = lax.axis_size("chip") * lax.axis_size("core")
     slabs = lax.axis_size(AXIAL)
 
-    row_pair, edge_pair = (2, depth, around), (2 * thick, around)
-    *row, edge_a, edge_b = call(
-        thermal_edges_kernel,
-        [row_pair, row_pair, edge_pair, edge_pair],
-        [u, k],
-    )
-    nu, *own = call(
-        prep_kernel,
-        [block, (2, *pack), (2, *pack)],
-        [v, substance_label, diag, inverse_permeability],
-        smem=(3,),
-    )
+    last, first = by_parity(is_even(SECTOR), thick - 1, 0)
+    row = [
+        jnp.concatenate([lax.dynamic_slice_in_dim(x, at, 1) for x in (u, k)])
+        for at in (last, first)
+    ]
+    edge_pair = (2 * thick, around)
+    edge_a, edge_b = call(thermal_edges_kernel, [edge_pair, edge_pair], [u, k])
+    (nu,) = call(nu_kernel, [block], [v, substance_label, inverse_permeability], smem=(2,))
+    own = call(packs_kernel, [(2, *pack), (2, *pack)], [nu, v, diag], micros=2)
     edge = (thick, around)
     line = (1, depth, around)
     longer = (1, depth, around + 4 * rows)
-    faces = (thick + 1, depth, around)
+    inner_faces = (thick - 1, depth, around)
+    part, *planes = call(
+        first_inner_kernel,
+        [u.shape, u.shape, inner_faces, u.shape, u.shape],
+        [u, k, heat],
+        micros=2,
+    )
     got = thermal_swaps(*row, edge_a, edge_b)
-    u, edge_b, *planes = call(
-        first_sweep_kernel,
-        [u.shape, edge, faces, u.shape, u.shape, u.shape],
-        [u, k, *got, heat],
-    )
-    *row, edge_a = call(rest_kernel, [longer, longer, edge], [u, *own])
-    got = thermal_swaps(*row, edge_a, edge_b)
-    static = [*own, *got[:2]]
+    u, edge_b, *faces = call(
+        first_outer_kernel,
+        [u.shape, edge, (2, depth, around), u.shape],
+        [u, k, part, *got],
+    )
+    for step in range(1, SWEEPS):
+        more = own if step == 2 else []
+        one = longer if step == 2 else line
+        row_b, row_a = call(rows_kernel, [one, one], [u, *more], micros=10)
+        part, edge_a = call(inner_kernel, [u.shape, edge], [u, heat, *planes], micros=2)
+        got = thermal_swaps(row_a, row_b, edge_a, edge_b)
+        if step == 2:
+            static = [*own, *got[:2]]
+        if step < SWEEPS - 1:
+            u, edge_b = call(outer_kernel, [u.shape, edge], [u, part, *faces, *got])
     spread = (2 * rows + 6 * per_pack, 2, width)
-    ax = call(edges_kernel, [spread, spread], [nu, v, diag, *static])
-    for _ in range(SWEEPS - 2):
-        u, edge_b = call(sweep_kernel, [u.shape, edge], [u, *got, heat, *planes])
-        *row, edge_a = call(rest_kernel, [line, line, edge], [u])
-        got = thermal_swaps(*row, edge_a, edge_b)
+    ax = call(edges_kernel, [spread, spread], [nu, v, diag, *static])[::-1]
+    (cut,) = call(
+        last_outer_kernel, [(sectors, thick, depth, width)], [u, part, *faces, *got]
+    )
     ax = swapped(*ax, AXIAL)
-    (cut,) = call(
-        last_sweep_kernel, [(sectors, thick, depth, width)], [u, *got, heat, *planes]
-    )
     sector_field = lax.all_to_all(cut, SECTOR, 0, 0).reshape(block)
     (relaxed,) = call(whole_kernel, [u.shape], [cut])
-    nu_tall, main, ready, nu_packs, main_side = call(
-        setup_kernel,
-        [padded, high, (3, *block), (4, *tall_pack), tall_pack],
+    (ready,) = call(
+        ready_kernel,
+        [(3 * rows + 2 * TABLE[0] * TABLE[1] // depth, depth, width)],
         [
             v,
             nu,
@@ -629,20 +702,27 @@
             magnet_quality_line,
             permanent_pole_mask,
             reverse_magnetizing_burden,
+            remanence_knot_chart,
+            coercivity_knot_chart,
             *static,
             *ax,
         ],
-        scratch=[
-            pltpu.VMEM(padded, F32),
-            pltpu.VMEM(padded, F32),
-            pltpu.VMEM((3, *tall_pack), F32),
-        ],
+        smem=(6, 7),
+        micros=3,
+        scratch=[pltpu.VMEM(padded, F32)] * 3 + [pltpu.VMEM((3, *tall_pack), F32)],
     )
     res, *own = call(
         residual_kernel,
         [block, pack, pack],
-        [sector_field, ready, remanence_knot_chart, coercivity_knot_chart],
-        smem=(2, 3),
+        [sector_field, ready],
+        micros=2,
+    )
+    nu_tall, main, nu_packs, main_side = call(
+        operator_kernel,
+        [padded, high, (4, *tall_pack), tall_pack],
+        [nu, diag, *static, *ax, *own],
+        micros=2,
+        scratch=[pltpu.VMEM(tall_pack, F32)],
     )
     packs = [*own, *swapped(*own, SECTOR)]
     spread = (rows + 4 * per_pack, 2, width)
@@ -652,6 +732,7 @@
         [block, block, (1, width)],
         [res, *packs, *swapped(*ax, AXIAL), nu_tall, main, nu_packs, main_side],
         scratch=[pltpu.VMEM(padded, F32)] * 4 + [pltpu.VMEM((4, *tall_pack), F32)],
+        micros=4,
     )
     sums = sums + lax.ppermute(sums, "core", [(0, 1), (1, 0)])
     chips = sectors * slabs // 2

time: 126 us -> 121 us (0.960)
  starting transfers between devices: 66.7 us -> 76.8 us
  waiting for transfers between devices: 27.6 us -> 19.6 us
  local copies, waits for them, and re-layouts: 12.2 us -> 4.54 us
    ppermute x6, starting transfers between devices: 14.4 us -> 23.3 us  [swapped(): return (lax.ppermute(a, AXIAL, first), b)]
    unnamed x44 -> x28, local copies, waits for them, and re-layouts: 11.5 us -> 2.66 us
    ppermute x6, waiting for transfers between devices: 12.8 us -> 7.73 us  [swapped(): return (lax.ppermute(a, AXIAL, first), b)]
    ppermute x10, starting transfers between devices: 9.62 us -> 12.7 us  [swapped(): return (lax.ppermute(a, SECTOR, first), lax.ppermute(b, SECTOR, second))]
    all_to_all x1, waiting for transfers between devices: 1.93 us -> 0.01 us  [local(): sector_field = lax.all_to_all(cut, SECTOR, 0, 0).reshape(block)]
    all_to_all x1, starting transfers between devices: 18.8 us -> 17.2 us  [local(): sums = lax.all_to_all(sums, ('chip', AXIAL), 0, 0)]
    pallas_call x16 -> x22, Pallas kernels: 17.9 us -> 18.7 us  [call(): pl.pallas_call(kernel, out_shape=[jax.ShapeDtypeStruct(s, F32) for s in o...]
  transfers between devices with their start and end apart: 25 -> 25, of which waited for: 10 -> 6; matrix products, arithmetic and copies ran while one was open for 0% -> 0% of each run, Pallas kernels for 5% -> 9%
where the time goes in v3:
time: 121 us
  starting transfers between devices  76.8 us (63%)
  waiting for transfers between devices  19.6 us (16%)
  Pallas kernels  18.7 us (15%)
  local copies, waits for them, and re-layouts  4.54 us (4%)
    ppermute x6, starting transfers between devices, swapped(): return (lax.ppermute(a, AXIAL, first), b)  23.3 us
    pallas_call x22, Pallas kernels, call(): pl.pallas_call(kernel, out_shape=[jax.ShapeDtypeStruct(s, F32) for s in o...  18.7 us
    all_to_all x1, starting transfers between devices, local(): sums = lax.all_to_all(sums, ('chip', AXIAL), 0, 0)  17.2 us
    ppermute x6, starting transfers between devices, swapped(): b = lax.ppermute(b, (*SECTOR, AXIAL), second)  16.2 us
    ppermute x10, starting transfers between devices, swapped(): return (lax.ppermute(a, SECTOR, first), lax.ppermute(b, SECTOR, second))  12.7 us
    all_to_all x1, waiting for transfers between devices, local(): sums = lax.all_to_all(sums, ('chip', AXIAL), 0, 0)  8.21 us
    ppermute x6, waiting for transfers between devices, swapped(): return (lax.ppermute(a, AXIAL, first), b)  7.73 us
    all_to_all x1, starting transfers between devices, local(): sector_field = lax.all_to_all(cut, SECTOR, 0, 0).reshape(block)  5.71 us
  transfers between devices with their start and end apart: 25, of which 6 were waited for; matrix products, arithmetic and copies ran while one was open for 0% of the time, Pallas kernels for 9%

profile of v3, /device:TPU:1, one launch (start us, length us, event | category | flops | bytes accessed | tf_op | source)
XLA Modules:
  0.0 120.7 jit_solution(2888476820197205107)
XLA Ops:
  1.9 3.3 %collective-permute-start = (f32[2,8,4096]{2,1,0:T(8,128)S(1)}, f32[2,8,4096]{2,1,0:T(8,128)S(1)}, u32[]{:S(2)}, u32[]{:S(2)}) collective-permute-start(f32[2,8,4096]{2,1,0:T(8,128)S(1)} %pad_maximum_fusion), channel_id=1, source_target_pairs={{0,8},{8,0},{16,24},{24,16},{32,40},{40,32},{48,56},{56,48},{64,72... | collective-permute-start | bytes 786440 | tf_op jit(solution)/shard_map/ppermute | solution.py:64
  6.2 6.1 %collective-permute-start.3 = (f32[8,4096]{1,0:T(8,128)S(1)}, f32[8,4096]{1,0:T(8,128)S(1)}, u32[]{:S(2)}, u32[]{:S(2)}) collective-permute-start(f32[8,4096]{1,0:T(8,128)S(1)} %get-tuple-element.50), channel_id=1, source_target_pairs={{0,8},{1,2},{2,1},{3,4},{4,3},{5,6},{6,5},{7,15},{8,0},{9,10},{10,... | collective-permute-start | bytes 393224 | tf_op jit(solution)/shard_map/ppermute | solution.py:74
  14.5 2.1 %collective-permute-start.4 = (f32[1,8,4096]{2,1,0:T(8,128)S(1)}, f32[1,8,4096]{2,1,0:T(8,128)S(1)}, u32[]{:S(2)}, u32[]{:S(2)}) collective-permute-start(f32[1,8,4096]{2,1,0:T(8,128)S(1)} %get-tuple-element.59), channel_id=1, source_target_pairs={{0,8},{8,0},{16,24},{24,16},{32,40},{40,32},{48,56},{56,48},{64,72... | collective-permute-start | bytes 393224 | tf_op jit(solution)/shard_map/ppermute | solution.py:64
  17.1 2.0 %collective-permute-start.6 = (f32[4,4096]{1,0:T(4,128)S(1)}, f32[4,4096]{1,0:T(4,128)S(1)}, u32[]{:S(2)}, u32[]{:S(2)}) collective-permute-start(f32[4,4096]{1,0:T(4,128)S(1)} %get-tuple-element.61), channel_id=1, source_target_pairs={{0,1},{1,0},{2,3},{3,2},{4,5},{5,4},{6,7},{7,6},{8,9},{9,8},{10,11... | collective-permute-start | bytes 196616 | tf_op jit(solution)/shard_map/ppermute | solution.py:75
  19.0 3.2 %collective-permute-start.7 = (f32[4,4096]{1,0:T(4,128)S(1)}, f32[4,4096]{1,0:T(4,128)S(1)}, u32[]{:S(2)}, u32[]{:S(2)}) collective-permute-start(f32[4,4096]{1,0:T(4,128)S(1)} %get-tuple-element.62), channel_id=1, source_target_pairs={{0,8},{1,2},{2,1},{3,4},{4,3},{5,6},{6,5},{7,15},{8,0},{9,10},{10,... | collective-permute-start | bytes 196616 | tf_op jit(solution)/shard_map/ppermute | solution.py:74
  23.4 3.3 %collective-permute-start.8 = (f32[1,8,4608]{2,1,0:T(8,128)S(1)}, f32[1,8,4608]{2,1,0:T(8,128)S(1)}, u32[]{:S(2)}, u32[]{:S(2)}) collective-permute-start(f32[1,8,4608]{2,1,0:T(8,128)S(1)} %get-tuple-element.67), channel_id=1, source_target_pairs={{0,8},{8,0},{16,24},{24,16},{32,40},{40,32},{48,56},{56,48},{64,72... | collective-permute-start | bytes 442376 | tf_op jit(solution)/shard_map/ppermute | solution.py:64
  27.3 3.3 %collective-permute-start.10 = (f32[4,4096]{1,0:T(4,128)S(1)}, f32[4,4096]{1,0:T(4,128)S(1)}, u32[]{:S(2)}, u32[]{:S(2)}) collective-permute-start(f32[4,4096]{1,0:T(4,128)S(1)} %get-tuple-element.69), channel_id=1, source_target_pairs={{0,1},{1,0},{2,3},{3,2},{4,5},{5,4},{6,7},{7,6},{8,9},{9,8},{10,11... | collective-permute-start | bytes 196616 | tf_op jit(solution)/shard_map/ppermute | solution.py:75
  30.6 3.3 %collective-permute-start.11 = (f32[4,4096]{1,0:T(4,128)S(1)}, f32[4,4096]{1,0:T(4,128)S(1)}, u32[]{:S(2)}, u32[]{:S(2)}) collective-permute-start(f32[4,4096]{1,0:T(4,128)S(1)} %get-tuple-element.70), channel_id=1, source_target_pairs={{0,8},{1,2},{2,1},{3,4},{4,3},{5,6},{6,5},{7,15},{8,0},{9,10},{10,... | collective-permute-start | bytes 196616 | tf_op jit(solution)/shard_map/ppermute | solution.py:74
  35.1 1.4 %collective-permute-start.12 = (f32[1,8,4096]{2,1,0:T(8,128)S(1)}, f32[1,8,4096]{2,1,0:T(8,128)S(1)}, u32[]{:S(2)}, u32[]{:S(2)}) collective-permute-start(f32[1,8,4096]{2,1,0:T(8,128)S(1)} %get-tuple-element.73), channel_id=1, source_target_pairs={{0,8},{8,0},{16,24},{24,16},{32,40},{40,32},{48,56},{56,48},{64,72... | collective-permute-start | bytes 393224 | tf_op jit(solution)/shard_map/ppermute | solution.py:64
  37.1 5.5 %collective-permute-start.14 = (f32[4,4096]{1,0:T(4,128)S(1)}, f32[4,4096]{1,0:T(4,128)S(1)}, u32[]{:S(2)}, u32[]{:S(2)}) collective-permute-start(f32[4,4096]{1,0:T(4,128)S(1)} %get-tuple-element.75), channel_id=1, source_target_pairs={{0,1},{1,0},{2,3},{3,2},{4,5},{5,4},{6,7},{7,6},{8,9},{9,8},{10,11... | collective-permute-start | bytes 196616 | tf_op jit(solution)/shard_map/ppermute | solution.py:75
  43.3 1.4 %collective-permute-done.14.edge_a = f32[4,4096]{1,0:T(4,128)S(1)} collective-permute-done((f32[4,4096]{1,0:T(4,128)S(1)}, f32[4,4096]{1,0:T(4,128)S(1)}, u32[]{:S(2)}, u32[]{:S(2)}) %collective-permute-start.14) | collective-permute-done | bytes 65568 | tf_op jit(solution)/shard_map/ppermute | solution.py:75
  45.7 5.7 %all-to-all-start = ((f32[32,4,8,128]{3,2,1,0:T(8,128)}), f32[32,4,8,128]{3,2,1,0:T(8,128)S(1)}, u32[]{:S(2)}, u32[]{:S(2)}) async-start(f32[32,4,8,128]{3,2,1,0:T(8,128)} %shard_map.152.cut), calls=%async_computation | async-start | bytes 1048576 | tf_op jit(solution)/shard_map/all_to_all | solution.py:693
  51.8 5.9 %collective-permute-start.16 = (f32[268,2,128]{2,1,0:T(2,128)S(1)}, f32[268,2,128]{2,1,0:T(2,128)S(1)}, u32[]{:S(2)}, u32[]{:S(2)}) collective-permute-start(f32[268,2,128]{2,1,0:T(2,128)S(1)} %get-tuple-element.77), channel_id=1, source_target_pairs={{0,1},{1,0},{2,3},{3,2},{4,5},{5,4},{6,7},{7,6},{8,9},{9,8},{10,11... | collective-permute-start | bytes 823304 | tf_op jit(solution)/shard_map/ppermute | solution.py:75
  58.3 6.3 %collective-permute-done.16.ax_a = f32[268,2,128]{2,1,0:T(2,128)S(1)} collective-permute-done((f32[268,2,128]{2,1,0:T(2,128)S(1)}, f32[268,2,128]{2,1,0:T(2,128)S(1)}, u32[]{:S(2)}, u32[]{:S(2)}) %collective-permute-start.16) | collective-permute-done | bytes 274464 | tf_op jit(solution)/shard_map/ppermute | solution.py:75
  64.6 2.8 %shard_map.155.ready = f32[388,8,128]{2,1,0:T(8,128)S(1)} custom-call(f32[128,8,128]{2,1,0:T(8,128)S(1)} %copy-done.8, f32[128,8,128]{2,1,0:T(8,128)S(1)} %shard_map.146.nu, f32[128,8,128]{2,1,0:T(8,128)S(1)} %copy-done.7, s32[128,8,128]{2,1,0:T(8,128)S(1)} %copy-done.4, s32[128,8,128]{2,1,0:T(8,128)S(1)} %copy-done.5, f32[128,8,128]{2,1,0:T(8,128)S(1)} %copy-done.6, ...), custom_call_target="tpu_custom_call" | custom-call | flops 3449999872 | bytes 4022400 | tf_op jit(solution)/shard_map/pallas_call | solution.py:22
  73.8 1.9 %collective-permute-done.19.got_b = f32[8,256]{1,0:T(8,128)S(1)} collective-permute-done((f32[8,256]{1,0:T(8,128)S(1)}, f32[8,256]{1,0:T(8,128)S(1)}, u32[]{:S(2)}, u32[]{:S(2)}) %collective-permute-start.19) | collective-permute-done | bytes 8224 | tf_op jit(solution)/shard_map/ppermute | solution.py:64
  75.9 5.9 %collective-permute-start.20 = (f32[136,2,128]{2,1,0:T(2,128)S(1)}, f32[136,2,128]{2,1,0:T(2,128)S(1)}, u32[]{:S(2)}, u32[]{:S(2)}) collective-permute-start(f32[136,2,128]{2,1,0:T(2,128)S(1)} %get-tuple-element.82), channel_id=1, source_target_pairs={{0,1},{1,0},{2,3},{3,2},{4,5},{5,4},{6,7},{7,6},{8,9},{9,8},{10,11... | collective-permute-start | bytes 417800 | tf_op jit(solution)/shard_map/ppermute | solution.py:75
  81.8 2.5 %collective-permute-start.21 = (f32[136,2,128]{2,1,0:T(2,128)S(1)}, f32[136,2,128]{2,1,0:T(2,128)S(1)}, u32[]{:S(2)}, u32[]{:S(2)}) collective-permute-start(f32[136,2,128]{2,1,0:T(2,128)S(1)} %get-tuple-element.83), channel_id=1, source_target_pairs={{0,8},{1,2},{2,1},{3,4},{4,3},{5,6},{6,5},{7,15},{8,0},{9,10},{10,... | collective-permute-start | bytes 417800 | tf_op jit(solution)/shard_map/ppermute | solution.py:74
  84.3 1.5 %shard_map.158 = (f32[130,16,128]{2,1,0:T(8,128)S(1)}, f32[128,16,128]{2,1,0:T(8,128)S(1)}, f32[4,16,256]{2,1,0:T(8,128)S(1)}, f32[16,256]{1,0:T(8,128)S(1)}) custom-call(f32[128,8,128]{2,1,0:T(8,128)S(1)} %shard_map.146.nu, f32[128,8,128]{2,1,0:T(8,128)S(1)} %copy-done.7, f32[2,8,256]{2,1,0:T(8,128)S(1)} %get-tuple-element.65.refs_0_.own_a, ...), custom_call_target="tpu_custom_call" | custom-call | flops 2300000000 | bytes 1941504 | tf_op jit(solution)/shard_map/pallas_call | solution.py:22
  85.8 3.2 %shard_map.159 = (f32[128,8,128]{2,1,0:T(8,128)S(1)}, f32[128,8,128]{2,1,0:T(8,128)S(1)}, f32[1,128]{1,0:T(1,128)S(1)}) custom-call(f32[128,8,128]{2,1,0:T(8,128)S(1)} %get-tuple-element.79.res, f32[8,256]{1,0:T(8,128)S(1)} %get-tuple-element.80.own_a.res_a, f32[8,256]{1,0:T(8,128)S(1)} %get-tuple-element.81.own_b.res_b, ...), custom_call_target="tpu_custom_call" | custom-call | flops 4600000000 | bytes 3031040 | tf_op jit(solution)/shard_map/pallas_call | solution.py:22
  89.0 1.6 %collective-permute-start.22 = (f32[1,128]{1,0:T(1,128)S(1)}, f32[1,128]{1,0:T(1,128)S(1)}, u32[]{:S(2)}, u32[]{:S(2)}) collective-permute-start(f32[1,128]{1,0:T(1,128)S(1)} %get-tuple-element.88), channel_id=1, source_target_pairs={{0,8},{8,0},{1,9},{9,1},{2,10},{10,2},{3,11},{11,3},{4,12},{12,4},... | collective-permute-start | bytes 1544 | tf_op jit(solution)/shard_map/ppermute | solution.py:737
  92.1 17.2 %all-to-all-start.1 = ((f32[128,1,128]{2,1,0:T(1,128)}), f32[128,1,128]{2,1,0:T(1,128)S(1)}, u32[]{:S(2)}, u32[]{:S(2)}) async-start(f32[128,1,128]{2,1,0:T(1,128)} %broadcast_in_dim.9), calls=%async_computation.1 | async-start | bytes 131072 | tf_op jit(solution)/shard_map/all_to_all | solution.py:740
  109.3 1.9 %shard_map.153 = f32[4,8,4096]{2,1,0:T(8,128)} custom-call(f32[32,4,8,128]{3,2,1,0:T(8,128)} %shard_map.152.cut), custom_call_target="tpu_custom_call" | custom-call | flops 1150000000 | bytes 524288 | tf_op jit(solution)/shard_map/pallas_call | solution.py:22
  111.2 8.2 %all-to-all-done.1 = f32[128,1,128]{2,1,0:T(1,128)S(1)} async-done(((f32[128,1,128]{2,1,0:T(1,128)}), f32[128,1,128]{2,1,0:T(1,128)S(1)}, u32[]{:S(2)}, u32[]{:S(2)}) %all-to-all-start.1) | async-done | bytes 65568 | tf_op jit(solution)/shard_map/all_to_all | solution.py:740
  (81 shorter events, 20.2 us)
Async XLA Ops:
  1.9 11.9 %collective-permute-start = (f32[2,8,4096]{2,1,0:T(8,128)S(1)}, f32[2,8,4096]{2,1,0:T(8,128)S(1)}, u32[]{:S(2)}, u32[]{:S(2)}) collective-permute-start(f32[2,8,4096]{2,1,0:T(8,128)S(1)} %pad_maximum_fusion), channel_id=1, source_target_pairs={{0,8},{8,0},{16,24},{24,16},{32,40},{40,32},{48,56},{56,48},{64,72... | collective-permute-start | bytes 786440 | tf_op jit(solution)/shard_map/ppermute | solution.py:64
  5.3 8.5 %collective-permute-start.1 = (f32[2,8,4096]{2,1,0:T(8,128)S(1)}, f32[2,8,4096]{2,1,0:T(8,128)S(1)}, u32[]{:S(2)}, u32[]{:S(2)}) collective-permute-start(f32[2,8,4096]{2,1,0:T(8,128)S(1)} %pad_maximum_fusion.1), channel_id=1, source_target_pairs={{0,248},{8,16},{16,8},{24,32},{32,24},{40,48},{48,40},{56,64},{64,... | collective-permute-start | bytes 786440 | tf_op jit(solution)/shard_map/ppermute | solution.py:64
  5.5 8.3 %collective-permute-start.2 = (f32[8,4096]{1,0:T(8,128)S(1)}, f32[8,4096]{1,0:T(8,128)S(1)}, u32[]{:S(2)}, u32[]{:S(2)}) collective-permute-start(f32[8,4096]{1,0:T(8,128)S(1)} %get-tuple-element.49), channel_id=1, source_target_pairs={{0,1},{1,0},{2,3},{3,2},{4,5},{5,4},{6,7},{7,6},{8,9},{9,8},{10,11... | collective-permute-start | bytes 393224 | tf_op jit(solution)/shard_map/ppermute | solution.py:75
  6.2 7.5 %collective-permute-start.3 = (f32[8,4096]{1,0:T(8,128)S(1)}, f32[8,4096]{1,0:T(8,128)S(1)}, u32[]{:S(2)}, u32[]{:S(2)}) collective-permute-start(f32[8,4096]{1,0:T(8,128)S(1)} %get-tuple-element.50), channel_id=1, source_target_pairs={{0,8},{1,2},{2,1},{3,4},{4,3},{5,6},{6,5},{7,15},{8,0},{9,10},{10,... | collective-permute-start | bytes 393224 | tf_op jit(solution)/shard_map/ppermute | solution.py:74
  14.5 8.6 %collective-permute-start.4 = (f32[1,8,4096]{2,1,0:T(8,128)S(1)}, f32[1,8,4096]{2,1,0:T(8,128)S(1)}, u32[]{:S(2)}, u32[]{:S(2)}) collective-permute-start(f32[1,8,4096]{2,1,0:T(8,128)S(1)} %get-tuple-element.59), channel_id=1, source_target_pairs={{0,8},{8,0},{16,24},{24,16},{32,40},{40,32},{48,56},{56,48},{64,72... | collective-permute-start | bytes 393224 | tf_op jit(solution)/shard_map/ppermute | solution.py:64
  16.5 6.6 %collective-permute-start.5 = (f32[1,8,4096]{2,1,0:T(8,128)S(1)}, f32[1,8,4096]{2,1,0:T(8,128)S(1)}, u32[]{:S(2)}, u32[]{:S(2)}) collective-permute-start(f32[1,8,4096]{2,1,0:T(8,128)S(1)} %get-tuple-element.60), channel_id=1, source_target_pairs={{0,248},{8,16},{16,8},{24,32},{32,24},{40,48},{48,40},{56,64},{64,... | collective-permute-start | bytes 393224 | tf_op jit(solution)/shard_map/ppermute | solution.py:64
  17.1 6.0 %collective-permute-start.6 = (f32[4,4096]{1,0:T(4,128)S(1)}, f32[4,4096]{1,0:T(4,128)S(1)}, u32[]{:S(2)}, u32[]{:S(2)}) collective-permute-start(f32[4,4096]{1,0:T(4,128)S(1)} %get-tuple-element.61), channel_id=1, source_target_pairs={{0,1},{1,0},{2,3},{3,2},{4,5},{5,4},{6,7},{7,6},{8,9},{9,8},{10,11... | collective-permute-start | bytes 196616 | tf_op jit(solution)/shard_map/ppermute | solution.py:75
  19.0 4.1 %collective-permute-start.7 = (f32[4,4096]{1,0:T(4,128)S(1)}, f32[4,4096]{1,0:T(4,128)S(1)}, u32[]{:S(2)}, u32[]{:S(2)}) collective-permute-start(f32[4,4096]{1,0:T(4,128)S(1)} %get-tuple-element.62), channel_id=1, source_target_pairs={{0,8},{1,2},{2,1},{3,4},{4,3},{5,6},{6,5},{7,15},{8,0},{9,10},{10,... | collective-permute-start | bytes 196616 | tf_op jit(solution)/shard_map/ppermute | solution.py:74
  23.4 11.4 %collective-permute-start.8 = (f32[1,8,4608]{2,1,0:T(8,128)S(1)}, f32[1,8,4608]{2,1,0:T(8,128)S(1)}, u32[]{:S(2)}, u32[]{:S(2)}) collective-permute-start(f32[1,8,4608]{2,1,0:T(8,128)S(1)} %get-tuple-element.67), channel_id=1, source_target_pairs={{0,8},{8,0},{16,24},{24,16},{32,40},{40,32},{48,56},{56,48},{64,72... | collective-permute-start | bytes 442376 | tf_op jit(solution)/shard_map/ppermute | solution.py:64
  26.8 8.0 %collective-permute-start.9 = (f32[1,8,4608]{2,1,0:T(8,128)S(1)}, f32[1,8,4608]{2,1,0:T(8,128)S(1)}, u32[]{:S(2)}, u32[]{:S(2)}) collective-permute-start(f32[1,8,4608]{2,1,0:T(8,128)S(1)} %get-tuple-element.68), channel_id=1, source_target_pairs={{0,248},{8,16},{16,8},{24,32},{32,24},{40,48},{48,40},{56,64},{64,... | collective-permute-start | bytes 442376 | tf_op jit(solution)/shard_map/ppermute | solution.py:64
  27.3 6.6 %collective-permute-start.10 = (f32[4,4096]{1,0:T(4,128)S(1)}, f32[4,4096]{1,0:T(4,128)S(1)}, u32[]{:S(2)}, u32[]{:S(2)}) collective-permute-start(f32[4,4096]{1,0:T(4,128)S(1)} %get-tuple-element.69), channel_id=1, source_target_pairs={{0,1},{1,0},{2,3},{3,2},{4,5},{5,4},{6,7},{7,6},{8,9},{9,8},{10,11... | collective-permute-start | bytes 196616 | tf_op jit(solution)/shard_map/ppermute | solution.py:75
  30.6 4.2 %collective-permute-start.11 = (f32[4,4096]{1,0:T(4,128)S(1)}, f32[4,4096]{1,0:T(4,128)S(1)}, u32[]{:S(2)}, u32[]{:S(2)}) collective-permute-start(f32[4,4096]{1,0:T(4,128)S(1)} %get-tuple-element.70), channel_id=1, source_target_pairs={{0,8},{1,2},{2,1},{3,4},{4,3},{5,6},{6,5},{7,15},{8,0},{9,10},{10,... | collective-permute-start | bytes 196616 | tf_op jit(solution)/shard_map/ppermute | solution.py:74
  35.1 9.6 %collective-permute-start.12 = (f32[1,8,4096]{2,1,0:T(8,128)S(1)}, f32[1,8,4096]{2,1,0:T(8,128)S(1)}, u32[]{:S(2)}, u32[]{:S(2)}) collective-permute-start(f32[1,8,4096]{2,1,0:T(8,128)S(1)} %get-tuple-element.73), channel_id=1, source_target_pairs={{0,8},{8,0},{16,24},{24,16},{32,40},{40,32},{48,56},{56,48},{64,72... | collective-permute-start | bytes 393224 | tf_op jit(solution)/shard_map/ppermute | solution.py:64
  36.6 8.2 %collective-permute-start.13 = (f32[1,8,4096]{2,1,0:T(8,128)S(1)}, f32[1,8,4096]{2,1,0:T(8,128)S(1)}, u32[]{:S(2)}, u32[]{:S(2)}) collective-permute-start(f32[1,8,4096]{2,1,0:T(8,128)S(1)} %get-tuple-element.74), channel_id=1, source_target_pairs={{0,248},{8,16},{16,8},{24,32},{32,24},{40,48},{48,40},{56,64},{64,... | collective-permute-start | bytes 393224 | tf_op jit(solution)/shard_map/ppermute | solution.py:64
  37.1 7.7 %collective-permute-start.14 = (f32[4,4096]{1,0:T(4,128)S(1)}, f32[4,4096]{1,0:T(4,128)S(1)}, u32[]{:S(2)}, u32[]{:S(2)}) collective-permute-start(f32[4,4096]{1,0:T(4,128)S(1)} %get-tuple-element.75), channel_id=1, source_target_pairs={{0,1},{1,0},{2,3},{3,2},{4,5},{5,4},{6,7},{7,6},{8,9},{9,8},{10,11... | collective-permute-start | bytes 196616 | tf_op jit(solution)/shard_map/ppermute | solution.py:75
  45.7 22.8 %all-to-all-start = ((f32[32,4,8,128]{3,2,1,0:T(8,128)}), f32[32,4,8,128]{3,2,1,0:T(8,128)S(1)}, u32[]{:S(2)}, u32[]{:S(2)}) async-start(f32[32,4,8,128]{3,2,1,0:T(8,128)} %shard_map.152.cut), calls=%async_computation | async-start | bytes 1048576 | tf_op jit(solution)/shard_map/all_to_all | solution.py:693
  51.8 12.7 %collective-permute-start.16 = (f32[268,2,128]{2,1,0:T(2,128)S(1)}, f32[268,2,128]{2,1,0:T(2,128)S(1)}, u32[]{:S(2)}, u32[]{:S(2)}) collective-permute-start(f32[268,2,128]{2,1,0:T(2,128)S(1)} %get-tuple-element.77), channel_id=1, source_target_pairs={{0,1},{1,0},{2,3},{3,2},{4,5},{5,4},{6,7},{7,6},{8,9},{9,8},{10,11... | collective-permute-start | bytes 823304 | tf_op jit(solution)/shard_map/ppermute | solution.py:75
  57.8 6.8 %collective-permute-start.17 = (f32[268,2,128]{2,1,0:T(2,128)S(1)}, f32[268,2,128]{2,1,0:T(2,128)S(1)}, u32[]{:S(2)}, u32[]{:S(2)}) collective-permute-start(f32[268,2,128]{2,1,0:T(2,128)S(1)} %get-tuple-element.78), channel_id=1, source_target_pairs={{0,8},{1,2},{2,1},{3,4},{4,3},{5,6},{6,5},{7,15},{8,0},{9,10},{10,... | collective-permute-start | bytes 823304 | tf_op jit(solution)/shard_map/ppermute | solution.py:74
  71.4 2.4 %collective-permute-start.18 = (f32[8,256]{1,0:T(8,128)S(1)}, f32[8,256]{1,0:T(8,128)S(1)}, u32[]{:S(2)}, u32[]{:S(2)}) collective-permute-start(f32[8,256]{1,0:T(8,128)S(1)} %get-tuple-element.80.own_a.res_a), channel_id=1, source_target_pairs={{0,8},{8,0},{16,24},{24,16},{32,40},{40,32},{48,56},{56,48},{64,72... | collective-permute-start | bytes 24584 | tf_op jit(solution)/shard_map/ppermute | solution.py:64
  72.7 3.1 %collective-permute-start.19 = (f32[8,256]{1,0:T(8,128)S(1)}, f32[8,256]{1,0:T(8,128)S(1)}, u32[]{:S(2)}, u32[]{:S(2)}) collective-permute-start(f32[8,256]{1,0:T(8,128)S(1)} %get-tuple-element.81.own_b.res_b), channel_id=1, source_target_pairs={{0,248},{8,16},{16,8},{24,32},{32,24},{40,48},{48,40},{56,64},{64,... | collective-permute-start | bytes 24584 | tf_op jit(solution)/shard_map/ppermute | solution.py:64
  75.9 9.9 %collective-permute-start.20 = (f32[136,2,128]{2,1,0:T(2,128)S(1)}, f32[136,2,128]{2,1,0:T(2,128)S(1)}, u32[]{:S(2)}, u32[]{:S(2)}) collective-permute-start(f32[136,2,128]{2,1,0:T(2,128)S(1)} %get-tuple-element.82), channel_id=1, source_target_pairs={{0,1},{1,0},{2,3},{3,2},{4,5},{5,4},{6,7},{7,6},{8,9},{9,8},{10,11... | collective-permute-start | bytes 417800 | tf_op jit(solution)/shard_map/ppermute | solution.py:75
  81.8 4.0 %collective-permute-start.21 = (f32[136,2,128]{2,1,0:T(2,128)S(1)}, f32[136,2,128]{2,1,0:T(2,128)S(1)}, u32[]{:S(2)}, u32[]{:S(2)}) collective-permute-start(f32[136,2,128]{2,1,0:T(2,128)S(1)} %get-tuple-element.83), channel_id=1, source_target_pairs={{0,8},{1,2},{2,1},{3,4},{4,3},{5,6},{6,5},{7,15},{8,0},{9,10},{10,... | collective-permute-start | bytes 417800 | tf_op jit(solution)/shard_map/ppermute | solution.py:74
  89.0 2.4 %collective-permute-start.22 = (f32[1,128]{1,0:T(1,128)S(1)}, f32[1,128]{1,0:T(1,128)S(1)}, u32[]{:S(2)}, u32[]{:S(2)}) collective-permute-start(f32[1,128]{1,0:T(1,128)S(1)} %get-tuple-element.88), channel_id=1, source_target_pairs={{0,8},{8,0},{1,9},{9,1},{2,10},{10,2},{3,11},{11,3},{4,12},{12,4},... | collective-permute-start | bytes 1544 | tf_op jit(solution)/shard_map/ppermute | solution.py:737
  92.1 27.3 %all-to-all-start.1 = ((f32[128,1,128]{2,1,0:T(1,128)}), f32[128,1,128]{2,1,0:T(1,128)S(1)}, u32[]{:S(2)}, u32[]{:S(2)}) async-start(f32[128,1,128]{2,1,0:T(1,128)} %broadcast_in_dim.9), calls=%async_computation.1 | async-start | bytes 131072 | tf_op jit(solution)/shard_map/all_to_all | solution.py:740
  (15 other events, 112.6 us)

commit v4 on v3

--- a/solution.py
+++ b/solution.py
@@ -27,7 +27,7 @@
         scratch_shapes=list(scratch),
         compiler_params=pltpu.CompilerParams(vmem_limit_bytes=vmem * MIB),
         cost_estimate=pl.CostEstimate(
-            flops=micros * 1_150_000_000, bytes_accessed=moved, transcendentals=0
+            flops=micros * 1_150_000_000, bytes_accessed=moved if micros else 0, transcendentals=0
         ),
     )(*args)
 
@@ -122,12 +122,9 @@
         part[r] = new
 
 
-def inner_kernel(u, heat, around, radial, minus, plus, part, edge_a):
-    even_slab = is_even(AXIAL)
-    depth = u.shape[1]
+def inner_kernel(u, heat, around, radial, minus, plus, part):
     for r, new in own_fluxes(u, heat, around, radial, minus, plus):
         part[r] = new
-        edge_a[r : r + 1] = by_parity(even_slab, u[r, depth - 1 : depth], u[r, 0:1])[0]
 
 
 def at_ends(low, high, between):
@@ -163,29 +160,33 @@
         yield r, new
 
 
-def keep_edge(swept, out, edge_b):
+def ends_kernel(u, edge_b, edge_a):
+    depth = u.shape[1]
     even_slab = is_even(AXIAL)
+    for r in range(u.shape[0]):
+        edge_a[r : r + 1], edge_b[r : r + 1] = by_parity(
+            even_slab, u[r, depth - 1 : depth], u[r, 0:1]
+        )
+
+
+def keep_rows(swept, rows, packs, out, row_b, row_a):
+    even = is_even(SECTOR)
     for r, new in swept:
-        depth = new.shape[0]
+        width = new.shape[1]
         out[r] = new
-        edge_b[r : r + 1] = by_parity(even_slab, new[depth - 1 : depth], new[0:1])[1]
-
-
-def rows_kernel(u, *refs):
-    *packs, row_b, row_a = refs
-    rows, _, width = u.shape
-    row_a[0, :, 0:width], row_b[0, :, 0:width] = by_parity(
-        is_even(SECTOR), u[rows - 1], u[0]
-    )
-    for out, pack in zip((row_a, row_b), packs):
+        if r == 0:
+            first = new
+    row_a[0, :, 0:width], row_b[0, :, 0:width] = by_parity(even, new, first)
+    for send, pack in zip((row_a, row_b), packs):
         for i in range(2):
             lanes = pack.shape[2]
-            out[0, :, width + i * lanes : width + (i + 1) * lanes] = pack[i]
+            send[0, :, width + i * lanes : width + (i + 1) * lanes] = pack[i]
 
 
 def first_outer_kernel(
-    u, k, part, row_a, row_b, edge_a, edge_b, out, edge_out, ends, rim
+    u, k, part, row_a, row_b, edge_a, edge_b, out, *rest
 ):
+    sent, (ends, rim) = rest[:2], rest[2:]
     refs = (row_a, row_b, edge_a, edge_b)
     rows, _, width = u.shape
     k_up, k_down, k_low, k_high = edges_of(refs, 1, rows, width)
@@ -195,13 +196,14 @@
         own = k[r]
         rim[r] = at_ends(0.08 * (own + k_low[r]), 0.08 * (own + k_high[r]), 0.0 * own)
     edges = edges_of(refs, 0, rows, width)
-    keep_edge(whole_sweep(u, part, edges, ends, rim), out, edge_out)
-
-
-def outer_kernel(u, part, ends, rim, row_a, row_b, edge_a, edge_b, out, edge_out):
+    keep_rows(whole_sweep(u, part, edges, ends, rim), rows, [], out, *sent)
+
+
+def outer_kernel(u, part, ends, rim, row_a, row_b, edge_a, edge_b, *rest):
+    packs, kept = rest[:-3], rest[-3:]
     rows, _, width = u.shape
     edges = edges_of((row_a, row_b, edge_a, edge_b), 0, rows, width)
-    keep_edge(whole_sweep(u, part, edges, ends, rim), out, edge_out)
+    keep_rows(whole_sweep(u, part, edges, ends, rim), rows, packs, *kept)
 
 
 def last_outer_kernel(u, part, ends, rim, row_a, row_b, edge_a, edge_b, *rest):
@@ -669,21 +671,23 @@
         micros=2,
     )
     got = thermal_swaps(*row, edge_a, edge_b)
-    u, edge_b, *faces = call(
+    u, row_b, row_a, *faces = call(
         first_outer_kernel,
-        [u.shape, edge, (2, depth, around), u.shape],
+        [u.shape, line, line, (2, depth, around), u.shape],
         [u, k, part, *got],
     )
     for step in range(1, SWEEPS):
-        more = own if step == 2 else []
-        one = longer if step == 2 else line
-        row_b, row_a = call(rows_kernel, [one, one], [u, *more], micros=10)
-        part, edge_a = call(inner_kernel, [u.shape, edge], [u, heat, *planes], micros=2)
+        edge_b, edge_a = call(ends_kernel, [edge, edge], [u], micros=0)
+        (part,) = call(inner_kernel, [u.shape], [u, heat, *planes], micros=0)
         got = thermal_swaps(row_a, row_b, edge_a, edge_b)
         if step == 2:
             static = [*own, *got[:2]]
         if step < SWEEPS - 1:
-            u, edge_b = call(outer_kernel, [u.shape, edge], [u, part, *faces, *got])
+            more = own if step == 1 else []
+            one = longer if step == 1 else line
+            u, row_b, row_a = call(
+                outer_kernel, [u.shape, one, one], [u, part, *faces, *got, *more]
+            )
     spread = (2 * rows + 6 * per_pack, 2, width)
     ax = call(edges_kernel, [spread, spread], [nu, v, diag, *static])[::-1]
     (cut,) = call(

time: 121 us -> 121 us (level)
  starting transfers between devices: 76.8 us -> 64.9 us
  waiting for transfers between devices: 19.6 us -> 30.6 us
    ppermute x10, waiting for transfers between devices: 1.93 us -> 13.6 us  [swapped(): return (lax.ppermute(a, SECTOR, first), lax.ppermute(b, SECTOR, second))]
    ppermute x6, starting transfers between devices: 23.3 us -> 17.3 us  [swapped(): return (lax.ppermute(a, AXIAL, first), b)]
    ppermute x6, starting transfers between devices: 16.2 us -> 11.3 us  [swapped(): b = lax.ppermute(b, (*SECTOR, AXIAL), second)]
    ppermute x10, starting transfers between devices: 12.7 us -> 10.4 us  [swapped(): return (lax.ppermute(a, SECTOR, first), lax.ppermute(b, SECTOR, second))]
    unnamed x28 -> x36, local copies, waits for them, and re-layouts: 2.66 us -> 4.74 us
  transfers between devices with their start and end apart: 25 -> 25, of which waited for: 6 -> 9; matrix products, arithmetic and copies ran while one was open for 0% -> 0% of each run, Pallas kernels for 9% -> 8%
where the time goes in v4:
time: 121 us; the launch traced here: 120 us
  starting transfers between devices  64.9 us (54%)
  waiting for transfers between devices  30.6 us (25%)
  Pallas kernels  18.3 us (15%)
  local copies, waits for them, and re-layouts  5.44 us (4%)
    pallas_call x22, Pallas kernels, call(): pl.pallas_call(kernel, out_shape=[jax.ShapeDtypeStruct(s, F32) for s in o...  18.3 us
    all_to_all x1, starting transfers between devices, local(): sums = lax.all_to_all(sums, ('chip', AXIAL), 0, 0)  18.2 us
    ppermute x6, starting transfers between devices, swapped(): return (lax.ppermute(a, AXIAL, first), b)  17.3 us
    ppermute x10, waiting for transfers between devices, swapped(): return (lax.ppermute(a, SECTOR, first), lax.ppermute(b, SECTOR, second))  13.6 us
    ppermute x6, starting transfers between devices, swapped(): b = lax.ppermute(b, (*SECTOR, AXIAL), second)  11.3 us
    ppermute x10, starting transfers between devices, swapped(): return (lax.ppermute(a, SECTOR, first), lax.ppermute(b, SECTOR, second))  10.4 us
    all_to_all x1, waiting for transfers between devices, local(): sums = lax.all_to_all(sums, ('chip', AXIAL), 0, 0)  8.21 us
    ppermute x6, waiting for transfers between devices, swapped(): return (lax.ppermute(a, AXIAL, first), b)  7.15 us
  transfers between devices with their start and end apart: 25, of which 9 were waited for; matrix products, arithmetic and copies ran while one was open for 0% of the time, Pallas kernels for 8%

profile of v4, /device:TPU:1, one launch (start us, length us, event | category | flops | bytes accessed | tf_op | source)
XLA Modules:
  0.0 120.3 jit_solution(13422561606971156927)
XLA Ops:
  2.8 2.1 %collective-permute-start.2 = (f32[8,4096]{1,0:T(8,128)S(1)}, f32[8,4096]{1,0:T(8,128)S(1)}, u32[]{:S(2)}, u32[]{:S(2)}) collective-permute-start(f32[8,4096]{1,0:T(8,128)S(1)} %get-tuple-element.46), channel_id=1, source_target_pairs={{0,1},{1,0},{2,3},{3,2},{4,5},{5,4},{6,7},{7,6},{8,9},{9,8},{10,11... | collective-permute-start | bytes 393224 | tf_op jit(solution)/shard_map/ppermute | solution.py:75
  9.4 9.5 %collective-permute-done.1.row_b = f32[2,8,4096]{2,1,0:T(8,128)S(1)} collective-permute-done((f32[2,8,4096]{2,1,0:T(8,128)S(1)}, f32[2,8,4096]{2,1,0:T(8,128)S(1)}, u32[]{:S(2)}, u32[]{:S(2)}) %collective-permute-start.1) | collective-permute-done | bytes 262176 | tf_op jit(solution)/shard_map/ppermute | solution.py:64
  22.9 2.2 %collective-permute-done.5.row_b = f32[1,8,4096]{2,1,0:T(8,128)S(1)} collective-permute-done((f32[1,8,4096]{2,1,0:T(8,128)S(1)}, f32[1,8,4096]{2,1,0:T(8,128)S(1)}, u32[]{:S(2)}, u32[]{:S(2)}) %collective-permute-start.5) | collective-permute-done | bytes 131104 | tf_op jit(solution)/shard_map/ppermute | solution.py:64
  25.3 3.7 %collective-permute-start.8 = (f32[1,8,4608]{2,1,0:T(8,128)S(1)}, f32[1,8,4608]{2,1,0:T(8,128)S(1)}, u32[]{:S(2)}, u32[]{:S(2)}) collective-permute-start(f32[1,8,4608]{2,1,0:T(8,128)S(1)} %get-tuple-element.62), channel_id=1, source_target_pairs={{0,8},{8,0},{16,24},{24,16},{32,40},{40,32},{48,56},{56,48},{64,72... | collective-permute-start | bytes 442376 | tf_op jit(solution)/shard_map/ppermute | solution.py:64
  29.0 2.2 %collective-permute-start.10 = (f32[4,4096]{1,0:T(4,128)S(1)}, f32[4,4096]{1,0:T(4,128)S(1)}, u32[]{:S(2)}, u32[]{:S(2)}) collective-permute-start(f32[4,4096]{1,0:T(4,128)S(1)} %get-tuple-element.64), channel_id=1, source_target_pairs={{0,1},{1,0},{2,3},{3,2},{4,5},{5,4},{6,7},{7,6},{8,9},{9,8},{10,11... | collective-permute-start | bytes 196616 | tf_op jit(solution)/shard_map/ppermute | solution.py:75
  31.2 4.2 %collective-permute-start.11 = (f32[4,4096]{1,0:T(4,128)S(1)}, f32[4,4096]{1,0:T(4,128)S(1)}, u32[]{:S(2)}, u32[]{:S(2)}) collective-permute-start(f32[4,4096]{1,0:T(4,128)S(1)} %get-tuple-element.65), channel_id=1, source_target_pairs={{0,8},{1,2},{2,1},{3,4},{4,3},{5,6},{6,5},{7,15},{8,0},{9,10},{10,... | collective-permute-start | bytes 196616 | tf_op jit(solution)/shard_map/ppermute | solution.py:74
  36.6 2.4 %collective-permute-start.12 = (f32[1,8,4096]{2,1,0:T(8,128)S(1)}, f32[1,8,4096]{2,1,0:T(8,128)S(1)}, u32[]{:S(2)}, u32[]{:S(2)}) collective-permute-start(f32[1,8,4096]{2,1,0:T(8,128)S(1)} %get-tuple-element.67), channel_id=1, source_target_pairs={{0,8},{8,0},{16,24},{24,16},{32,40},{40,32},{48,56},{56,48},{64,72... | collective-permute-start | bytes 393224 | tf_op jit(solution)/shard_map/ppermute | solution.py:64
  39.0 1.8 %collective-permute-start.14 = (f32[4,4096]{1,0:T(4,128)S(1)}, f32[4,4096]{1,0:T(4,128)S(1)}, u32[]{:S(2)}, u32[]{:S(2)}) collective-permute-start(f32[4,4096]{1,0:T(4,128)S(1)} %get-tuple-element.69), channel_id=1, source_target_pairs={{0,1},{1,0},{2,3},{3,2},{4,5},{5,4},{6,7},{7,6},{8,9},{9,8},{10,11... | collective-permute-start | bytes 196616 | tf_op jit(solution)/shard_map/ppermute | solution.py:75
  40.8 1.7 %collective-permute-start.15 = (f32[4,4096]{1,0:T(4,128)S(1)}, f32[4,4096]{1,0:T(4,128)S(1)}, u32[]{:S(2)}, u32[]{:S(2)}) collective-permute-start(f32[4,4096]{1,0:T(4,128)S(1)} %get-tuple-element.70), channel_id=1, source_target_pairs={{0,8},{1,2},{2,1},{3,4},{4,3},{5,6},{6,5},{7,15},{8,0},{9,10},{10,... | collective-permute-start | bytes 196616 | tf_op jit(solution)/shard_map/ppermute | solution.py:74
  44.4 6.0 %all-to-all-start = ((f32[32,4,8,128]{3,2,1,0:T(8,128)}), f32[32,4,8,128]{3,2,1,0:T(8,128)S(1)}, u32[]{:S(2)}, u32[]{:S(2)}) async-start(f32[32,4,8,128]{3,2,1,0:T(8,128)} %shard_map.152.cut), calls=%async_computation | async-start | bytes 1048576 | tf_op jit(solution)/shard_map/all_to_all | solution.py:697
  50.8 5.5 %collective-permute-start.16 = (f32[268,2,128]{2,1,0:T(2,128)S(1)}, f32[268,2,128]{2,1,0:T(2,128)S(1)}, u32[]{:S(2)}, u32[]{:S(2)}) collective-permute-start(f32[268,2,128]{2,1,0:T(2,128)S(1)} %get-tuple-element.71), channel_id=1, source_target_pairs={{0,1},{1,0},{2,3},{3,2},{4,5},{5,4},{6,7},{7,6},{8,9},{9,8},{10,11... | collective-permute-start | bytes 823304 | tf_op jit(solution)/shard_map/ppermute | solution.py:75
  56.9 6.3 %collective-permute-done.16.ax_a = f32[268,2,128]{2,1,0:T(2,128)S(1)} collective-permute-done((f32[268,2,128]{2,1,0:T(2,128)S(1)}, f32[268,2,128]{2,1,0:T(2,128)S(1)}, u32[]{:S(2)}, u32[]{:S(2)}) %collective-permute-start.16) | collective-permute-done | bytes 274464 | tf_op jit(solution)/shard_map/ppermute | solution.py:75
  63.2 2.7 %shard_map.155.ready = f32[388,8,128]{2,1,0:T(8,128)S(1)} custom-call(f32[128,8,128]{2,1,0:T(8,128)S(1)} %copy-done.10, f32[128,8,128]{2,1,0:T(8,128)S(1)} %shard_map.144.nu, f32[128,8,128]{2,1,0:T(8,128)S(1)} %copy-done.9, s32[128,8,128]{2,1,0:T(8,128)S(1)} %copy-done.6, s32[128,8,128]{2,1,0:T(8,128)S(1)} %copy-done.7, f32[128,8,128]{2,1,0:T(8,128)S(1)} %copy-done.8, ...), custom_call_target="tpu_custom_call" | custom-call | flops 3449999872 | bytes 4022400 | tf_op jit(solution)/shard_map/pallas_call | solution.py:22
  68.6 1.4 %shard_map.156 = (f32[128,8,128]{2,1,0:T(8,128)S(1)}, f32[8,256]{1,0:T(8,128)S(1)}, f32[8,256]{1,0:T(8,128)S(1)}) custom-call(f32[128,8,128]{2,1,0:T(8,128)S(1)} %bitcast.4, f32[388,8,128]{2,1,0:T(8,128)S(1)} %copy-done.17), custom_call_target="tpu_custom_call" | custom-call | flops 2300000000 | bytes 2113536 | tf_op jit(solution)/shard_map/pallas_call | solution.py:22
  70.0 1.6 %collective-permute-start.18 = (f32[8,256]{1,0:T(8,128)S(1)}, f32[8,256]{1,0:T(8,128)S(1)}, u32[]{:S(2)}, u32[]{:S(2)}) collective-permute-start(f32[8,256]{1,0:T(8,128)S(1)} %get-tuple-element.74.own_a.res_a), channel_id=1, source_target_pairs={{0,8},{8,0},{16,24},{24,16},{32,40},{40,32},{48,56},{56,48},{64,72... | collective-permute-start | bytes 24584 | tf_op jit(solution)/shard_map/ppermute | solution.py:64
  72.8 1.9 %collective-permute-done.19.got_b = f32[8,256]{1,0:T(8,128)S(1)} collective-permute-done((f32[8,256]{1,0:T(8,128)S(1)}, f32[8,256]{1,0:T(8,128)S(1)}, u32[]{:S(2)}, u32[]{:S(2)}) %collective-permute-start.19) | collective-permute-done | bytes 8224 | tf_op jit(solution)/shard_map/ppermute | solution.py:64
  74.8 5.5 %collective-permute-start.20 = (f32[136,2,128]{2,1,0:T(2,128)S(1)}, f32[136,2,128]{2,1,0:T(2,128)S(1)}, u32[]{:S(2)}, u32[]{:S(2)}) collective-permute-start(f32[136,2,128]{2,1,0:T(2,128)S(1)} %get-tuple-element.76), channel_id=1, source_target_pairs={{0,1},{1,0},{2,3},{3,2},{4,5},{5,4},{6,7},{7,6},{8,9},{9,8},{10,11... | collective-permute-start | bytes 417800 | tf_op jit(solution)/shard_map/ppermute | solution.py:75
  80.4 2.5 %collective-permute-start.21 = (f32[136,2,128]{2,1,0:T(2,128)S(1)}, f32[136,2,128]{2,1,0:T(2,128)S(1)}, u32[]{:S(2)}, u32[]{:S(2)}) collective-permute-start(f32[136,2,128]{2,1,0:T(2,128)S(1)} %get-tuple-element.77), channel_id=1, source_target_pairs={{0,8},{1,2},{2,1},{3,4},{4,3},{5,6},{6,5},{7,15},{8,0},{9,10},{10,... | collective-permute-start | bytes 417800 | tf_op jit(solution)/shard_map/ppermute | solution.py:74
  82.9 1.5 %shard_map.158 = (f32[130,16,128]{2,1,0:T(8,128)S(1)}, f32[128,16,128]{2,1,0:T(8,128)S(1)}, f32[4,16,256]{2,1,0:T(8,128)S(1)}, f32[16,256]{1,0:T(8,128)S(1)}) custom-call(f32[128,8,128]{2,1,0:T(8,128)S(1)} %copy-done.15, f32[128,8,128]{2,1,0:T(8,128)S(1)} %copy-done.9, f32[2,8,256]{2,1,0:T(8,128)S(1)} %get-tuple-element.59.rest_0_.own_a, ...), custom_call_target="tpu_custom_call" | custom-call | flops 2300000000 | bytes 1941504 | tf_op jit(solution)/shard_map/pallas_call | solution.py:22
  84.4 3.2 %shard_map.159 = (f32[128,8,128]{2,1,0:T(8,128)S(1)}, f32[128,8,128]{2,1,0:T(8,128)S(1)}, f32[1,128]{1,0:T(1,128)S(1)}) custom-call(f32[128,8,128]{2,1,0:T(8,128)S(1)} %get-tuple-element.73.res, f32[8,256]{1,0:T(8,128)S(1)} %get-tuple-element.74.own_a.res_a, f32[8,256]{1,0:T(8,128)S(1)} %get-tuple-element.75.own_b.res_b, ...), custom_call_target="tpu_custom_call" | custom-call | flops 4600000000 | bytes 3031040 | tf_op jit(solution)/shard_map/pallas_call | solution.py:22
  87.5 1.6 %collective-permute-start.22 = (f32[1,128]{1,0:T(1,128)S(1)}, f32[1,128]{1,0:T(1,128)S(1)}, u32[]{:S(2)}, u32[]{:S(2)}) collective-permute-start(f32[1,128]{1,0:T(1,128)S(1)} %get-tuple-element.82), channel_id=1, source_target_pairs={{0,8},{8,0},{1,9},{9,1},{2,10},{10,2},{3,11},{11,3},{4,12},{12,4},... | collective-permute-start | bytes 1544 | tf_op jit(solution)/shard_map/ppermute | solution.py:741
  90.7 18.2 %all-to-all-start.1 = ((f32[128,1,128]{2,1,0:T(1,128)}), f32[128,1,128]{2,1,0:T(1,128)S(1)}, u32[]{:S(2)}, u32[]{:S(2)}) async-start(f32[128,1,128]{2,1,0:T(1,128)} %broadcast_in_dim.9), calls=%async_computation.1 | async-start | bytes 131072 | tf_op jit(solution)/shard_map/all_to_all | solution.py:744
  108.9 1.9 %shard_map.153 = f32[4,8,4096]{2,1,0:T(8,128)} custom-call(f32[32,4,8,128]{3,2,1,0:T(8,128)} %shard_map.152.cut), custom_call_target="tpu_custom_call" | custom-call | flops 1150000000 | bytes 524288 | tf_op jit(solution)/shard_map/pallas_call | solution.py:22
  110.8 8.2 %all-to-all-done.1 = f32[128,1,128]{2,1,0:T(1,128)S(1)} async-done(((f32[128,1,128]{2,1,0:T(1,128)}), f32[128,1,128]{2,1,0:T(1,128)S(1)}, u32[]{:S(2)}, u32[]{:S(2)}) %all-to-all-start.1) | async-done | bytes 65568 | tf_op jit(solution)/shard_map/all_to_all | solution.py:744
  (89 shorter events, 21.3 us)
Async XLA Ops:
  2.8 6.6 %collective-permute-start.2 = (f32[8,4096]{1,0:T(8,128)S(1)}, f32[8,4096]{1,0:T(8,128)S(1)}, u32[]{:S(2)}, u32[]{:S(2)}) collective-permute-start(f32[8,4096]{1,0:T(8,128)S(1)} %get-tuple-element.46), channel_id=1, source_target_pairs={{0,1},{1,0},{2,3},{3,2},{4,5},{5,4},{6,7},{7,6},{8,9},{9,8},{10,11... | collective-permute-start | bytes 393224 | tf_op jit(solution)/shard_map/ppermute | solution.py:75
  4.9 4.4 %collective-permute-start.3 = (f32[8,4096]{1,0:T(8,128)S(1)}, f32[8,4096]{1,0:T(8,128)S(1)}, u32[]{:S(2)}, u32[]{:S(2)}) collective-permute-start(f32[8,4096]{1,0:T(8,128)S(1)} %get-tuple-element.47), channel_id=1, source_target_pairs={{0,8},{1,2},{2,1},{3,4},{4,3},{5,6},{6,5},{7,15},{8,0},{9,10},{10,... | collective-permute-start | bytes 393224 | tf_op jit(solution)/shard_map/ppermute | solution.py:74
  6.3 3.1 %collective-permute-start = (f32[2,8,4096]{2,1,0:T(8,128)S(1)}, f32[2,8,4096]{2,1,0:T(8,128)S(1)}, u32[]{:S(2)}, u32[]{:S(2)}) collective-permute-start(f32[2,8,4096]{2,1,0:T(8,128)S(1)} %pad_maximum_fusion), channel_id=1, source_target_pairs={{0,8},{8,0},{16,24},{24,16},{32,40},{40,32},{48,56},{56,48},{64,72... | collective-permute-start | bytes 786440 | tf_op jit(solution)/shard_map/ppermute | solution.py:64
  7.4 11.5 %collective-permute-start.1 = (f32[2,8,4096]{2,1,0:T(8,128)S(1)}, f32[2,8,4096]{2,1,0:T(8,128)S(1)}, u32[]{:S(2)}, u32[]{:S(2)}) collective-permute-start(f32[2,8,4096]{2,1,0:T(8,128)S(1)} %pad_maximum_fusion.1), channel_id=1, source_target_pairs={{0,248},{8,16},{16,8},{24,32},{32,24},{40,48},{48,40},{56,64},{64,... | collective-permute-start | bytes 786440 | tf_op jit(solution)/shard_map/ppermute | solution.py:64
  19.5 3.4 %collective-permute-start.6 = (f32[4,4096]{1,0:T(4,128)S(1)}, f32[4,4096]{1,0:T(4,128)S(1)}, u32[]{:S(2)}, u32[]{:S(2)}) collective-permute-start(f32[4,4096]{1,0:T(4,128)S(1)} %get-tuple-element.57), channel_id=1, source_target_pairs={{0,1},{1,0},{2,3},{3,2},{4,5},{5,4},{6,7},{7,6},{8,9},{9,8},{10,11... | collective-permute-start | bytes 196616 | tf_op jit(solution)/shard_map/ppermute | solution.py:75
  19.6 3.3 %collective-permute-start.7 = (f32[4,4096]{1,0:T(4,128)S(1)}, f32[4,4096]{1,0:T(4,128)S(1)}, u32[]{:S(2)}, u32[]{:S(2)}) collective-permute-start(f32[4,4096]{1,0:T(4,128)S(1)} %get-tuple-element.58), channel_id=1, source_target_pairs={{0,8},{1,2},{2,1},{3,4},{4,3},{5,6},{6,5},{7,15},{8,0},{9,10},{10,... | collective-permute-start | bytes 196616 | tf_op jit(solution)/shard_map/ppermute | solution.py:74
  20.6 4.4 %collective-permute-start.5 = (f32[1,8,4096]{2,1,0:T(8,128)S(1)}, f32[1,8,4096]{2,1,0:T(8,128)S(1)}, u32[]{:S(2)}, u32[]{:S(2)}) collective-permute-start(f32[1,8,4096]{2,1,0:T(8,128)S(1)} %get-tuple-element.56), channel_id=1, source_target_pairs={{0,248},{8,16},{16,8},{24,32},{32,24},{40,48},{48,40},{56,64},{64,... | collective-permute-start | bytes 393224 | tf_op jit(solution)/shard_map/ppermute | solution.py:64
  25.3 11.1 %collective-permute-start.8 = (f32[1,8,4608]{2,1,0:T(8,128)S(1)}, f32[1,8,4608]{2,1,0:T(8,128)S(1)}, u32[]{:S(2)}, u32[]{:S(2)}) collective-permute-start(f32[1,8,4608]{2,1,0:T(8,128)S(1)} %get-tuple-element.62), channel_id=1, source_target_pairs={{0,8},{8,0},{16,24},{24,16},{32,40},{40,32},{48,56},{56,48},{64,72... | collective-permute-start | bytes 442376 | tf_op jit(solution)/shard_map/ppermute | solution.py:64
  29.0 7.4 %collective-permute-start.9 = (f32[1,8,4608]{2,1,0:T(8,128)S(1)}, f32[1,8,4608]{2,1,0:T(8,128)S(1)}, u32[]{:S(2)}, u32[]{:S(2)}) collective-permute-start(f32[1,8,4608]{2,1,0:T(8,128)S(1)} %get-tuple-element.63), channel_id=1, source_target_pairs={{0,248},{8,16},{16,8},{24,32},{32,24},{40,48},{48,40},{56,64},{64,... | collective-permute-start | bytes 442376 | tf_op jit(solution)/shard_map/ppermute | solution.py:64
  29.0 7.0 %collective-permute-start.10 = (f32[4,4096]{1,0:T(4,128)S(1)}, f32[4,4096]{1,0:T(4,128)S(1)}, u32[]{:S(2)}, u32[]{:S(2)}) collective-permute-start(f32[4,4096]{1,0:T(4,128)S(1)} %get-tuple-element.64), channel_id=1, source_target_pairs={{0,1},{1,0},{2,3},{3,2},{4,5},{5,4},{6,7},{7,6},{8,9},{9,8},{10,11... | collective-permute-start | bytes 196616 | tf_op jit(solution)/shard_map/ppermute | solution.py:75
  31.2 5.1 %collective-permute-start.11 = (f32[4,4096]{1,0:T(4,128)S(1)}, f32[4,4096]{1,0:T(4,128)S(1)}, u32[]{:S(2)}, u32[]{:S(2)}) collective-permute-start(f32[4,4096]{1,0:T(4,128)S(1)} %get-tuple-element.65), channel_id=1, source_target_pairs={{0,8},{1,2},{2,1},{3,4},{4,3},{5,6},{6,5},{7,15},{8,0},{9,10},{10,... | collective-permute-start | bytes 196616 | tf_op jit(solution)/shard_map/ppermute | solution.py:74
  36.6 6.9 %collective-permute-start.12 = (f32[1,8,4096]{2,1,0:T(8,128)S(1)}, f32[1,8,4096]{2,1,0:T(8,128)S(1)}, u32[]{:S(2)}, u32[]{:S(2)}) collective-permute-start(f32[1,8,4096]{2,1,0:T(8,128)S(1)} %get-tuple-element.67), channel_id=1, source_target_pairs={{0,8},{8,0},{16,24},{24,16},{32,40},{40,32},{48,56},{56,48},{64,72... | collective-permute-start | bytes 393224 | tf_op jit(solution)/shard_map/ppermute | solution.py:64
  39.0 4.5 %collective-permute-start.13 = (f32[1,8,4096]{2,1,0:T(8,128)S(1)}, f32[1,8,4096]{2,1,0:T(8,128)S(1)}, u32[]{:S(2)}, u32[]{:S(2)}) collective-permute-start(f32[1,8,4096]{2,1,0:T(8,128)S(1)} %get-tuple-element.68), channel_id=1, source_target_pairs={{0,248},{8,16},{16,8},{24,32},{32,24},{40,48},{48,40},{56,64},{64,... | collective-permute-start | bytes 393224 | tf_op jit(solution)/shard_map/ppermute | solution.py:64
  39.0 4.0 %collective-permute-start.14 = (f32[4,4096]{1,0:T(4,128)S(1)}, f32[4,4096]{1,0:T(4,128)S(1)}, u32[]{:S(2)}, u32[]{:S(2)}) collective-permute-start(f32[4,4096]{1,0:T(4,128)S(1)} %get-tuple-element.69), channel_id=1, source_target_pairs={{0,1},{1,0},{2,3},{3,2},{4,5},{5,4},{6,7},{7,6},{8,9},{9,8},{10,11... | collective-permute-start | bytes 196616 | tf_op jit(solution)/shard_map/ppermute | solution.py:75
  40.8 2.6 %collective-permute-start.15 = (f32[4,4096]{1,0:T(4,128)S(1)}, f32[4,4096]{1,0:T(4,128)S(1)}, u32[]{:S(2)}, u32[]{:S(2)}) collective-permute-start(f32[4,4096]{1,0:T(4,128)S(1)} %get-tuple-element.70), channel_id=1, source_target_pairs={{0,8},{1,2},{2,1},{3,4},{4,3},{5,6},{6,5},{7,15},{8,0},{9,10},{10,... | collective-permute-start | bytes 196616 | tf_op jit(solution)/shard_map/ppermute | solution.py:74
  44.4 22.7 %all-to-all-start = ((f32[32,4,8,128]{3,2,1,0:T(8,128)}), f32[32,4,8,128]{3,2,1,0:T(8,128)S(1)}, u32[]{:S(2)}, u32[]{:S(2)}) async-start(f32[32,4,8,128]{3,2,1,0:T(8,128)} %shard_map.152.cut), calls=%async_computation | async-start | bytes 1048576 | tf_op jit(solution)/shard_map/all_to_all | solution.py:697
  50.8 12.3 %collective-permute-start.16 = (f32[268,2,128]{2,1,0:T(2,128)S(1)}, f32[268,2,128]{2,1,0:T(2,128)S(1)}, u32[]{:S(2)}, u32[]{:S(2)}) collective-permute-start(f32[268,2,128]{2,1,0:T(2,128)S(1)} %get-tuple-element.71), channel_id=1, source_target_pairs={{0,1},{1,0},{2,3},{3,2},{4,5},{5,4},{6,7},{7,6},{8,9},{9,8},{10,11... | collective-permute-start | bytes 823304 | tf_op jit(solution)/shard_map/ppermute | solution.py:75
  56.4 6.8 %collective-permute-start.17 = (f32[268,2,128]{2,1,0:T(2,128)S(1)}, f32[268,2,128]{2,1,0:T(2,128)S(1)}, u32[]{:S(2)}, u32[]{:S(2)}) collective-permute-start(f32[268,2,128]{2,1,0:T(2,128)S(1)} %get-tuple-element.72), channel_id=1, source_target_pairs={{0,8},{1,2},{2,1},{3,4},{4,3},{5,6},{6,5},{7,15},{8,0},{9,10},{10,... | collective-permute-start | bytes 823304 | tf_op jit(solution)/shard_map/ppermute | solution.py:74
  70.0 2.8 %collective-permute-start.18 = (f32[8,256]{1,0:T(8,128)S(1)}, f32[8,256]{1,0:T(8,128)S(1)}, u32[]{:S(2)}, u32[]{:S(2)}) collective-permute-start(f32[8,256]{1,0:T(8,128)S(1)} %get-tuple-element.74.own_a.res_a), channel_id=1, source_target_pairs={{0,8},{8,0},{16,24},{24,16},{32,40},{40,32},{48,56},{56,48},{64,72... | collective-permute-start | bytes 24584 | tf_op jit(solution)/shard_map/ppermute | solution.py:64
  71.6 3.1 %collective-permute-start.19 = (f32[8,256]{1,0:T(8,128)S(1)}, f32[8,256]{1,0:T(8,128)S(1)}, u32[]{:S(2)}, u32[]{:S(2)}) collective-permute-start(f32[8,256]{1,0:T(8,128)S(1)} %get-tuple-element.75.own_b.res_b), channel_id=1, source_target_pairs={{0,248},{8,16},{16,8},{24,32},{32,24},{40,48},{48,40},{56,64},{64,... | collective-permute-start | bytes 24584 | tf_op jit(solution)/shard_map/ppermute | solution.py:64
  74.8 9.5 %collective-permute-start.20 = (f32[136,2,128]{2,1,0:T(2,128)S(1)}, f32[136,2,128]{2,1,0:T(2,128)S(1)}, u32[]{:S(2)}, u32[]{:S(2)}) collective-permute-start(f32[136,2,128]{2,1,0:T(2,128)S(1)} %get-tuple-element.76), channel_id=1, source_target_pairs={{0,1},{1,0},{2,3},{3,2},{4,5},{5,4},{6,7},{7,6},{8,9},{9,8},{10,11... | collective-permute-start | bytes 417800 | tf_op jit(solution)/shard_map/ppermute | solution.py:75
  80.4 4.0 %collective-permute-start.21 = (f32[136,2,128]{2,1,0:T(2,128)S(1)}, f32[136,2,128]{2,1,0:T(2,128)S(1)}, u32[]{:S(2)}, u32[]{:S(2)}) collective-permute-start(f32[136,2,128]{2,1,0:T(2,128)S(1)} %get-tuple-element.77), channel_id=1, source_target_pairs={{0,8},{1,2},{2,1},{3,4},{4,3},{5,6},{6,5},{7,15},{8,0},{9,10},{10,... | collective-permute-start | bytes 417800 | tf_op jit(solution)/shard_map/ppermute | solution.py:74
  87.5 2.4 %collective-permute-start.22 = (f32[1,128]{1,0:T(1,128)S(1)}, f32[1,128]{1,0:T(1,128)S(1)}, u32[]{:S(2)}, u32[]{:S(2)}) collective-permute-start(f32[1,128]{1,0:T(1,128)S(1)} %get-tuple-element.82), channel_id=1, source_target_pairs={{0,8},{8,0},{1,9},{9,1},{2,10},{10,2},{3,11},{11,3},{4,12},{12,4},... | collective-permute-start | bytes 1544 | tf_op jit(solution)/shard_map/ppermute | solution.py:741
  90.7 28.3 %all-to-all-start.1 = ((f32[128,1,128]{2,1,0:T(1,128)}), f32[128,1,128]{2,1,0:T(1,128)S(1)}, u32[]{:S(2)}, u32[]{:S(2)}) async-start(f32[128,1,128]{2,1,0:T(1,128)} %broadcast_in_dim.9), calls=%async_computation.1 | async-start | bytes 131072 | tf_op jit(solution)/shard_map/all_to_all | solution.py:744
  (19 other events, 150.0 us)
